TPU v7x, 256 devices: a whole 4x4x8 slice. The times are simulated.
256 devices in a mesh: section: 32 (over x, z), tensor: 4 (over y_hi, core), dp: 2 (over y_lo).
Axes of the slice: x: 4, y: 4 (y_hi: 2, y_lo: 2; y = y_hi * 2 + y_lo), z: 8, core: 2. Of those that a mesh axis runs over, the one named last changes fastest.
Arguments:
- grad_in: bfloat16 [32, 512, 2560], P('section', 'dp', 'tensor'), parts along dimension 1, may hold values from -6 to 6
- grad_top: bfloat16 [1, 512, 2560], P(None, 'dp', 'tensor'), parts along dimension 1, may hold values from -6 to 6
- queries: bfloat16 [32, 2, 512, 2560], P('section', None, 'dp', 'tensor'), parts along dimension 2, may hold values from -80 to 80
- keys: bfloat16 [32, 1024, 2560], P('section', 'dp', 'tensor'), parts along dimension 1, may hold values from -4 to 4
- values: bfloat16 [32, 1024, 2560], P('section', 'dp', 'tensor'), parts along dimension 1, may hold values from -4 to 4
- query_weight: bfloat16 [32, 2560, 2560], P('section', None, 'tensor'), may hold values from -0.75 to 0.75
- key_weight: bfloat16 [32, 2560, 2560], P('section', None, 'tensor'), may hold values from -0.125 to 0.125
- value_weight: bfloat16 [32, 2560, 2560], P('section', None, 'tensor'), may hold values from -0.125 to 0.125
- text_weight: bfloat16 [2560, 2560], P('section', 'tensor'), may hold values from -0.125 to 0.125
- text_hidden: bfloat16 [2560, 1024], P('tensor', ('dp', 'section')), parts along dimension 1, may hold values from -5 to 5
Outputs:
- sent: bfloat16 [32, 2, 512, 2560], P('section', None, 'dp', 'tensor'), parts along dimension 2
- text_grad: float32 [2560, 1024], P('tensor', ('dp', 'section')), parts along dimension 1
There are 2 independent parts, one for each index of `dp`. A program takes and returns all parts, laid end to end along the dimension named above; an argument that names none is the same for every part. Nothing has to cross between parts.
All inputs are finite; a program needn't handle non-finite values.
Results may differ from a plain program's by a relative error of at most 0.03.
Values may be sent and summed in bfloat16 or wider, within the bound.
No kernel may reach another device: no remote copies, remote signals or barrier semaphores. Data moves between devices by JAX's collectives and lax.ppermute only.
A program may use at most 64 MiB of HBM per device.

v0:
```python
import jax
import jax.numpy as jnp
from jax import lax
from jax.sharding import PartitionSpec as P

HEAD_DIM = 128
TICKS = 2


def passed_along(value, axis, steps):
    count = lax.axis_size(axis)
    initial, last = (max(0, -steps), min(count, count - steps))
    return lax.ppermute(value, axis, [(source, source + steps) for source in range(initial, last)])


def smooth_gate(inputs):
    return jax.nn.gelu(inputs, approximate=True)


def gelu_slope(inputs):
    unused_out, backward = jax.vjp(smooth_gate, inputs)
    return backward(jnp.ones_like(inputs))[0]


def attention_back(query_rows, key_rows, value_rows, grad_rows, head_count, head_width):
    token_count = query_rows.shape[0]
    context_count = key_rows.shape[0]
    query_heads = query_rows.reshape(token_count, head_count, head_width)
    key_heads = key_rows.reshape(context_count, head_count, head_width)
    value_heads = value_rows.reshape(context_count, head_count, head_width)
    grad_heads = grad_rows.reshape(token_count, head_count, head_width)
    scale_factor = head_width ** (-0.5)
    scores = (
        jnp.einsum("qhd,chd->hqc", query_heads, key_heads, preferred_element_type=jnp.float32)
        * scale_factor
    )
    peak = jnp.max(scores, axis=-1, keepdims=True)
    shifted = jnp.exp(scores - peak)
    attention = shifted / jnp.sum(shifted, axis=-1, keepdims=True)
    attention_low = attention.astype(jnp.bfloat16)
    attention_grad = jnp.einsum(
        "qhd,chd->hqc", grad_heads, value_heads, preferred_element_type=jnp.float32
    )
    row_dot = jnp.sum(attention * attention_grad, axis=-1, keepdims=True)
    score_grad = (attention * (attention_grad - row_dot)).astype(jnp.bfloat16)
    query_grad = (
        jnp.einsum("hqc,chd->qhd", score_grad, key_heads, preferred_element_type=jnp.float32)
        * scale_factor
    ).astype(jnp.bfloat16)
    key_grad = (
        jnp.einsum("hqc,qhd->chd", score_grad, query_heads, preferred_element_type=jnp.float32)
        * scale_factor
    )
    value_grad = jnp.einsum(
        "hqc,qhd->chd", attention_low, grad_heads, preferred_element_type=jnp.float32
    )
    return (
        query_grad.reshape(token_count, head_count * head_width),
        key_grad.reshape(context_count, head_count * head_width),
        value_grad.reshape(context_count, head_count * head_width),
    )


def shards(
    grad_in,
    grad_top,
    queries,
    keys,
    values,
    query_weight,
    key_weight,
    value_weight,
    text_weight,
    text_hidden,
):
    section_count = lax.axis_size("section")
    section_place = lax.axis_index("section")
    head_count = keys.shape[-1] // HEAD_DIM
    key_rows = keys[0]
    value_rows = values[0]
    weight_rows = query_weight[0]
    incoming = grad_in[0]
    outgoing = incoming
    key_total = jnp.zeros(key_rows.shape, jnp.float32)
    value_total = jnp.zeros(value_rows.shape, jnp.float32)
    sent_list = []
    for step_index in range(TICKS):
        if step_index > 0:
            received = passed_along(outgoing, "section", -1)
            incoming = jnp.where(
                section_place == section_count - 1, grad_top[step_index - 1], received
            )
        query_grad, key_grad, value_grad = attention_back(
            queries[0, step_index], key_rows, value_rows, incoming, head_count, HEAD_DIM
        )
        key_total = key_total + key_grad
        value_total = value_total + value_grad
        head_terms = lax.dot_general(
            query_grad, weight_rows, (((1,), (1,)), ((), ())), preferred_element_type=jnp.float32
        )
        head_total = lax.psum_scatter(
            head_terms.astype(jnp.bfloat16), "tensor", scatter_dimension=1, tiled=True
        ).astype(jnp.float32)
        outgoing = (incoming.astype(jnp.float32) + head_total).astype(jnp.bfloat16)
        sent_list.append(outgoing)
    sent = jnp.stack(sent_list, axis=0)[None]
    key_low = key_total.astype(jnp.bfloat16)
    value_low = value_total.astype(jnp.bfloat16)
    key_matrix = key_weight[0]
    value_matrix = value_weight[0]
    first = lax.dot_general(
        key_matrix, key_low, (((1,), (1,)), ((), ())), preferred_element_type=jnp.float32
    )
    second = lax.dot_general(
        value_matrix, value_low, (((1,), (1,)), ((), ())), preferred_element_type=jnp.float32
    )
    context_local = lax.psum_scatter(
        (first + second).astype(jnp.bfloat16), "tensor", scatter_dimension=0, tiled=True
    )
    context_share = lax.psum_scatter(context_local, "section", scatter_dimension=1, tiled=True)
    hidden_terms = jnp.dot(
        lax.all_gather(text_weight, "section", axis=0, tiled=True),
        context_share,
        preferred_element_type=jnp.float32,
    )
    hidden_back = lax.psum_scatter(
        hidden_terms.astype(jnp.bfloat16), "tensor", scatter_dimension=0, tiled=True
    ).astype(jnp.float32)
    return (sent, hidden_back * gelu_slope(text_hidden.astype(jnp.float32)))


def solution(mesh):
    placed = (
        P("section", "dp", "tensor"),
        P(None, "dp", "tensor"),
        P("section", None, "dp", "tensor"),
        P("section", "dp", "tensor"),
        P("section", "dp", "tensor"),
        P("section", None, "tensor"),
        P("section", None, "tensor"),
        P("section", None, "tensor"),
        P("section", "tensor"),
        P("tensor", ("dp", "section")),
    )
    return jax.shard_map(
        shards,
        mesh=mesh,
        in_specs=placed,
        out_specs=(P("section", None, "dp", "tensor"), P("tensor", ("dp", "section"))),
        check_vma=False,
    )
```

profile of v0, /device:TPU:1, one launch (start us, length us, event | category | flops | bytes accessed | tf_op | source)
XLA Modules:
  0.0 470.2 jit_solution(6970807234348190731)
XLA Ops:
  8.0 0.0 copy-start
  8.0 0.0 reduce-scatter.16.cloned.1.call-start
  8.1 2.3 copy.40
  10.4 2.0 fusion.41
  12.4 1.9 copy.72
  14.2 1.9 copy.38
  16.1 2.2 copy.44
  18.3 3.7 fusion.42
  22.0 2.8 multiply_reduce_fusion.1
  24.8 0.0 copy-start.1
  24.8 0.4 multiply_convert_fusion.1
  25.3 0.6 copy-done.1
  25.9 0.5 fusion.23
  26.5 0.5 copy-done.3
  27.0 0.2 copy-done.11
  27.1 2.3 convolution_convert_fusion.1
  29.5 2.5 copy.64
  31.9 0.0 reduce-scatter.16.cloned.1.call-update
  31.9 0.0 reduce-scatter.20.cloned.1.call-start
  32.0 3.3 convolution_bitcast_fusion
  35.3 39.2 %reduce-scatter.16.cloned.1.call-done = bf16[640,256]{1,0:T(8,128)(2,1)} async-done(((bf16[2560,256]{1,0:T(8,128)(2,1)}), bf16[640,256]{1,0:T(8,128)(2,1)}) %reduce-scatter.16.cloned.1.call-update) | async-done | bytes 327696
  74.5 1.9 fusion.25
  76.4 1.5 collective-permute-start
  77.8 2.9 fusion.44
  80.7 1.9 copy.48
  82.6 1.9 copy.73
  84.5 3.7 fusion.43
  88.1 1.1 bitcast_select_fusion
  89.3 2.7 multiply_reduce_fusion
  92.0 0.1 copy-done.5
  92.1 0.4 copy-done.12
  92.5 0.4 fusion.17
  92.9 0.4 multiply_convert_fusion
  93.4 0.9 copy-done.6
  94.2 0.0 copy-done.7
  94.3 0.3 fusion.18
  94.7 2.3 fusion.5
  96.9 3.7 fusion.2
  100.7 4.4 copy.68
  105.1 0.0 reduce-scatter.20.cloned.1.call-update
  105.1 0.0 all-gather.2.cloned.1.call-start
  105.2 0.5 all-gather.2.cloned.1.call-update
  105.7 0.0 reduce-scatter.14.cloned.1.call-start
  105.8 46.9 %reduce-scatter.20.cloned.1.call-done = bf16[640,512]{1,0:T(8,128)(2,1)} async-done(((bf16[2560,512]{1,0:T(8,128)(2,1)}), bf16[640,512]{1,0:T(8,128)(2,1)}) %reduce-scatter.20.cloned.1.call-update) | async-done | bytes 655376
  152.7 2.2 copy.69
  154.9 0.0 reduce-scatter.14.cloned.1.call-update
  154.9 0.0 reduce-scatter.18.cloned.1.call-start
  154.9 2.0 fusion.24
  157.0 4.3 convolution_convert_fusion
  161.2 2.4 copy.66
  163.7 0.0 reduce-scatter.18.cloned.1.call-update
  163.7 0.0 reduce-scatter.22.cloned.1.call-start
  163.8 22.1 %all-gather.2.cloned.1.call-done = bf16[2560,640]{1,0:T(8,128)(2,1)} async-done(((bf16[80,640]{1,0:T(8,128)(2,1)}), bf16[2560,640]{1,0:T(8,128)(2,1)}) %all-gather.2.cloned.1.call-update) | async-done | bytes 3276816 | tf_op jit(solution)/shard_map/all_gather | solution.py:122
  185.8 193.3 %reduce-scatter.14.cloned.1.call-done = bf16[640,16]{0,1:T(8,128)(2,1)} async-done(((bf16[640,512]{0,1:T(8,128)(2,1)}), bf16[640,16]{0,1:T(8,128)(2,1)}) %reduce-scatter.14.cloned.1.call-update) | async-done | bytes 20496 | tf_op jit(solution)/shard_map/reduce_scatter | solution.py:120
  379.2 2.9 fusion.3
  382.0 1.1 copy.70
  383.1 0.0 reduce-scatter.22.cloned.1.call-update
  383.2 40.9 %reduce-scatter.18.cloned.1.call-done = bf16[640,256]{1,0:T(8,128)(2,1)} async-done(((bf16[2560,256]{1,0:T(8,128)(2,1)}), bf16[640,256]{1,0:T(8,128)(2,1)}) %reduce-scatter.18.cloned.1.call-update) | async-done | bytes 327696
  424.0 1.2 fusion.26
  425.2 1.9 maximum_bitcast_fusion
  427.1 2.2 copy.55
  429.3 31.7 %reduce-scatter.22.cloned.1.call-done = bf16[640,16]{1,0:T(8,128)(2,1)} async-done(((bf16[2560,16]{1,0:T(8,128)(2,1)}), bf16[640,16]{1,0:T(8,128)(2,1)}) %reduce-scatter.22.cloned.1.call-update) | async-done | bytes 20496
  460.9 1.0 copy.71
  462.0 0.7 fusion.34
  (18 shorter events, 0.0 us)
Async XLA Ops:
  8.0 86.6 %copy-start = (bf16[1,2560,640]{2,1,0:T(8,128)(2,1)S(1)}, bf16[1,2560,640]{2,1,0:T(8,128)(2,1)}, u32[]{:S(2)}) copy-start(bf16[1,2560,640]{2,1,0:T(8,128)(2,1)} %param.16) | copy-start | bytes 9830404
  8.0 66.5 %reduce-scatter.16.cloned.1.call-start = ((), (), s32[]{:S(2)}) async-start(), calls=%async_computation.7 | async-start | bytes 1638400
  22.0 2.8 copy-start.4
  24.8 1.1 copy-start.1
  24.8 2.3 copy-start.11
  25.9 1.1 copy-start.3
  31.9 120.7 %reduce-scatter.20.cloned.1.call-start = ((), (), s32[]{:S(2)}) async-start(), calls=%async_computation.9 | async-start | bytes 3276800
  76.4 11.8 %collective-permute-start = (bf16[256,640]{0,1:T(8,128)(2,1)}, bf16[256,640]{0,1:T(8,128)(2,1)}, u32[]{:S(2)}, u32[]{:S(2)}) collective-permute-start(bf16[256,640]{0,1:T(8,128)(2,1)} %fusion.25), channel_id=1, source_target_pairs={{8,0},{16,8},{24,16},{32,24},{40,32},{48,40},{56,48},{64,56},{72,6... | collective-permute-start | bytes 983048 | tf_op jit(solution)/shard_map/ppermute | solution.py:13
  89.3 2.8 copy-start.8
  89.3 2.8 copy-start.5
  89.3 3.2 copy-start.12
  92.9 1.3 copy-start.6
  92.9 1.4 copy-start.7
  94.3 2.6 copy-start.2
  94.6 2.3 copy-start.10
  105.1 80.7 %all-gather.2.cloned.1.call-start = ((), (), s32[]{:S(2)}) async-start(), calls=%async_computation.6 | async-start | bytes 3379200 | tf_op jit(solution)/shard_map/all_gather | solution.py:122
  105.7 273.5 %reduce-scatter.14.cloned.1.call-start = ((), (), s32[]{:S(2)}) async-start(), calls=%async_computation.5 | async-start | bytes 675840 | tf_op jit(solution)/shard_map/reduce_scatter | solution.py:120
  154.9 269.1 %reduce-scatter.18.cloned.1.call-start = ((), (), s32[]{:S(2)}) async-start(), calls=%async_computation.8 | async-start | bytes 1638400
  163.7 297.2 %reduce-scatter.22.cloned.1.call-start = ((), (), s32[]{:S(2)}) async-start(), calls=%async_computation.10 | async-start | bytes 819200
  382.0 79.9 %copy-start.9 = (bf16[640,16]{0,1:T(8,128)(2,1)S(1)}, bf16[640,16]{0,1:T(8,128)(2,1)}, u32[]{:S(2)}) copy-start(bf16[640,16]{0,1:T(8,128)(2,1)} %param.19) | copy-start | bytes 61444
Sparse Core Ops, SparseCore 0:
  32.1 42.3 reduce-scatter.15
  105.2 47.3 reduce-scatter.19
Sparse Core Ops, SparseCore 1:
  108.5 77.3 all-gather.1
  189.4 189.7 reduce-scatter.13
  381.8 42.2 reduce-scatter.17
  427.1 33.8 reduce-scatter.21
where the time goes:
time: 471 us; the launch traced here: 470 us
  waiting for transfers between devices  375 us (80%)
  matrix products  38 us (8%)
  local copies, waits for them, and re-layouts  32.5 us (7%)
  between operations  15.9 us (3%)
  other arithmetic  7.52 us (2%)
    reduce_scatter x1, waiting for transfers between devices, shards(): lax.psum_scatter(context_local, 'section', scatter_dimension=1, tiled=True)  193 us
    unnamed x10, waiting for transfers between devices  159 us
    unnamed x39, local copies, waits for them, and re-layouts  30.5 us
    all_gather x1, waiting for transfers between devices, shards(): lax.all_gather(text_weight, 'section', axis=0, tiled=True)  22.1 us
  transfers between devices with their start and end apart: 7, of which 6 were waited for; matrix products, arithmetic and copies ran while one was open for 7% of the time, Pallas kernels for 0%

commit v1 on v0

v1 whole, which is shorter than its diff:
```python
import functools
import math

import jax
import jax.numpy as jnp
from jax import lax
from jax.experimental import pallas as pl
from jax.experimental.pallas import tpu as pltpu
from jax.sharding import PartitionSpec as P

HEAD = 128
NX, NZ = 4, 8
SECTIONS = NX * NZ
TENSOR = 4
VMEM_LIMIT = 40 * 1024 * 1024
F32 = jnp.float32
BF16 = jnp.bfloat16
NT = (((1,), (1,)), ((), ()))
NN = (((1,), (0,)), ((), ()))
TN = (((0,), (0,)), ((), ()))


def dot(a, b, dims):
    return lax.dot_general(a, b, dims, preferred_element_type=F32)


def positions():
    section = lax.axis_index("section")
    tensor = lax.axis_index("tensor")
    return jnp.stack(
        [
            section // NZ,
            section % NZ,
            tensor // 2,
            tensor % 2,
            (section == SECTIONS - 1).astype(jnp.int32),
        ]
    ).astype(jnp.int32)


def block_for(pos, j, other):
    core = pos[3] ^ other
    return (pos[2] ^ (j % 2)) * 2 + (core ^ (j // 2))


def swap_tensor(value, bit):
    return lax.ppermute(value, "tensor", [(i, i ^ bit) for i in range(TENSOR)])


def send_x(value, step):
    pairs = [
        (x * NZ + z, ((x + step) % NX) * NZ + z) for x in range(NX) for z in range(NZ)
    ]
    return lax.ppermute(value, "section", pairs)


def send_z(value, step):
    pairs = []
    for x in range(NX):
        for z in range(NZ):
            for t in range(TENSOR):
                to = (z + step + 4 * (t % 2)) % NZ
                pairs.append(((x * NZ + z) * TENSOR + t, (x * NZ + to) * TENSOR + t))
    return lax.ppermute(value, ("section", "tensor"), pairs)


def pass_back(value, bit):
    pairs = [
        ((s + 1) * TENSOR + t, s * TENSOR + (t ^ bit))
        for s in range(SECTIONS - 1)
        for t in range(TENSOR)
    ]
    return lax.ppermute(value, ("section", "tensor"), pairs)


def probabilities(q, k):
    factor = HEAD ** (-0.5) * math.log2(math.e)
    scores = dot(k, q, NT)
    peak = jnp.max(scores, axis=0, keepdims=True)
    shifted = jnp.exp2((scores - peak) * factor)
    return shifted * (1.0 / jnp.sum(shifted, axis=0, keepdims=True))


def score_gradient(attention, v, g):
    attention_grad = dot(v, g, NT)
    row_dot = jnp.sum(attention * attention_grad, axis=0, keepdims=True)
    return (attention * (attention_grad - row_dot)).astype(BF16)


def heads_of(width):
    return [slice(i, i + HEAD) for i in range(0, width, HEAD)]


def call(body, grid, in_specs, out_specs, out_shape, flops, nbytes, scratch=()):
    return pl.pallas_call(
        body,
        grid_spec=pltpu.PrefetchScalarGridSpec(
            num_scalar_prefetch=1,
            grid=grid,
            in_specs=in_specs,
            out_specs=out_specs,
            scratch_shapes=list(scratch),
        ),
        out_shape=out_shape,
        compiler_params=pltpu.CompilerParams(vmem_limit_bytes=VMEM_LIMIT),
        cost_estimate=pl.CostEstimate(flops=flops, bytes_accessed=nbytes, transcendentals=0),
    )


def full(*shape):
    return pl.BlockSpec(shape, lambda *a: (0,) * len(shape))


ANY = pl.BlockSpec(memory_space=pl.ANY)


def tick_spec(tick, rows, cols):
    return pl.BlockSpec((None, None, rows, cols), lambda *a: (0, tick, 0, 0))


def first_kernel(pos, q_ref, k_ref, v_ref, g_ref, w_ref, dq_ref, out_ref):
    @pl.when(pl.program_id(0) == 0)
    def _():
        for h in heads_of(q_ref.shape[-1]):
            k = k_ref[:, h]
            attention = probabilities(q_ref[:, h], k)
            score_grad = score_gradient(attention, v_ref[:, h], g_ref[:, h])
            dq = dot(score_grad, k, TN) * HEAD ** (-0.5)
            dq_ref[:, h] = dq.astype(BF16)

    out_ref[...] = dot(dq_ref[...], w_ref[...], NT).astype(BF16)


def project_kernel(pos, dq_ref, w_ref, out_ref):
    out_ref[...] = dot(dq_ref[...], w_ref[...], NT).astype(BF16)


def between_kernel(pos, q0_ref, q1_ref, k_ref, v_ref, g_ref, after, dk_ref, dv_ref, p_ref):
    for i, h in enumerate(heads_of(k_ref.shape[-1])):
        k = k_ref[:, h]
        q = q0_ref[:, h]
        g = g_ref[:, h]
        attention = probabilities(q, k)
        score_grad = score_gradient(attention, v_ref[:, h], g)
        dk_ref[:, h] = dot(score_grad, q, NN) * HEAD ** (-0.5)
        dv_ref[:, h] = dot(attention.astype(BF16), g, NN)
        p_ref[i] = probabilities(q1_ref[:, h], k)


def second_kernel(
    pos, q_ref, v_ref, a_ref, b_ref, top_ref, dk_ref, dv_ref, p_ref, g_ref, ds_ref, low_ref, held
):
    width = q_ref.shape[-1]
    came = a_ref[...].astype(F32) + b_ref[...].astype(F32)
    g_ref[...] = jnp.where(pos[4] == 1, top_ref[...].astype(F32), came).astype(BF16)
    for i, h in enumerate(heads_of(width)):
        g = g_ref[:, h]
        attention = p_ref[i]
        score_grad = score_gradient(attention, v_ref[:, h], g)
        ds_ref[i] = score_grad
        dk = dk_ref[:, h] + dot(score_grad, q_ref[:, h], NN) * HEAD ** (-0.5)
        dv = dv_ref[:, h] + dot(attention.astype(BF16), g, NN)
        held[:, h] = dk.astype(BF16)
        held[:, slice(width + h.start, width + h.stop)] = dv.astype(BF16)
    rows = held.shape[0] // SECTIONS
    for other in range(2):
        core = pos[3] ^ (1 - other)
        for dx in range(NX):
            for kz in range(NZ // 2):
                to_x = (pos[0] + dx) % NX
                to_z = (pos[1] + kz + 4 * core) % NZ
                source = pl.multiple_of((to_x * NZ + to_z) * rows, rows)
                place = ((other * NX + dx) * (NZ // 2) + kz) * rows
                low_ref[place : place + rows, :] = held[pl.ds(source, rows), :]


def context_kernel(pos, low_ref, kw_ref, vw_ref, *rest):
    out_ref = rest[-1]
    width = kw_ref.shape[-1]
    total = dot(low_ref[:, :width], kw_ref[...], NT) + dot(low_ref[:, width:], vw_ref[...], NT)
    out_ref[...] = total.astype(BF16)


def third_kernel(pos, ds_ref, k_ref, w_ref, after, dq_ref, out_ref):
    @pl.when(pl.program_id(0) == 0)
    def _():
        for i, h in enumerate(heads_of(k_ref.shape[-1])):
            dq = dot(ds_ref[i], k_ref[:, h], TN) * HEAD ** (-0.5)
            dq_ref[:, h] = dq.astype(BF16)

    out_ref[...] = dot(dq_ref[...], w_ref[...], NT).astype(BF16)


def text_kernel(pos, context_ref, w_ref, out_ref):
    out_ref[...] = dot(context_ref[...], w_ref[...], NT).astype(BF16)


def sent_kernel(pos, a0_ref, b0_ref, a1_ref, b1_ref, out_ref):
    out_ref[0] = (a0_ref[...].astype(F32) + b0_ref[...].astype(F32)).astype(BF16)
    out_ref[1] = (a1_ref[...].astype(F32) + b1_ref[...].astype(F32)).astype(BF16)


def smooth_gate(inputs):
    return jax.nn.gelu(inputs, approximate=True)


def gelu_slope(inputs):
    unused_out, backward = jax.vjp(smooth_gate, inputs)
    return backward(jnp.ones_like(inputs))[0]


def add_low(*terms):
    total = terms[0].astype(F32)
    for term in terms[1:]:
        total = total + term.astype(F32)
    return total.astype(BF16)


def shards(
    grad_in,
    grad_top,
    queries,
    keys,
    values,
    query_weight,
    key_weight,
    value_weight,
    text_weight,
    text_hidden,
):
    pos = positions()
    rows, width = grad_in.shape[1], grad_in.shape[2]
    text = keys.shape[1]
    heads = width // HEAD
    model = width * TENSOR
    k, v, g0, top = keys[0], values[0], grad_in[0], grad_top[0]
    wq, wk, wv = query_weight[0], key_weight[0], value_weight[0]

    z_groups = [[x * NZ + z for z in range(NZ)] for x in range(NX)]
    x_groups = [[x * NZ + z for x in range(NX)] for z in range(NZ)]
    gathered = lax.all_gather(
        text_weight, "section", axis=0, tiled=True, axis_index_groups=z_groups
    )
    gathered = lax.all_gather(gathered, "section", axis=0, tiled=True, axis_index_groups=x_groups)

    act = jax.ShapeDtypeStruct((rows, width), BF16)
    pair = jax.ShapeDtypeStruct((2, rows, width), BF16)
    pair_spec = pl.BlockSpec((None, rows, width), lambda j, pos: (j, 0, 0))

    def weight_spec(other):
        return pl.BlockSpec((width, width), lambda j, pos: (block_for(pos, j, other), 0))

    project_flops = 4 * rows * width * width
    head_flops = 2 * rows * text * width

    dq0, send0 = call(
        first_kernel,
        (2,),
        [
            tick_spec(0, rows, width),
            full(text, width),
            full(text, width),
            full(rows, width),
            weight_spec(1),
        ],
        [full(rows, width), pair_spec],
        [act, pair],
        project_flops + 3 * head_flops,
        8_000_000,
    )(pos, queries, k, v, g0, wq)
    came0 = swap_tensor(send0, 1)
    keep0 = call(
        project_kernel,
        (2,),
        [full(rows, width), weight_spec(0)],
        pair_spec,
        pair,
        project_flops,
        2_600_000,
    )(pos, dq0, wq)
    near0 = add_low(g0, keep0[0], came0[0])
    far0 = add_low(keep0[1], came0[1])
    from_near = pass_back(near0, 0)
    from_far = pass_back(far0, 2)

    square = jax.ShapeDtypeStruct((text, width), F32)
    dk0, dv0, p1 = call(
        between_kernel,
        (1,),
        [
            tick_spec(0, rows, width),
            tick_spec(1, rows, width),
            full(text, width),
            full(text, width),
            full(rows, width),
            ANY,
        ],
        [full(text, width), full(text, width), full(heads, text, rows)],
        [square, square, jax.ShapeDtypeStruct((heads, text, rows), F32)],
        6 * head_flops,
        8_000_000,
    )(pos, queries, queries, k, v, g0, far0)

    g1, ds1, low = call(
        second_kernel,
        (1,),
        [
            tick_spec(1, rows, width),
            full(text, width),
            full(rows, width),
            full(rows, width),
            full(rows, width),
            full(text, width),
            full(text, width),
            full(heads, text, rows),
        ],
        [full(rows, width), full(heads, text, rows), full(text, 2 * width)],
        [
            act,
            jax.ShapeDtypeStruct((heads, text, rows), BF16),
            jax.ShapeDtypeStruct((text, 2 * width), BF16),
        ],
        3 * head_flops,
        10_000_000,
        [pltpu.VMEM((text, 2 * width), BF16)],
    )(pos, queries, v, from_near, from_far, top, dk0, dv0, p1)
    far0_back = swap_tensor(far0, 2)

    def context_half(other, *after):
        weight = pl.BlockSpec((width, width), lambda j, pos: (block_for(pos, j, other), 0))
        return call(
            context_kernel,
            (TENSOR,),
            [pl.BlockSpec((text // 2, 2 * width), lambda j, pos: (1 - other, 0)), weight, weight]
            + [ANY] * len(after),
            pl.BlockSpec((text // 2, width), lambda j, pos: (0, j)),
            jax.ShapeDtypeStruct((text // 2, model), BF16),
            2 * text * width * model,
            8_000_000,
        )(pos, low, wk, wv, *after)

    send = context_half(1)
    keep = context_half(0, send)
    came = swap_tensor(send, 1)
    part = text // 2 // NX
    by_x = [
        add_low(keep[i * part : (i + 1) * part], came[i * part : (i + 1) * part])
        for i in range(NX)
    ]
    came_x = [send_x(by_x[i], i) for i in range(1, NX)]

    dq1, send1 = call(
        third_kernel,
        (2,),
        [full(heads, text, rows), full(text, width), weight_spec(1), ANY],
        [full(rows, width), pair_spec],
        [act, pair],
        project_flops + head_flops,
        5_000_000,
    )(pos, ds1, k, wq, by_x[1])
    came1 = swap_tensor(send1, 1)
    keep1 = call(
        project_kernel,
        (2,),
        [full(rows, width), weight_spec(0)],
        pair_spec,
        pair,
        project_flops,
        2_600_000,
    )(pos, dq1, wq)
    near1 = add_low(g1, keep1[0], came1[0])
    far1 = add_low(keep1[1], came1[1])
    far1_back = swap_tensor(far1, 2)
    sent = call(
        sent_kernel,
        (1,),
        [full(rows, width)] * 4,
        full(2, rows, width),
        jax.ShapeDtypeStruct((2, rows, width), BF16),
        1_000_000,
        2_000_000,
    )(pos, near0, far0_back, near1, far1_back)

    by_z = add_low(by_x[0], *came_x)
    few = part // (NZ // 2)
    came_z = [send_z(by_z[i * few : (i + 1) * few], i) for i in range(NZ // 2)]

    def over_tensor(terms):
        total = sum(term.astype(F32) for term in terms)
        half = total.shape[1] // 2
        came = swap_tensor(total[:, half:].astype(BF16), 1)
        total = total[:, :half] + came.astype(F32)
        half = total.shape[1] // 2
        came = swap_tensor(total[:, half:].astype(BF16), 2)
        return total[:, :half] + came.astype(F32)

    context = over_tensor(came_z).astype(BF16)
    hidden = call(
        text_kernel,
        (TENSOR,),
        [
            full(few, width),
            pl.BlockSpec((width, width), lambda j, pos: (block_for(pos, j, 0), 0)),
        ],
        pl.BlockSpec((few, width), lambda j, pos: (0, j)),
        jax.ShapeDtypeStruct((few, model), BF16),
        2 * few * width * model,
        3_300_000,
    )(pos, context, gathered)
    hidden_back = over_tensor([hidden])
    text_grad = hidden_back.T * gelu_slope(text_hidden.astype(F32))
    return (sent[None], text_grad)


def solution(mesh):
    placed = (
        P("section", "dp", "tensor"),
        P(None, "dp", "tensor"),
        P("section", None, "dp", "tensor"),
        P("section", "dp", "tensor"),
        P("section", "dp", "tensor"),
        P("section", None, "tensor"),
        P("section", None, "tensor"),
        P("section", None, "tensor"),
        P("section", "tensor"),
        P("tensor", ("dp", "section")),
    )
    return jax.shard_map(
        shards,
        mesh=mesh,
        in_specs=placed,
        out_specs=(P("section", None, "dp", "tensor"), P("tensor", ("dp", "section"))),
        check_vma=False,
    )
```

time: 471 us -> 175 us (0.37)
  waiting for transfers between devices: 375 us -> 44.9 us
  matrix products: 38 us -> 0 us
  starting transfers between devices: 1.71 us -> 34.8 us
  Pallas kernels: 0 us -> 30.9 us
  blocking collectives: 0 us -> 27.9 us
  local copies, waits for them, and re-layouts: 32.5 us -> 14.3 us
    reduce_scatter x1 -> x0, waiting for transfers between devices: 193 us -> none  [shards(): lax.psum_scatter(context_local, 'section', scatter_dimension=1, tiled=True)]
    unnamed x10 -> x1, waiting for transfers between devices: 159 us -> 0.02 us
    ppermute x1 -> x18, waiting for transfers between devices: 0.01 us -> 44.9 us  [the longest x3 19.1 us: send_x(): return lax.ppermute(value, 'section', pairs)]
    ppermute x1 -> x18, starting transfers between devices: 1.46 us -> 34.7 us  [the longest x9 19.1 us: swap_tensor(): return lax.ppermute(value, 'tensor', [(i, i ^ bit) for i in range(TENSOR)])]
    pallas_call x0 -> x10, Pallas kernels: none -> 30.9 us  [the longest x2 8.54 us: context_half(): call(context_kernel, (TENSOR,), [pl.BlockSpec((text // 2, 2 * width), lam...]
    dot_general x13 -> x0, matrix products: 30.6 us -> none  [the longest x2 6.57 us: shards(): lax.dot_general(query_grad, weight_rows, (((1,), (1,)), ((), ())), prefer...]
    all_gather x0 -> x1, blocking collectives: none -> 27.9 us  [shards(): lax.all_gather(text_weight, 'section', axis=0, tiled=True, axis_index_gro...]
    all_gather x1, waiting for transfers between devices: 22.1 us -> 0.02 us  [shards(): lax.all_gather(gathered, 'section', axis=0, tiled=True, axis_index_groups...]
  transfers between devices with their start and end apart: 7 -> 19, of which waited for: 6 -> 11; matrix products, arithmetic and copies ran while one was open for 7% -> 3% of each run, Pallas kernels for 0% -> 11%
where the time goes in v1:
time: 175 us; the launch traced here: 174 us
  waiting for transfers between devices  44.9 us (26%)
  starting transfers between devices  34.8 us (20%)
  Pallas kernels  30.9 us (18%)
  blocking collectives  27.9 us (16%)
  between operations  14.4 us (8%)
  local copies, waits for them, and re-layouts  14.3 us (8%)
  other arithmetic  6.42 us (4%)
    all_gather x1, blocking collectives, shards(): lax.all_gather(text_weight, 'section', axis=0, tiled=True, axis_index_gro...  27.9 us
    ppermute x3, waiting for transfers between devices, send_x(): return lax.ppermute(value, 'section', pairs)  19.1 us
    ppermute x9, starting transfers between devices, swap_tensor(): return lax.ppermute(value, 'tensor', [(i, i ^ bit) for i in range(TENSOR)])  19.1 us
    unnamed x54, local copies, waits for them, and re-layouts  14.2 us
    ppermute x2, waiting for transfers between devices, pass_back(): return lax.ppermute(value, ('section', 'tensor'), pairs)  11.7 us
    pallas_call x2, Pallas kernels, context_half(): call(context_kernel, (TENSOR,), [pl.BlockSpec((text // 2, 2 * width), lam...  8.54 us
    ppermute x9, waiting for transfers between devices, swap_tensor(): return lax.ppermute(value, 'tensor', [(i, i ^ bit) for i in range(TENSOR)])  8.49 us
    ppermute x4, starting transfers between devices, send_z(): return lax.ppermute(value, ('section', 'tensor'), pairs)  8.02 us
  transfers between devices with their start and end apart: 19, of which 11 were waited for; matrix products, arithmetic and copies ran while one was open for 3% of the time, Pallas kernels for 11%

profile of v1, /device:TPU:1, one launch (start us, length us, event | category | flops | bytes accessed | tf_op | source)
XLA Modules:
  0.0 173.7 jit_solution(15156092479890097016)
XLA Ops:
  7.2 0.0 all-gather.2.cloned.1.call-start
  7.2 0.1 stack.27.pos
  7.3 1.9 %copy-done = bf16[1,2560,640]{2,1,0:T(8,128)(2,1)S(1)} copy-done((bf16[1,2560,640]{2,1,0:T(8,128)(2,1)S(1)}, bf16[1,2560,640]{2,1,0:T(8,128)(2,1)}, u32[]{:S(2)}) %copy-start) | copy-done | bytes 3276824
  9.3 1.1 copy-done.11
  10.3 1.1 copy-done.13
  11.4 1.1 copy-done.15
  12.5 1.0 copy-done.17
  13.5 4.6 %shard_map.113 = (bf16[256,640]{1,0:T(8,128)(2,1)S(1)}, bf16[2,256,640]{2,1,0:T(8,128)(2,1)S(1)}) custom-call(s32[5]{0:T(128)S(1)} %stack.27.pos, bf16[1,2,256,640]{3,2,1,0:T(8,128)(2,1)S(1)} %copy-done.11, bf16[512,640]{1,0:T(8,128)(2,1)S(1)} %bitcast.53, bf16[512,640]{1,0:T(8,128)(2,1)S(1)} %bitcast.50, bf16[256,640]{1,0:T(8,128)(2,1)S(1)} %bitcast.56, ...), custom_call_target="tpu_custom_call" | custom-call | flops 922746880 | bytes 8000000 | tf_op jit(solution)/shard_map/pallas_call | solution.py:256
  18.1 3.3 %collective-permute-start = (bf16[2,256,640]{2,1,0:T(8,128)(2,1)S(1)}, bf16[2,256,640]{2,1,0:T(8,128)(2,1)S(1)}, u32[]{:S(2)}, u32[]{:S(2)}) collective-permute-start(bf16[2,256,640]{2,1,0:T(8,128)(2,1)S(1)} %get-tuple-element.13), channel_id=1, source_target_pairs={{0,2},{2,0},{4,6},{6,4},{1,3},{3,1},{5,7},{7,5},{8,10},{10,8},{12,... | collective-permute-start | bytes 1966088 | tf_op jit(solution)/shard_map/ppermute | solution.py:47
  21.4 1.5 shard_map.114
  23.0 0.0 copy-start.12
  23.0 0.2 collective-permute-done
  23.2 0.8 fusion.2.after
  24.0 1.3 collective-permute-start.3
  25.3 0.1 fusion.1.a0_ref
  25.4 0.0 copy-start.14
  25.4 0.0 copy-start.24
  25.4 1.4 collective-permute-start.2
  26.9 4.3 %shard_map.115 = (f32[512,640]{1,0:T(8,128)S(1)}, f32[512,640]{1,0:T(8,128)S(1)}, f32[5,512,256]{2,1,0:T(8,128)S(1)}) custom-call(s32[5]{0:T(128)S(1)} %stack.27.pos, bf16[1,2,256,640]{3,2,1,0:T(8,128)(2,1)S(1)} %copy-done.12, bf16[1,2,256,640]{3,2,1,0:T(8,128)(2,1)S(1)} %copy-done.12, bf16[512,640]{1,0:T(8,128)(2,1)S(1)} %bitcast.54, ...), custom_call_target="tpu_custom_call" | custom-call | flops 1006632960 | bytes 8000000 | tf_op jit(solution)/shard_map/pallas_call | solution.py:287
  31.2 6.2 %collective-permute-done.3.b_ref = bf16[256,640]{1,0:T(8,128)(2,1)S(1)} collective-permute-done((bf16[256,640]{1,0:T(8,128)(2,1)}, bf16[256,640]{1,0:T(8,128)(2,1)S(1)}, u32[]{:S(2)}, u32[]{:S(2)}) %collective-permute-start.3) | collective-permute-done | bytes 327712 | tf_op jit(solution)/shard_map/ppermute | solution.py:73
  37.4 5.5 %collective-permute-done.2.a_ref = bf16[256,640]{1,0:T(8,128)(2,1)S(1)} collective-permute-done((bf16[256,640]{1,0:T(8,128)(2,1)S(1)}, bf16[256,640]{1,0:T(8,128)(2,1)S(1)}, u32[]{:S(2)}, u32[]{:S(2)}) %collective-permute-start.2) | collective-permute-done | bytes 327712 | tf_op jit(solution)/shard_map/ppermute | solution.py:73
  42.9 3.2 %shard_map.116 = (bf16[256,640]{1,0:T(8,128)(2,1)S(1)}, bf16[5,512,256]{2,1,0:T(8,128)(2,1)S(1)}, bf16[512,1280]{1,0:T(8,128)(2,1)S(1)}) custom-call(s32[5]{0:T(128)S(1)} %stack.27.pos, bf16[1,2,256,640]{3,2,1,0:T(8,128)(2,1)S(1)} %copy-done.12, bf16[512,640]{1,0:T(8,128)(2,1)S(1)} %bitcast.52, bf16[256,640]{1,0:T(8,128)(2,1)S(1)} %collective-permute-done.2.a_ref, ...), custom_call_target="tpu_custom_call" | custom-call | flops 503316480 | bytes 10000000 | tf_op jit(solution)/shard_map/pallas_call | solution.py:304
  46.1 0.0 copy-start.25
  46.2 4.6 %shard_map.117.rest_0_ = bf16[256,2560]{1,0:T(8,128)(2,1)} custom-call(s32[5]{0:T(128)S(1)} %stack.27.pos, bf16[512,1280]{1,0:T(8,128)(2,1)S(1)} %get-tuple-element.19.low_ref, bf16[2560,640]{1,0:T(8,128)(2,1)S(1)} %bitcast.46, bf16[2560,640]{1,0:T(8,128)(2,1)S(1)} %bitcast.48), custom_call_target="tpu_custom_call" | custom-call | flops 1677721600 | bytes 8000000 | tf_op jit(solution)/shard_map/pallas_call | solution.py:331
  50.8 1.3 collective-permute-start.4
  52.1 27.9 %all_gather.6 = bf16[640,640]{1,0:T(8,128)(2,1)} all-gather(bf16[80,640]{1,0:T(8,128)(2,1)S(1)} %copy-done.25), channel_id=1, replica_groups={{0,8,16,24,32,40,48,56},{64,72,80,88,96,104,112,120},{128,136,144,152,1..., dimensions={0}, use_global_device_ids=true | all-gather | bytes 921600 | tf_op jit(solution)/shard_map/all_gather | solution.py:241
  80.0 0.0 all-gather.2.cloned.1.call-update
  80.0 0.0 copy-start.3
  80.0 1.9 %copy-done.3 = bf16[1,2560,640]{2,1,0:T(8,128)(2,1)S(1)} copy-done((bf16[1,2560,640]{2,1,0:T(8,128)(2,1)S(1)}, bf16[1,2560,640]{2,1,0:T(8,128)(2,1)}, u32[]{:S(2)}) %copy-start.3) | copy-done | bytes 3276824
  82.0 1.9 %copy-done.5 = bf16[1,2560,640]{2,1,0:T(8,128)(2,1)S(1)} copy-done((bf16[1,2560,640]{2,1,0:T(8,128)(2,1)S(1)}, bf16[1,2560,640]{2,1,0:T(8,128)(2,1)}, u32[]{:S(2)}) %copy-start.5) | copy-done | bytes 3276824
  83.9 1.3 copy-done.7
  85.2 3.9 %shard_map.118 = bf16[256,2560]{1,0:T(8,128)(2,1)S(1)} custom-call(s32[5]{0:T(128)S(1)} %stack.27.pos, bf16[512,1280]{1,0:T(8,128)(2,1)S(1)} %copy-done.7, bf16[2560,640]{1,0:T(8,128)(2,1)S(1)} %bitcast.47, bf16[2560,640]{1,0:T(8,128)(2,1)S(1)} %bitcast.49, bf16[256,2560]{1,0:T(8,128)(2,1)} %shard_map.117.rest_0_), custom_call_target="tpu_custom_call" | custom-call | flops 1677721600 | bytes 8000000 | tf_op jit(solution)/shard_map/pallas_call | solution.py:331
  89.1 1.4 add_convert_fusion.2
  90.5 1.3 collective-permute-start.7
  91.8 1.6 collective-permute-start.8
  93.5 2.0 %collective-permute-start.9 = (bf16[64,2560]{1,0:T(8,128)(2,1)S(1)}, bf16[64,2560]{1,0:T(8,128)(2,1)S(1)}, u32[]{:S(2)}, u32[]{:S(2)}) collective-permute-start(bf16[64,2560]{1,0:T(8,128)(2,1)S(1)} %get-tuple-element.23), channel_id=1, source_target_pairs={{0,192},{8,200},{16,208},{24,216},{32,224},{40,232},{48,240},{56,2... | collective-permute-start | bytes 983048 | tf_op jit(solution)/shard_map/ppermute | solution.py:54
  95.4 2.3 %collective-permute-done.7 = bf16[64,2560]{1,0:T(8,128)(2,1)S(1)} collective-permute-done((bf16[64,2560]{1,0:T(8,128)(2,1)S(1)}, bf16[64,2560]{1,0:T(8,128)(2,1)S(1)}, u32[]{:S(2)}, u32[]{:S(2)}) %collective-permute-start.7) | collective-permute-done | bytes 327712 | tf_op jit(solution)/shard_map/ppermute | solution.py:54
  97.8 13.2 %collective-permute-done.8 = bf16[64,2560]{1,0:T(8,128)(2,1)S(1)} collective-permute-done((bf16[64,2560]{1,0:T(8,128)(2,1)S(1)}, bf16[64,2560]{1,0:T(8,128)(2,1)S(1)}, u32[]{:S(2)}, u32[]{:S(2)}) %collective-permute-start.8) | collective-permute-done | bytes 327712 | tf_op jit(solution)/shard_map/ppermute | solution.py:54
  111.0 3.6 %collective-permute-done.9 = bf16[64,2560]{1,0:T(8,128)(2,1)S(1)} collective-permute-done((bf16[64,2560]{1,0:T(8,128)(2,1)S(1)}, bf16[64,2560]{1,0:T(8,128)(2,1)S(1)}, u32[]{:S(2)}, u32[]{:S(2)}) %collective-permute-start.9) | collective-permute-done | bytes 327712 | tf_op jit(solution)/shard_map/ppermute | solution.py:54
  114.6 1.2 add_convert_fusion
  115.8 1.9 %collective-permute-start.10 = (bf16[16,2560]{1,0:T(8,128)(2,1)S(1)}, bf16[16,2560]{1,0:T(8,128)(2,1)S(1)}, u32[]{:S(2)}, u32[]{:S(2)}) collective-permute-start(bf16[16,2560]{1,0:T(8,128)(2,1)S(1)} %get-tuple-element.25), channel_id=1, source_target_pairs={{0,0},{2,34},{4,4},{6,38},{8,8},{10,42},{12,12},{14,46},{16,16},{1... | collective-permute-start | bytes 245768 | tf_op jit(solution)/shard_map/ppermute | solution.py:64
  117.7 5.2 %collective-permute-start.11 = (bf16[16,2560]{1,0:T(8,128)(2,1)S(1)}, bf16[16,2560]{1,0:T(8,128)(2,1)S(1)}, u32[]{:S(2)}, u32[]{:S(2)}) collective-permute-start(bf16[16,2560]{1,0:T(8,128)(2,1)S(1)} %get-tuple-element.28), channel_id=1, source_target_pairs={{0,8},{2,42},{4,12},{6,46},{8,16},{10,50},{12,20},{14,54},{16,24},... | collective-permute-start | bytes 245768 | tf_op jit(solution)/shard_map/ppermute | solution.py:64
  122.9 0.9 collective-permute-start.12
  123.8 1.1 collective-permute-done.10
  124.9 4.0 %collective-permute-done.12 = bf16[16,2560]{1,0:T(8,128)(2,1)S(1)} collective-permute-done((bf16[16,2560]{1,0:T(8,128)(2,1)S(1)}, bf16[16,2560]{1,0:T(8,128)(2,1)S(1)}, u32[]{:S(2)}, u32[]{:S(2)}) %collective-permute-start.12) | collective-permute-done | bytes 81952 | tf_op jit(solution)/shard_map/ppermute | solution.py:64
  128.8 0.5 collective-permute-done.13
  129.4 9.5 %collective-permute-start.14 = (bf16[16,1280]{1,0:T(8,128)(2,1)S(1)}, bf16[16,1280]{1,0:T(8,128)(2,1)S(1)}, u32[]{:S(2)}, u32[]{:S(2)}) collective-permute-start(bf16[16,1280]{1,0:T(8,128)(2,1)S(1)} %slice.186), channel_id=1, source_target_pairs={{0,2},{2,0},{4,6},{6,4},{1,3},{3,1},{5,7},{7,5},{8,10},{10,8},{12,... | collective-permute-start | bytes 122888 | tf_op jit(solution)/shard_map/ppermute | solution.py:47
  138.9 2.8 %shard_map.119 = (bf16[256,640]{1,0:T(8,128)(2,1)S(1)}, bf16[2,256,640]{2,1,0:T(8,128)(2,1)}) custom-call(s32[5]{0:T(128)S(1)} %stack.27.pos, bf16[5,512,256]{2,1,0:T(8,128)(2,1)S(1)} %copy-done.21, bf16[512,640]{1,0:T(8,128)(2,1)S(1)} %bitcast.55, bf16[2560,640]{1,0:T(8,128)(2,1)S(1)} %bitcast.44, bf16[64,2560]{1,0:T(8,128)(2,1)S(1)} %get-tuple-element.24.after), custom_call_target="tpu_custom_call" | custom-call | flops 587202560 | bytes 5000000 | tf_op jit(solution)/shard_map/pallas_call | solution.py:352
  141.7 0.0 collective-permute-start.5
  141.8 0.1 collective-permute-start.15
  141.9 1.5 shard_map.120
  143.4 0.8 copy-done.9
  144.3 1.7 %collective-permute-done.15 = bf16[16,640]{1,0:T(8,128)(2,1)S(1)} collective-permute-done((bf16[16,640]{1,0:T(8,128)(2,1)S(1)}, bf16[16,640]{1,0:T(8,128)(2,1)S(1)}, u32[]{:S(2)}, u32[]{:S(2)}) %collective-permute-start.15) | collective-permute-done | bytes 20512 | tf_op jit(solution)/shard_map/ppermute | solution.py:47
  146.0 0.0 all-gather.2.cloned.1.call-done.w_ref
  146.1 1.9 %copy-done.8 = bf16[2560,640]{1,0:T(8,128)(2,1)S(1)} copy-done((bf16[2560,640]{1,0:T(8,128)(2,1)S(1)}, bf16[2560,640]{1,0:T(8,128)(2,1)}, u32[]{:S(2)}) %copy-start.8) | copy-done | bytes 3276824
  148.0 2.0 %shard_map.122 = bf16[16,2560]{1,0:T(8,128)(2,1)S(1)} custom-call(s32[5]{0:T(128)S(1)} %stack.27.pos, bf16[16,640]{1,0:T(8,128)(2,1)S(1)} %fusion.13.context_ref, bf16[2560,640]{1,0:T(8,128)(2,1)S(1)} %copy-done.8), custom_call_target="tpu_custom_call" | custom-call | flops 52428800 | bytes 3300000 | tf_op jit(solution)/shard_map/pallas_call | solution.py:398
  150.0 1.7 collective-permute-start.16
  151.7 1.1 fusion.3
  152.8 0.4 collective-permute-start.6
  153.3 2.7 %collective-permute-start.17 = (bf16[16,640]{1,0:T(8,128)(2,1)S(1)}, bf16[16,640]{1,0:T(8,128)(2,1)S(1)}, u32[]{:S(2)}, u32[]{:S(2)}) collective-permute-start(bf16[16,640]{1,0:T(8,128)(2,1)S(1)} %slice.187), channel_id=1, source_target_pairs={{0,4},{2,6},{4,0},{6,2},{1,5},{3,7},{5,1},{7,3},{8,12},{10,14},{12... | collective-permute-start | bytes 61448 | tf_op jit(solution)/shard_map/ppermute | solution.py:47
  156.0 1.1 fusion.a1_ref
  157.1 6.5 %collective-permute-done.6.b1_ref = bf16[256,640]{1,0:T(8,128)(2,1)S(1)} collective-permute-done((bf16[256,640]{1,0:T(8,128)(2,1)S(1)}, bf16[256,640]{1,0:T(8,128)(2,1)S(1)}, u32[]{:S(2)}, u32[]{:S(2)}) %collective-permute-start.6) | collective-permute-done | bytes 327712 | tf_op jit(solution)/shard_map/ppermute | solution.py:47
  163.7 2.5 %shard_map.121 = bf16[2,256,640]{2,1,0:T(8,128)(2,1)} custom-call(s32[5]{0:T(128)S(1)} %stack.27.pos, bf16[256,640]{1,0:T(8,128)(2,1)S(1)} %copy-done.19, bf16[256,640]{1,0:T(8,128)(2,1)} %collective-permute-done.1.b0_ref, bf16[256,640]{1,0:T(8,128)(2,1)S(1)} %fusion.a1_ref, bf16[256,640]{1,0:T(8,128)(2,1)S(1)} %collective-permute-done.6.b1_ref), custom_call_target="tpu_custom_call" | custom-call | flops 1000000 | bytes 2000000 | tf_op jit(solution)/shard_map/pallas_call | solution.py:374
  166.2 0.7 fusion.7
  (57 shorter events, 0.2 us)
Async XLA Ops:
  7.2 138.9 %all-gather.2.cloned.1.call-start = ((), (), s32[]{:S(2)}) async-start(), calls=%async_computation | async-start | bytes 4096000 | tf_op jit(solution)/shard_map/all_gather | solution.py:244
  7.3 1.9 %copy-start = (bf16[1,2560,640]{2,1,0:T(8,128)(2,1)S(1)}, bf16[1,2560,640]{2,1,0:T(8,128)(2,1)}, u32[]{:S(2)}) copy-start(bf16[1,2560,640]{2,1,0:T(8,128)(2,1)} %param.15) | copy-start | bytes 9830404
  9.3 1.1 copy-start.11
  10.3 1.1 copy-start.13
  11.4 1.1 copy-start.15
  12.5 1.0 copy-start.17
  13.5 7.9 %copy-start.1 = (bf16[1,2560,640]{2,1,0:T(8,128)(2,1)S(1)}, bf16[1,2560,640]{2,1,0:T(8,128)(2,1)}, u32[]{:S(2)}) copy-start(bf16[1,2560,640]{2,1,0:T(8,128)(2,1)} %param.15) | copy-start | bytes 9830404
  18.1 5.1 %collective-permute-start = (bf16[2,256,640]{2,1,0:T(8,128)(2,1)S(1)}, bf16[2,256,640]{2,1,0:T(8,128)(2,1)S(1)}, u32[]{:S(2)}, u32[]{:S(2)}) collective-permute-start(bf16[2,256,640]{2,1,0:T(8,128)(2,1)S(1)} %get-tuple-element.13), channel_id=1, source_target_pairs={{0,2},{2,0},{4,6},{6,4},{1,3},{3,1},{5,7},{7,5},{8,10},{10,8},{12,... | collective-permute-start | bytes 1966088 | tf_op jit(solution)/shard_map/ppermute | solution.py:47
  23.0 3.9 %copy-start.12 = (bf16[1,2,256,640]{3,2,1,0:T(8,128)(2,1)S(1)}, bf16[1,2,256,640]{3,2,1,0:T(8,128)(2,1)}, u32[]{:S(2)}) copy-start(bf16[1,2,256,640]{3,2,1,0:T(8,128)(2,1)} %q_ref.3) | copy-start | bytes 1966084
  24.0 13.4 %collective-permute-start.3 = (bf16[256,640]{1,0:T(8,128)(2,1)}, bf16[256,640]{1,0:T(8,128)(2,1)S(1)}, u32[]{:S(2)}, u32[]{:S(2)}) collective-permute-start(bf16[256,640]{1,0:T(8,128)(2,1)} %fusion.2.after), channel_id=1, source_target_pairs={{8,4},{10,6},{12,0},{14,2},{16,12},{18,14},{20,8},{22,10},{24,20},... | collective-permute-start | bytes 983048 | tf_op jit(solution)/shard_map/ppermute | solution.py:73
  25.4 5.8 %copy-start.18 = (bf16[256,640]{1,0:T(8,128)(2,1)}, bf16[256,640]{1,0:T(8,128)(2,1)S(1)}, u32[]{:S(2)}) copy-start(bf16[256,640]{1,0:T(8,128)(2,1)S(1)} %fusion.1.a0_ref) | copy-start | bytes 983044
  25.4 17.5 %copy-start.14 = (bf16[1,512,640]{2,1,0:T(8,128)(2,1)S(1)}, bf16[1,512,640]{2,1,0:T(8,128)(2,1)}, u32[]{:S(2)}) copy-start(bf16[1,512,640]{2,1,0:T(8,128)(2,1)} %param.14) | copy-start | bytes 1966084
  25.4 17.5 %copy-start.24 = (bf16[1,256,640]{2,1,0:T(8,128)(2,1)S(1)}, bf16[1,256,640]{2,1,0:T(8,128)(2,1)}, u32[]{:S(2)}) copy-start(bf16[1,256,640]{2,1,0:T(8,128)(2,1)} %param.11) | copy-start | bytes 983044
  25.4 17.5 %collective-permute-start.2 = (bf16[256,640]{1,0:T(8,128)(2,1)S(1)}, bf16[256,640]{1,0:T(8,128)(2,1)S(1)}, u32[]{:S(2)}, u32[]{:S(2)}) collective-permute-start(bf16[256,640]{1,0:T(8,128)(2,1)S(1)} %fusion.1.a0_ref), channel_id=1, source_target_pairs={{8,0},{10,2},{12,4},{14,6},{16,8},{18,10},{20,12},{22,14},{24,16},... | collective-permute-start | bytes 983048 | tf_op jit(solution)/shard_map/ppermute | solution.py:73
  42.9 3.2 %copy-start.2 = (bf16[1,2560,640]{2,1,0:T(8,128)(2,1)S(1)}, bf16[1,2560,640]{2,1,0:T(8,128)(2,1)}, u32[]{:S(2)}) copy-start(bf16[1,2560,640]{2,1,0:T(8,128)(2,1)} %param.16) | copy-start | bytes 9830404
  42.9 3.2 %copy-start.4 = (bf16[1,2560,640]{2,1,0:T(8,128)(2,1)S(1)}, bf16[1,2560,640]{2,1,0:T(8,128)(2,1)}, u32[]{:S(2)}) copy-start(bf16[1,2560,640]{2,1,0:T(8,128)(2,1)} %param.17) | copy-start | bytes 9830404
  46.1 4.7 %copy-start.6 = (bf16[512,1280]{1,0:T(8,128)(2,1)}, bf16[512,1280]{1,0:T(8,128)(2,1)S(1)}, u32[]{:S(2)}) copy-start(bf16[512,1280]{1,0:T(8,128)(2,1)S(1)} %get-tuple-element.19.low_ref) | copy-start | bytes 3932164
  46.1 4.7 %copy-start.20 = (bf16[5,512,256]{2,1,0:T(8,128)(2,1)}, bf16[5,512,256]{2,1,0:T(8,128)(2,1)S(1)}, u32[]{:S(2)}) copy-start(bf16[5,512,256]{2,1,0:T(8,128)(2,1)S(1)} %get-tuple-element.18.ds_ref) | copy-start | bytes 3932164
  46.1 4.7 %copy-start.22 = (bf16[256,640]{1,0:T(8,128)(2,1)}, bf16[256,640]{1,0:T(8,128)(2,1)S(1)}, u32[]{:S(2)}) copy-start(bf16[256,640]{1,0:T(8,128)(2,1)S(1)} %get-tuple-element.17) | copy-start | bytes 983044
  46.1 5.9 %copy-start.25 = (bf16[80,640]{1,0:T(8,128)(2,1)S(1)}, bf16[80,640]{1,0:T(8,128)(2,1)}, u32[]{:S(2)}) copy-start(bf16[80,640]{1,0:T(8,128)(2,1)} %param.18) | copy-start | bytes 307204
  50.8 38.3 %collective-permute-start.4 = (bf16[256,2560]{1,0:T(8,128)(2,1)}, bf16[256,2560]{1,0:T(8,128)(2,1)}, u32[]{:S(2)}, u32[]{:S(2)}) collective-permute-start(bf16[256,2560]{1,0:T(8,128)(2,1)} %shard_map.117.rest_0_), channel_id=1, source_target_pairs={{0,2},{2,0},{4,6},{6,4},{1,3},{3,1},{5,7},{7,5},{8,10},{10,8},{12,... | collective-permute-start | bytes 3932168 | tf_op jit(solution)/shard_map/ppermute | solution.py:47
  80.0 1.9 %copy-start.3 = (bf16[1,2560,640]{2,1,0:T(8,128)(2,1)S(1)}, bf16[1,2560,640]{2,1,0:T(8,128)(2,1)}, u32[]{:S(2)}) copy-start(bf16[1,2560,640]{2,1,0:T(8,128)(2,1)} %param.16) | copy-start | bytes 9830404
  82.0 1.9 %copy-start.5 = (bf16[1,2560,640]{2,1,0:T(8,128)(2,1)S(1)}, bf16[1,2560,640]{2,1,0:T(8,128)(2,1)}, u32[]{:S(2)}) copy-start(bf16[1,2560,640]{2,1,0:T(8,128)(2,1)} %param.17) | copy-start | bytes 9830404
  83.9 1.3 copy-start.7
  90.5 7.2 %collective-permute-start.7 = (bf16[64,2560]{1,0:T(8,128)(2,1)S(1)}, bf16[64,2560]{1,0:T(8,128)(2,1)S(1)}, u32[]{:S(2)}, u32[]{:S(2)}) collective-permute-start(bf16[64,2560]{1,0:T(8,128)(2,1)S(1)} %get-tuple-element.24.after), channel_id=1, source_target_pairs={{0,64},{8,72},{16,80},{24,88},{32,96},{40,104},{48,112},{56,120},{... | collective-permute-start | bytes 983048 | tf_op jit(solution)/shard_map/ppermute | solution.py:54
  91.8 19.2 %collective-permute-start.8 = (bf16[64,2560]{1,0:T(8,128)(2,1)S(1)}, bf16[64,2560]{1,0:T(8,128)(2,1)S(1)}, u32[]{:S(2)}, u32[]{:S(2)}) collective-permute-start(bf16[64,2560]{1,0:T(8,128)(2,1)S(1)} %get-tuple-element.22), channel_id=1, source_target_pairs={{0,128},{8,136},{16,144},{24,152},{32,160},{40,168},{48,176},{56,1... | collective-permute-start | bytes 983048 | tf_op jit(solution)/shard_map/ppermute | solution.py:54
  93.5 45.5 %copy-start.16 = (bf16[1,512,640]{2,1,0:T(8,128)(2,1)S(1)}, bf16[1,512,640]{2,1,0:T(8,128)(2,1)}, u32[]{:S(2)}) copy-start(bf16[1,512,640]{2,1,0:T(8,128)(2,1)} %param.13) | copy-start | bytes 1966084
  93.5 45.5 %copy-start.21 = (bf16[5,512,256]{2,1,0:T(8,128)(2,1)S(1)}, bf16[5,512,256]{2,1,0:T(8,128)(2,1)}, u32[]{:S(2)}) copy-start(bf16[5,512,256]{2,1,0:T(8,128)(2,1)} %copy-done.20) | copy-start | bytes 3932164
  93.5 21.1 %collective-permute-start.9 = (bf16[64,2560]{1,0:T(8,128)(2,1)S(1)}, bf16[64,2560]{1,0:T(8,128)(2,1)S(1)}, u32[]{:S(2)}, u32[]{:S(2)}) collective-permute-start(bf16[64,2560]{1,0:T(8,128)(2,1)S(1)} %get-tuple-element.23), channel_id=1, source_target_pairs={{0,192},{8,200},{16,208},{24,216},{32,224},{40,232},{48,240},{56,2... | collective-permute-start | bytes 983048 | tf_op jit(solution)/shard_map/ppermute | solution.py:54
  115.8 9.1 %collective-permute-start.10 = (bf16[16,2560]{1,0:T(8,128)(2,1)S(1)}, bf16[16,2560]{1,0:T(8,128)(2,1)S(1)}, u32[]{:S(2)}, u32[]{:S(2)}) collective-permute-start(bf16[16,2560]{1,0:T(8,128)(2,1)S(1)} %get-tuple-element.25), channel_id=1, source_target_pairs={{0,0},{2,34},{4,4},{6,38},{8,8},{10,42},{12,12},{14,46},{16,16},{1... | collective-permute-start | bytes 245768 | tf_op jit(solution)/shard_map/ppermute | solution.py:64
  117.7 7.2 %collective-permute-start.11 = (bf16[16,2560]{1,0:T(8,128)(2,1)S(1)}, bf16[16,2560]{1,0:T(8,128)(2,1)S(1)}, u32[]{:S(2)}, u32[]{:S(2)}) collective-permute-start(bf16[16,2560]{1,0:T(8,128)(2,1)S(1)} %get-tuple-element.28), channel_id=1, source_target_pairs={{0,8},{2,42},{4,12},{6,46},{8,16},{10,50},{12,20},{14,54},{16,24},... | collective-permute-start | bytes 245768 | tf_op jit(solution)/shard_map/ppermute | solution.py:64
  122.9 6.0 %collective-permute-start.12 = (bf16[16,2560]{1,0:T(8,128)(2,1)S(1)}, bf16[16,2560]{1,0:T(8,128)(2,1)S(1)}, u32[]{:S(2)}, u32[]{:S(2)}) collective-permute-start(bf16[16,2560]{1,0:T(8,128)(2,1)S(1)} %get-tuple-element.27), channel_id=1, source_target_pairs={{0,16},{2,50},{4,20},{6,54},{8,24},{10,58},{12,28},{14,62},{16,32}... | collective-permute-start | bytes 245768 | tf_op jit(solution)/shard_map/ppermute | solution.py:64
  123.8 5.6 %collective-permute-start.13 = (bf16[16,2560]{1,0:T(8,128)(2,1)S(1)}, bf16[16,2560]{1,0:T(8,128)(2,1)S(1)}, u32[]{:S(2)}, u32[]{:S(2)}) collective-permute-start(bf16[16,2560]{1,0:T(8,128)(2,1)S(1)} %get-tuple-element.26), channel_id=1, source_target_pairs={{0,24},{2,58},{4,28},{6,62},{8,32},{10,2},{12,36},{14,6},{16,40},{... | collective-permute-start | bytes 245768 | tf_op jit(solution)/shard_map/ppermute | solution.py:64
  123.8 33.3 %collective-permute-start.1 = (bf16[256,640]{1,0:T(8,128)(2,1)}, bf16[256,640]{1,0:T(8,128)(2,1)}, u32[]{:S(2)}, u32[]{:S(2)}) collective-permute-start(bf16[256,640]{1,0:T(8,128)(2,1)} %fusion.2.after), channel_id=1, source_target_pairs={{0,4},{2,6},{4,0},{6,2},{1,5},{3,7},{5,1},{7,3},{8,12},{10,14},{12... | collective-permute-start | bytes 983048 | tf_op jit(solution)/shard_map/ppermute | solution.py:47
  129.4 12.3 %collective-permute-start.14 = (bf16[16,1280]{1,0:T(8,128)(2,1)S(1)}, bf16[16,1280]{1,0:T(8,128)(2,1)S(1)}, u32[]{:S(2)}, u32[]{:S(2)}) collective-permute-start(bf16[16,1280]{1,0:T(8,128)(2,1)S(1)} %slice.186), channel_id=1, source_target_pairs={{0,2},{2,0},{4,6},{6,4},{1,3},{3,1},{5,7},{7,5},{8,10},{10,8},{12,... | collective-permute-start | bytes 122888 | tf_op jit(solution)/shard_map/ppermute | solution.py:47
  141.7 10.0 %collective-permute-start.5 = (bf16[2,256,640]{2,1,0:T(8,128)(2,1)}, bf16[2,256,640]{2,1,0:T(8,128)(2,1)}, u32[]{:S(2)}, u32[]{:S(2)}) collective-permute-start(bf16[2,256,640]{2,1,0:T(8,128)(2,1)} %get-tuple-element.21), channel_id=1, source_target_pairs={{0,2},{2,0},{4,6},{6,4},{1,3},{3,1},{5,7},{7,5},{8,10},{10,8},{12,... | collective-permute-start | bytes 1966088 | tf_op jit(solution)/shard_map/ppermute | solution.py:47
  141.8 4.2 %collective-permute-start.15 = (bf16[16,640]{1,0:T(8,128)(2,1)S(1)}, bf16[16,640]{1,0:T(8,128)(2,1)S(1)}, u32[]{:S(2)}, u32[]{:S(2)}) collective-permute-start(bf16[16,640]{1,0:T(8,128)(2,1)S(1)} %slice.188), channel_id=1, source_target_pairs={{0,4},{2,6},{4,0},{6,2},{1,5},{3,7},{5,1},{7,3},{8,12},{10,14},{12... | collective-permute-start | bytes 61448 | tf_op jit(solution)/shard_map/ppermute | solution.py:47
  143.4 0.8 copy-start.9
  146.1 1.9 %copy-start.8 = (bf16[2560,640]{1,0:T(8,128)(2,1)S(1)}, bf16[2560,640]{1,0:T(8,128)(2,1)}, u32[]{:S(2)}) copy-start(bf16[2560,640]{1,0:T(8,128)(2,1)} %all-gather.2.cloned.1.call-done.w_ref) | copy-start | bytes 9830404
  148.0 3.8 %copy-start.10 = (bf16[2,256,640]{2,1,0:T(8,128)(2,1)S(1)}, bf16[2,256,640]{2,1,0:T(8,128)(2,1)}, u32[]{:S(2)}) copy-start(bf16[2,256,640]{2,1,0:T(8,128)(2,1)} %copy-done.9) | copy-start | bytes 1966084
  150.0 6.0 %copy-start.23 = (bf16[256,640]{1,0:T(8,128)(2,1)S(1)}, bf16[256,640]{1,0:T(8,128)(2,1)}, u32[]{:S(2)}) copy-start(bf16[256,640]{1,0:T(8,128)(2,1)} %copy-done.22) | copy-start | bytes 983044
  150.0 13.7 %copy-start.19 = (bf16[256,640]{1,0:T(8,128)(2,1)S(1)}, bf16[256,640]{1,0:T(8,128)(2,1)}, u32[]{:S(2)}) copy-start(bf16[256,640]{1,0:T(8,128)(2,1)} %copy-done.18) | copy-start | bytes 983044
  150.0 3.2 %collective-permute-start.16 = (bf16[16,1280]{1,0:T(8,128)(2,1)S(1)}, bf16[16,1280]{1,0:T(8,128)(2,1)S(1)}, u32[]{:S(2)}, u32[]{:S(2)}) collective-permute-start(bf16[16,1280]{1,0:T(8,128)(2,1)S(1)} %slice.145), channel_id=1, source_target_pairs={{0,2},{2,0},{4,6},{6,4},{1,3},{3,1},{5,7},{7,5},{8,10},{10,8},{12,... | collective-permute-start | bytes 122888 | tf_op jit(solution)/shard_map/ppermute | solution.py:47
  152.8 10.9 %collective-permute-start.6 = (bf16[256,640]{1,0:T(8,128)(2,1)S(1)}, bf16[256,640]{1,0:T(8,128)(2,1)S(1)}, u32[]{:S(2)}, u32[]{:S(2)}) collective-permute-start(bf16[256,640]{1,0:T(8,128)(2,1)S(1)} %fusion.3), channel_id=1, source_target_pairs={{0,4},{2,6},{4,0},{6,2},{1,5},{3,7},{5,1},{7,3},{8,12},{10,14},{12... | collective-permute-start | bytes 983048 | tf_op jit(solution)/shard_map/ppermute | solution.py:47
  153.3 12.9 %collective-permute-start.17 = (bf16[16,640]{1,0:T(8,128)(2,1)S(1)}, bf16[16,640]{1,0:T(8,128)(2,1)S(1)}, u32[]{:S(2)}, u32[]{:S(2)}) collective-permute-start(bf16[16,640]{1,0:T(8,128)(2,1)S(1)} %slice.187), channel_id=1, source_target_pairs={{0,4},{2,6},{4,0},{6,2},{1,5},{3,7},{5,1},{7,3},{8,12},{10,14},{12... | collective-permute-start | bytes 61448 | tf_op jit(solution)/shard_map/ppermute | solution.py:47
  157.1 9.1 %copy-start.26 = (bf16[640,16]{0,1:T(8,128)(2,1)S(1)}, bf16[640,16]{0,1:T(8,128)(2,1)}, u32[]{:S(2)}) copy-start(bf16[640,16]{0,1:T(8,128)(2,1)} %param.19) | copy-start | bytes 61444
Sparse Core Ops, SparseCore 0:
  80.2 55.6 all-gather.1

commit v2 on v0

v2 whole, which is shorter than its diff:
```python
import functools
import math

import jax
import jax.numpy as jnp
from jax import lax
from jax.experimental import pallas as pl
from jax.experimental.pallas import tpu as pltpu
from jax.sharding import PartitionSpec as P

HEAD = 128
NX, NZ = 4, 8
SECTIONS = NX * NZ
TENSOR = 4
VMEM_LIMIT = 20 * 1024 * 1024
F32 = jnp.float32
BF16 = jnp.bfloat16
NT = (((1,), (1,)), ((), ()))
NN = (((1,), (0,)), ((), ()))
TN = (((0,), (0,)), ((), ()))


def dot(a, b, dims):
    return lax.dot_general(a, b, dims, preferred_element_type=F32)


def positions():
    section = lax.axis_index("section")
    tensor = lax.axis_index("tensor")
    return jnp.stack(
        [
            section // NZ,
            section % NZ,
            tensor // 2,
            tensor % 2,
            (section == SECTIONS - 1).astype(jnp.int32),
        ]
    ).astype(jnp.int32)


def block_for(pos, j, other):
    core = pos[3] ^ other
    return (pos[2] ^ (j % 2)) * 2 + (core ^ (j // 2))


def swap_tensor(value, bit):
    return lax.ppermute(value, "tensor", [(i, i ^ bit) for i in range(TENSOR)])


def send_x(value, step):
    pairs = [
        (x * NZ + z, ((x + step) % NX) * NZ + z) for x in range(NX) for z in range(NZ)
    ]
    return lax.ppermute(value, "section", pairs)


def send_z(value, step):
    pairs = []
    for x in range(NX):
        for z in range(NZ):
            for t in range(TENSOR):
                to = (z + step + 4 * (t % 2)) % NZ
                pairs.append(((x * NZ + z) * TENSOR + t, (x * NZ + to) * TENSOR + t))
    return lax.ppermute(value, ("section", "tensor"), pairs)


def turn(value, bits):
    pairs = [
        ((x * NZ + z) * TENSOR + t, (t * NZ + (z ^ bits)) * TENSOR + x)
        for x in range(NX)
        for z in range(NZ)
        for t in range(TENSOR)
    ]
    return lax.ppermute(value, ("section", "tensor"), pairs)


def swap_z(value, bits):
    pairs = [(s, s // NZ * NZ + ((s % NZ) ^ bits)) for s in range(SECTIONS)]
    return lax.ppermute(value, "section", pairs)


def from_z(value, step):
    pairs = [(s, s // NZ * NZ + (s - step) % NZ) for s in range(SECTIONS)]
    return lax.ppermute(value, "section", pairs)


def pass_back(value):
    return lax.ppermute(value, "section", [(s + 1, s) for s in range(SECTIONS - 1)])


def weights_of(q, k):
    factor = HEAD ** (-0.5) * math.log2(math.e)
    scores = dot(k, q, NT)
    peak = jnp.max(scores, axis=0, keepdims=True)
    shifted = jnp.exp2((scores - peak) * factor)
    return shifted, 1.0 / jnp.sum(shifted, axis=0, keepdims=True)


def score_gradient(shifted, factor, v, g):
    attention_grad = dot(v, g, NT)
    row_dot = jnp.sum(shifted * attention_grad, axis=0, keepdims=True) * factor
    return (shifted * (attention_grad * factor - row_dot * factor)).astype(BF16)


def heads_of(width):
    return [slice(i, i + HEAD) for i in range(0, width, HEAD)]

HBM = pl.BlockSpec(memory_space=pltpu.HBM)
VMEM = pl.BlockSpec(memory_space=pltpu.VMEM)
ANY = pl.BlockSpec(memory_space=pl.ANY)


def call(body, ins, outs, scratch=(), place=VMEM):
    arrays = [
        pltpu.with_memory_space_constraint(array, pltpu.HBM) if spec is HBM else array
        for array, spec in ins
    ]
    shapes = [jax.ShapeDtypeStruct(*out) for out in outs]
    return pl.pallas_call(
        body,
        in_specs=[spec for array, spec in ins],
        out_specs=[place] * len(shapes),
        out_shape=shapes,
        scratch_shapes=list(scratch),
        compiler_params=pltpu.CompilerParams(vmem_limit_bytes=VMEM_LIMIT),
        cost_estimate=pl.CostEstimate(flops=1, bytes_accessed=1, transcendentals=0),
    )(*arrays)


def copies(pairs, sems):
    started = []
    for i, (source, target) in enumerate(pairs):
        started.append(pltpu.make_async_copy(source, target, sems.at[i]))
        started[-1].start()
    return started


def rows_of(ref, block, count):
    return ref[pl.ds(pl.multiple_of(block * count, count), count), :]


def first_kernel(
    pos, q_hbm, k_hbm, v_hbm, g_hbm, w_hbm, dq_ref, w_ref, g_ref, q_ref, k_ref, v_ref, sems
):
    width = k_ref.shape[-1]
    heads = heads_of(width)
    pairs = []
    for h in heads:
        pairs.append((k_hbm.at[0, :, h], k_ref.at[:, h]))
        pairs.append((q_hbm.at[0, 0, :, h], q_ref.at[:, h]))
        pairs.append((v_hbm.at[0, :, h], v_ref.at[:, h]))
        pairs.append((g_hbm.at[0, :, h], g_ref.at[:, h]))
    pairs.append((w_hbm.at[0], w_ref))
    started = copies(pairs, sems)
    for i, h in enumerate(heads):
        for copy in started[4 * i : 4 * i + 4]:
            copy.wait()
        k = k_ref[:, h]
        shifted, factor = weights_of(q_ref[:, h], k)
        score_grad = score_gradient(shifted, factor, v_ref[:, h], g_ref[:, h])
        dq_ref[:, h] = (dot(score_grad, k, TN) * HEAD ** (-0.5)).astype(BF16)
    started[-1].wait()


def project_kernel(other, pos, dq_ref, w_ref, *rest):
    out_ref = rest[-1]
    width = w_ref.shape[-1]
    for j in range(2):
        weight = rows_of(w_ref, block_for(pos, j, other), width)
        out_ref[j] = dot(dq_ref[...], weight, NT).astype(BF16)


def meet_core_kernel(pos, g_ref, keep_ref, came_ref, near_ref, far_ref):
    near = keep_ref[0].astype(F32) + came_ref[0].astype(F32)
    near_ref[...] = near + g_ref[...].astype(F32)
    far_ref[...] = (keep_ref[1].astype(F32) + came_ref[1].astype(F32)).astype(BF16)


def meet_far_kernel(pos, near_ref, far_ref, text_a, text_b, after, out_ref, text_ref):
    out_ref[...] = (near_ref[...] + far_ref[...].astype(F32)).astype(BF16)
    text_ref[0] = text_a[...]
    text_ref[1] = text_b[...]


def between_kernel(
    pos,
    q_hbm,
    k_hbm,
    v_hbm,
    g_hbm,
    top_hbm,
    wk_hbm,
    wv_hbm,
    after,
    dk_ref,
    dv_ref,
    q_ref,
    k_ref,
    v_ref,
    top_ref,
    wk_ref,
    wv_ref,
    q0_ref,
    g_ref,
    sems,
):
    pairs = [(q_hbm.at[0, 0], q0_ref), (g_hbm.at[0], g_ref)]
    rows = k_ref.shape[0] // SECTIONS
    for other in range(2):
        core = pos[3] ^ (1 - other)
        for kz in range(NZ // 2):
            to_z = (pos[1] + kz + 4 * core) % NZ
            for to_x in range(NX):
                source = pl.ds(pl.multiple_of((to_x * NZ + to_z) * rows, rows), rows)
                place = pl.ds(((other * (NZ // 2) + kz) * NX + to_x) * rows, rows)
                pairs.append((k_hbm.at[0, source], k_ref.at[place]))
                pairs.append((v_hbm.at[0, source], v_ref.at[place]))
    first = len(pairs)
    pairs.append((q_hbm.at[0, 1], q_ref))
    pairs.append((top_hbm.at[0], top_ref))
    pairs.append((wk_hbm.at[0], wk_ref))
    pairs.append((wv_hbm.at[0], wv_ref))
    started = copies(pairs, sems)
    for copy in started[:first]:
        copy.wait()
    for h in heads_of(k_ref.shape[-1]):
        q = q0_ref[:, h]
        g = g_ref[:, h]
        shifted, factor = weights_of(q, k_ref[:, h])
        score_grad = score_gradient(shifted, factor, v_ref[:, h], g)
        dk_ref[:, h] = dot(score_grad, q, NN) * HEAD ** (-0.5)
        dv_ref[:, h] = dot((shifted * factor).astype(BF16), g, NN)
    for copy in started[first:]:
        copy.wait()


def ahead_kernel(pos, q_ref, k_ref, after, p_ref, low_ref):
    for i, h in enumerate(heads_of(k_ref.shape[-1])):
        shifted, factor = weights_of(q_ref[:, h], k_ref[:, h])
        attention = shifted * factor
        p_ref[i] = attention
        low_ref[i] = attention.astype(BF16)


def second_kernel(
    pos, q_ref, v_ref, came_ref, top_ref, dk_ref, dv_ref, p_ref, p_low_ref, g_ref, ds_ref, low_ref
):
    width = q_ref.shape[-1]
    g_ref[...] = jnp.where(pos[4] == 1, top_ref[...].astype(F32), came_ref[...].astype(F32)).astype(
        BF16
    )
    for i, h in enumerate(heads_of(width)):
        g = g_ref[:, h]
        attention_grad = dot(v_ref[:, h], g, NT)
        row_dot = jnp.sum(p_ref[i] * attention_grad, axis=0, keepdims=True)
        score_grad = (p_ref[i] * (attention_grad - row_dot)).astype(BF16)
        ds_ref[i] = score_grad
        dk = dk_ref[:, h] + dot(score_grad, q_ref[:, h], NN) * HEAD ** (-0.5)
        dv = dv_ref[:, h] + dot(p_low_ref[i], g, NN)
        low_ref[:, h] = dk.astype(BF16)
        low_ref[:, slice(width + h.start, width + h.stop)] = dv.astype(BF16)


def context_block(pos, step, half, low_ref, kw_ref, vw_ref):
    width = kw_ref.shape[-1]
    count = low_ref.shape[0] // 2
    rows = slice(half * count, (half + 1) * count)
    block = (pos[0] + step) % NX
    total = dot(rows_of(kw_ref, block, width), low_ref[rows, :width], NT)
    return total + dot(rows_of(vw_ref, block, width), low_ref[rows, width:], NT)


def context_kernel(half, pos, low_ref, kw_ref, vw_ref, *rest):
    out_ref = rest[-1]
    for step in range(NX):
        total = context_block(pos, step, half, low_ref, kw_ref, vw_ref)
        out_ref[step] = total.astype(BF16)


def x_add_kernel(pos, keep_ref, came_ref, two_ref, late_two, *outs):
    late_two[...] = two_ref[...]
    for i, out in enumerate(outs):
        out[...] = (keep_ref[i + 1].astype(F32) + came_ref[i + 1].astype(F32)).astype(BF16)


def z_add_kernel(pos, keep_ref, came_ref, b_ref, c_ref, d_ref, *outs):
    rows = outs[0].shape[0]
    width = outs[0].shape[1]
    for place in (slice(0, width // 2), slice(width // 2, width)):
        total = keep_ref[0, place, :].astype(F32) + came_ref[0, place, :].astype(F32)
        total = total + b_ref[place, :].astype(F32)
        total = total + c_ref[place, :].astype(F32) + d_ref[place, :].astype(F32)
        total = total.T.astype(BF16)
        for j, out in enumerate(outs):
            out[:, place] = total[j * rows : (j + 1) * rows]


def third_kernel(
    pos,
    ds_ref,
    k_ref,
    w_ref,
    g_ref,
    after,
    near_ref,
    far_out,
    core_out,
    both_out,
    dq_ref,
):
    width = w_ref.shape[-1]
    for i, h in enumerate(heads_of(width)):
        dq_ref[:, h] = (dot(ds_ref[i], k_ref[:, h], TN) * HEAD ** (-0.5)).astype(BF16)
    for j, out in enumerate((near_ref, far_out, core_out, both_out)):
        weight = rows_of(w_ref, block_for(pos, j, 0), width)
        total = dot(dq_ref[...], weight, NT)
        if j == 0:
            total = total + g_ref[...].astype(F32)
        out[...] = total.astype(out.dtype)


def z_sum_kernel(pos, a_ref, b_ref, c_ref, d_ref, after, keep_ref, send_ref):
    total = a_ref[...].astype(F32) + b_ref[...].astype(F32)
    total = total + c_ref[...].astype(F32) + d_ref[...].astype(F32)
    keep_ref[...] = total
    send_ref[...] = total.astype(BF16)


def core_sum_kernel(pos, keep_ref, came_ref, out_ref, send_ref):
    total = keep_ref[...] + came_ref[...].astype(F32)
    out_ref[...] = total
    send_ref[...] = total.astype(BF16)


def text_kernel(pos, keep_ref, far_ref, own, two, up, down, *rest):
    *outs, context_ref, w_ref = rest
    rows = own.shape[1]
    places = (pos[1], pos[1] ^ 2, (pos[1] + 1) % NZ, (pos[1] + NZ - 1) % NZ)
    for ref, z in zip((own, two, up, down), places):
        for r in range(2):
            row = pl.multiple_of((z ^ (4 * r)) * rows, rows)
            w_ref[pl.ds(row, rows), :] = ref[r]
    context_ref[...] = (keep_ref[...] + far_ref[...].astype(F32)).astype(BF16)
    tokens = outs[0].shape[0]
    for i, out in enumerate(outs):
        row = pl.multiple_of((pos[0] + i) % NX * tokens, tokens)
        total = dot(context_ref[pl.ds(row, tokens), :], w_ref[...], NT)
        out[...] = total.astype(out.dtype)


def sent_kernel(pos, first_ref, a_ref, b_ref, c_ref, d_ref, out_hbm, out_ref, sems):
    out_ref[0] = first_ref[...]
    total = a_ref[...] + b_ref[...].astype(F32)
    total = total + c_ref[...].astype(F32) + d_ref[...].astype(F32)
    out_ref[1] = total.astype(BF16)
    copies([(out_ref, out_hbm)], sems)[0].wait()


def smooth_gate(inputs):
    return jax.nn.gelu(inputs, approximate=True)


def gelu_slope(inputs):
    unused_out, backward = jax.vjp(smooth_gate, inputs)
    return backward(jnp.ones_like(inputs))[0]


def shards(
    grad_in,
    grad_top,
    queries,
    keys,
    values,
    query_weight,
    key_weight,
    value_weight,
    text_weight,
    text_hidden,
):
    pos = positions()
    rows, width = grad_in.shape[1], grad_in.shape[2]
    text = keys.shape[1]
    heads = width // HEAD
    model = width * TENSOR
    where = (pos, pl.BlockSpec(memory_space=pltpu.SMEM))

    act = ((rows, width), BF16)
    pair = ((2, rows, width), BF16)
    square = ((text, width), F32)
    narrow = ((text, width), BF16)
    matrix = ((model, width), BF16)

    def vm(*shape_dtype):
        return pltpu.VMEM(*shape_dtype)

    def dma(count):
        return pltpu.SemaphoreType.DMA((count,))

    block = text_weight.shape
    text_a, text_b = turn(text_weight, 0), turn(text_weight, 4)

    dq0, wq, g_first = call(
        first_kernel,
        [where, (queries, HBM), (keys, HBM), (values, HBM), (grad_in, HBM), (query_weight, HBM)],
        [act, matrix, act],
        [vm(*act), vm(*narrow), vm(*narrow), dma(4 * heads + 1)],
    )
    def project(other, *after):
        return call(
            functools.partial(project_kernel, other),
            [where, (dq0, VMEM), (wq, VMEM)] + [(a, ANY) for a in after],
            [pair],
        )[0]

    send0 = project(1)
    came0 = swap_tensor(send0, 1)
    keep0 = project(0, send0)
    near0, far0 = call(
        meet_core_kernel,
        [where] + [(a, VMEM) for a in (g_first, keep0, came0)],
        [((rows, width), F32), act],
    )
    far0_back = swap_tensor(far0, 2)

    dk0, dv0, q1, k, v, top, wk, wv = call(
        between_kernel,
        [
            where,
            (queries, HBM),
            (keys, HBM),
            (values, HBM),
            (grad_in, HBM),
            (grad_top, HBM),
            (key_weight, HBM),
            (value_weight, HBM),
            (far0, ANY),
        ],
        [square, square, act, narrow, narrow, act, matrix, matrix],
        [vm(*act), vm(*act), dma(2 * SECTIONS + 6)],
    )

    sent0, text_two = call(
        meet_far_kernel,
        [where] + [(a, VMEM) for a in (near0, far0_back, text_a, text_b)]
        + [(dk0, ANY)],
        [act, ((2,) + block, BF16)],
    )
    came_back = pass_back(sent0)
    p1, p1_low = call(
        ahead_kernel,
        [where, (q1, VMEM), (k, VMEM), (sent0, ANY)],
        [((heads, text, rows), F32), ((heads, text, rows), BF16)],
    )

    g1, ds1, low = call(
        second_kernel,
        [where] + [(a, VMEM) for a in (q1, v, came_back, top, dk0, dv0, p1, p1_low)],
        [act, ((heads, text, rows), BF16), ((text, 2 * width), BF16)],
    )

    terms = ((NX, width, text // 2), BF16)
    (send,) = call(
        functools.partial(context_kernel, 0), [where, (low, VMEM), (wk, VMEM), (wv, VMEM)], [terms]
    )
    came = swap_tensor(send, 1)
    (keep,) = call(
        functools.partial(context_kernel, 1),
        [where, (low, VMEM), (wk, VMEM), (wv, VMEM), (send, ANY)],
        [terms],
    )
    text_two, *by_x = call(
        x_add_kernel,
        [where, (keep, VMEM), (came, VMEM), (text_two, VMEM)],
        [((2,) + block, BF16)] + [((width, text // 2), BF16)] * (NX - 1),
    )
    came_x = [send_x(piece, i + 1) for i, piece in enumerate(by_x)]
    text_more = [swap_z(text_two, 2), from_z(text_two, 1), from_z(text_two, -1)]

    near1, far1, core1, both1 = call(
        third_kernel,
        [where, (ds1, VMEM), (k, VMEM), (wq, VMEM), (g1, VMEM), (by_x[1], ANY)],
        [((rows, width), F32)] + [act] * 3,
        [vm(*act)],
    )
    others = (
        near1,
        swap_tensor(far1, 2),
        swap_tensor(core1, 1),
        swap_tensor(both1, 3),
    )
    (sent,) = call(
        sent_kernel,
        [where, (sent0, VMEM)] + [(a, VMEM) for a in others],
        [pair],
        [vm(*pair), dma(1)],
        ANY,
    )

    few = text // NZ
    by_z = call(
        z_add_kernel,
        [where] + [(a, VMEM) for a in (keep, came, *came_x)],
        [((few, width), BF16)] * (NZ // 2),
    )
    came_z = [send_z(by_z[i], i) for i in range(NZ // 2)]
    context, context_low = call(
        z_sum_kernel,
        [where] + [(a, VMEM) for a in came_z] + [(sent, HBM)],
        [((few, width), F32), ((few, width), BF16)],
    )
    context, context_low = call(
        core_sum_kernel,
        [where, (context, VMEM), (swap_tensor(context_low, 1), VMEM)],
        [((few, width), F32), ((few, width), BF16)],
    )
    far_context = swap_tensor(context_low, 2)
    tokens = few // NX
    hidden, *to_send = call(
        text_kernel,
        [where] + [(a, VMEM) for a in (context, far_context, text_two, *text_more)],
        [((tokens, width), F32)] + [((tokens, width), BF16)] * (NX - 1),
        [vm((few, width), BF16), vm((width, width), BF16)],
    )
    for i, piece in enumerate(to_send):
        hidden = hidden + send_x(piece, i + 1).astype(F32)
    text_grad = hidden.T * gelu_slope(text_hidden.astype(F32))
    return (sent[None], text_grad)


def solution(mesh):
    placed = (
        P("section", "dp", "tensor"),
        P(None, "dp", "tensor"),
        P("section", None, "dp", "tensor"),
        P("section", "dp", "tensor"),
        P("section", "dp", "tensor"),
        P("section", None, "tensor"),
        P("section", None, "tensor"),
        P("section", None, "tensor"),
        P("section", "tensor"),
        P("tensor", ("dp", "section")),
    )
    return jax.shard_map(
        shards,
        mesh=mesh,
        in_specs=placed,
        out_specs=(P("section", None, "dp", "tensor"), P("tensor", ("dp", "section"))),
        check_vma=False,
    )
```

time: 471 us -> 115 us (0.24)
  waiting for transfers between devices: 375 us -> 22.2 us
  starting transfers between devices: 1.71 us -> 56.5 us
  matrix products: 38 us -> 0 us
  Pallas kernels: 0 us -> 34.3 us
  local copies, waits for them, and re-layouts: 32.5 us -> 0.1 us
  between operations: 15.9 us -> 0.9 us
  other arithmetic: 7.52 us -> 0.66 us
    reduce_scatter x1 -> x0, waiting for transfers between devices: 193 us -> none  [shards(): lax.psum_scatter(context_local, 'section', scatter_dimension=1, tiled=True)]
    unnamed x10 -> x0, waiting for transfers between devices: 159 us -> none
    ppermute x1 -> x24, starting transfers between devices: 1.46 us -> 56.5 us  [the longest x8 19.7 us: swap_tensor(): return lax.ppermute(value, 'tensor', [(i, i ^ bit) for i in range(TENSOR)])]
    pallas_call x0 -> x17, Pallas kernels: none -> 34.3 us  [call(): pl.pallas_call(body, in_specs=[spec for array, spec in ins], out_specs=[p...]
    dot_general x13 -> x0, matrix products: 30.6 us -> none  [the longest x2 6.57 us: shards(): lax.dot_general(query_grad, weight_rows, (((1,), (1,)), ((), ())), prefer...]
    unnamed x39 -> x4, local copies, waits for them, and re-layouts: 30.5 us -> 0.01 us
    ppermute x1 -> x24, waiting for transfers between devices: 0.01 us -> 22.2 us  [the longest x1 8.7 us: swap_z(): return lax.ppermute(value, 'section', pairs)]
    all_gather x1 -> x0, waiting for transfers between devices: 22.1 us -> none  [shards(): lax.all_gather(text_weight, 'section', axis=0, tiled=True)]
  transfers between devices with their start and end apart: 7 -> 24, of which waited for: 6 -> 12; matrix products, arithmetic and copies ran while one was open for 7% -> 0% of each run, Pallas kernels for 0% -> 15%
where the time goes in v2:
time: 115 us
  starting transfers between devices  56.5 us (49%)
  Pallas kernels  34.3 us (30%)
  waiting for transfers between devices  22.2 us (19%)
    pallas_call x17, Pallas kernels, call(): pl.pallas_call(body, in_specs=[spec for array, spec in ins], out_specs=[p...  34.3 us
    ppermute x8, starting transfers between devices, swap_tensor(): return lax.ppermute(value, 'tensor', [(i, i ^ bit) for i in range(TENSOR)])  19.7 us
    ppermute x6, starting transfers between devices, send_x(): return lax.ppermute(value, 'section', pairs)  11.8 us
    ppermute x2, starting transfers between devices, turn(): return lax.ppermute(value, ('section', 'tensor'), pairs)  10.3 us
    ppermute x4, starting transfers between devices, send_z(): return lax.ppermute(value, ('section', 'tensor'), pairs)  9.52 us
    ppermute x1, waiting for transfers between devices, swap_z(): return lax.ppermute(value, 'section', pairs)  8.7 us
    ppermute x1, waiting for transfers between devices, pass_back(): lax.ppermute(value, 'section', [(s + 1, s) for s in range(SECTIONS - 1)])  6.8 us
    ppermute x2, starting transfers between devices, from_z(): return lax.ppermute(value, 'section', pairs)  2.75 us
  transfers between devices with their start and end apart: 24, of which 12 were waited for; matrix products, arithmetic and copies ran while one was open for 0% of the time, Pallas kernels for 15%

profile of v2, /device:TPU:1, one launch (start us, length us, event | category | flops | bytes accessed | tf_op | source)
XLA Modules:
  0.0 114.7 jit_solution(6390192370832039763)
XLA Ops:
  0.7 0.1 stack.27.pos
  0.8 5.8 %shard_map.113 = (bf16[256,640]{1,0:T(8,128)(2,1)S(1)}, bf16[2560,640]{1,0:T(8,128)(2,1)S(1)}, bf16[256,640]{1,0:T(8,128)(2,1)S(1)}) custom-call(s32[5]{0:T(128)S(1)} %stack.27.pos, bf16[1,2,256,640]{3,2,1,0:T(8,128)(2,1)} %q_hbm.3, bf16[1,512,640]{2,1,0:T(8,128)(2,1)} %k_hbm.3, bf16[1,512,640]{2,1,0:T(8,128)(2,1)} %v_hbm.3, bf16[1,256,640]{2,1,0:T(8,128)(2,1)} %g_hbm.3, ...), custom_call_target="tpu_custom_call" | custom-call | flops 1 | bytes 1 | tf_op jit(solution)/shard_map/pallas_call | solution.py:119
  6.6 1.4 %shard_map.114.rest_0_ = bf16[2,256,640]{2,1,0:T(8,128)(2,1)S(1)} custom-call(s32[5]{0:T(128)S(1)} %stack.27.pos, bf16[256,640]{1,0:T(8,128)(2,1)S(1)} %get-tuple-element.43.dq_ref, bf16[2560,640]{1,0:T(8,128)(2,1)S(1)} %get-tuple-element.44.w_ref), custom_call_target="tpu_custom_call" | custom-call | flops 1 | bytes 1 | tf_op jit(solution)/shard_map/pallas_call | solution.py:119
  7.9 3.3 %collective-permute-start = (bf16[2,256,640]{2,1,0:T(8,128)(2,1)S(1)}, bf16[2,256,640]{2,1,0:T(8,128)(2,1)S(1)}, u32[]{:S(2)}, u32[]{:S(2)}) collective-permute-start(bf16[2,256,640]{2,1,0:T(8,128)(2,1)S(1)} %shard_map.114.rest_0_), channel_id=1, source_target_pairs={{0,2},{2,0},{4,6},{6,4},{1,3},{3,1},{5,7},{7,5},{8,10},{10,8},{12,... | collective-permute-start | bytes 1966088 | tf_op jit(solution)/shard_map/ppermute | solution.py:47
  11.2 1.4 %shard_map.115.keep_ref = bf16[2,256,640]{2,1,0:T(8,128)(2,1)S(1)} custom-call(s32[5]{0:T(128)S(1)} %stack.27.pos, bf16[256,640]{1,0:T(8,128)(2,1)S(1)} %get-tuple-element.43.dq_ref, bf16[2560,640]{1,0:T(8,128)(2,1)S(1)} %get-tuple-element.44.w_ref, bf16[2,256,640]{2,1,0:T(8,128)(2,1)S(1)} %shard_map.114.rest_0_), custom_call_target="tpu_custom_call" | custom-call | flops 1 | bytes 1 | tf_op jit(solution)/shard_map/pallas_call | solution.py:119
  12.6 0.0 copy-start.1
  12.6 0.3 collective-permute-done.came_ref
  13.0 0.7 shard_map.116
  13.7 1.3 %collective-permute-start.1 = (bf16[256,640]{1,0:T(8,128)(2,1)S(1)}, bf16[256,640]{1,0:T(8,128)(2,1)S(1)}, u32[]{:S(2)}, u32[]{:S(2)}) collective-permute-start(bf16[256,640]{1,0:T(8,128)(2,1)S(1)} %get-tuple-element.46.after), channel_id=1, source_target_pairs={{0,4},{2,6},{4,0},{6,2},{1,5},{3,7},{5,1},{7,3},{8,12},{10,14},{12... | collective-permute-start | bytes 983048 | tf_op jit(solution)/shard_map/ppermute | solution.py:47
  15.0 8.4 %collective-permute-start.3 = (bf16[80,640]{1,0:T(8,128)(2,1)S(1)}, bf16[80,640]{1,0:T(8,128)(2,1)S(1)}, u32[]{:S(2)}, u32[]{:S(2)}) collective-permute-start(bf16[80,640]{1,0:T(8,128)(2,1)S(1)} %copy-done.1), channel_id=1, source_target_pairs={{0,32},{2,96},{4,160},{6,224},{8,40},{10,104},{12,168},{14,232},{1... | collective-permute-start | bytes 307208 | tf_op jit(solution)/shard_map/ppermute | solution.py:74
  23.3 1.9 %collective-permute-start.2 = (bf16[80,640]{1,0:T(8,128)(2,1)S(1)}, bf16[80,640]{1,0:T(8,128)(2,1)S(1)}, u32[]{:S(2)}, u32[]{:S(2)}) collective-permute-start(bf16[80,640]{1,0:T(8,128)(2,1)S(1)} %copy-done.1), channel_id=1, source_target_pairs={{0,0},{2,64},{4,128},{6,192},{8,8},{10,72},{12,136},{14,200},{16,1... | collective-permute-start | bytes 307208 | tf_op jit(solution)/shard_map/ppermute | solution.py:74
  25.3 5.8 %shard_map.117 = (f32[512,640]{1,0:T(8,128)S(1)}, f32[512,640]{1,0:T(8,128)S(1)}, bf16[256,640]{1,0:T(8,128)(2,1)S(1)}, bf16[512,640]{1,0:T(8,128)(2,1)S(1)}, bf...) custom-call(s32[5]{0:T(128)S(1)} %stack.27.pos, ...), custom_call_target="tpu_custom_call" | custom-call | flops 1 | bytes 1 | tf_op jit(solution)/shard_map/pallas_call | solution.py:119
  31.0 0.0 collective-permute-done.3.text_b
  31.0 0.0 collective-permute-done.2.text_a
  31.1 0.0 collective-permute-done.1.far_ref
  31.1 0.6 shard_map.118
  31.7 1.5 %collective-permute-start.4 = (bf16[256,640]{1,0:T(8,128)(2,1)S(1)}, bf16[256,640]{1,0:T(8,128)(2,1)S(1)}, u32[]{:S(2)}, u32[]{:S(2)}) collective-permute-start(bf16[256,640]{1,0:T(8,128)(2,1)S(1)} %get-tuple-element.48.after.first_ref), channel_id=1, source_target_pairs={{8,0},{16,8},{24,16},{32,24},{40,32},{48,40},{56,48},{64,56},{72,6... | collective-permute-start | bytes 983048 | tf_op jit(solution)/shard_map/ppermute | solution.py:88
  33.2 1.7 %shard_map.119 = (f32[5,512,256]{2,1,0:T(8,128)S(1)}, bf16[5,512,256]{2,1,0:T(8,128)(2,1)S(1)}) custom-call(s32[5]{0:T(128)S(1)} %stack.27.pos, bf16[256,640]{1,0:T(8,128)(2,1)S(1)} %get-tuple-element.49.q_ref, bf16[512,640]{1,0:T(8,128)(2,1)S(1)} %get-tuple-element.53.k_ref, bf16[256,640]{1,0:T(8,128)(2,1)S(1)} %get-tuple-element.48.after.first_ref), custom_call_target="tpu_custom_call" | custom-call | flops 1 | bytes 1 | tf_op jit(solution)/shard_map/pallas_call | solution.py:119
  34.9 6.8 %collective-permute-done.4.came_ref = bf16[256,640]{1,0:T(8,128)(2,1)S(1)} collective-permute-done((bf16[256,640]{1,0:T(8,128)(2,1)S(1)}, bf16[256,640]{1,0:T(8,128)(2,1)S(1)}, u32[]{:S(2)}, u32[]{:S(2)}) %collective-permute-start.4) | collective-permute-done | bytes 327712 | tf_op jit(solution)/shard_map/ppermute | solution.py:88
  41.7 3.0 %shard_map.120 = (bf16[256,640]{1,0:T(8,128)(2,1)S(1)}, bf16[5,512,256]{2,1,0:T(8,128)(2,1)S(1)}, bf16[512,1280]{1,0:T(8,128)(2,1)S(1)}) custom-call(s32[5]{0:T(128)S(1)} %stack.27.pos, bf16[256,640]{1,0:T(8,128)(2,1)S(1)} %get-tuple-element.49.q_ref, bf16[512,640]{1,0:T(8,128)(2,1)S(1)} %get-tuple-element.50.v_ref, ...), custom_call_target="tpu_custom_call" | custom-call | flops 1 | bytes 1 | tf_op jit(solution)/shard_map/pallas_call | solution.py:119
  44.7 2.8 %shard_map.121.rest_0_ = bf16[4,640,256]{2,1,0:T(8,128)(2,1)S(1)} custom-call(s32[5]{0:T(128)S(1)} %stack.27.pos, bf16[512,1280]{1,0:T(8,128)(2,1)S(1)} %get-tuple-element.58.low_ref, bf16[2560,640]{1,0:T(8,128)(2,1)S(1)} %get-tuple-element.59.kw_ref, bf16[2560,640]{1,0:T(8,128)(2,1)S(1)} %get-tuple-element.60.vw_ref), custom_call_target="tpu_custom_call" | custom-call | flops 1 | bytes 1 | tf_op jit(solution)/shard_map/pallas_call | solution.py:119
  47.5 0.1 collective-permute-start.5
  47.6 2.8 %shard_map.122.keep_ref = bf16[4,640,256]{2,1,0:T(8,128)(2,1)S(1)} custom-call(s32[5]{0:T(128)S(1)} %stack.27.pos, bf16[512,1280]{1,0:T(8,128)(2,1)S(1)} %get-tuple-element.58.low_ref, bf16[2560,640]{1,0:T(8,128)(2,1)S(1)} %get-tuple-element.59.kw_ref, bf16[2560,640]{1,0:T(8,128)(2,1)S(1)} %get-tuple-element.60.vw_ref, ...), custom_call_target="tpu_custom_call" | custom-call | flops 1 | bytes 1 | tf_op jit(solution)/shard_map/pallas_call | solution.py:119
  50.4 0.2 collective-permute-done.5.came_ref
  50.6 0.8 shard_map.123
  51.4 0.8 collective-permute-start.9
  52.2 7.2 %collective-permute-start.11 = (bf16[640,256]{1,0:T(8,128)(2,1)S(1)}, bf16[640,256]{1,0:T(8,128)(2,1)S(1)}, u32[]{:S(2)}, u32[]{:S(2)}) collective-permute-start(bf16[640,256]{1,0:T(8,128)(2,1)S(1)} %get-tuple-element.68), channel_id=1, source_target_pairs={{0,192},{8,200},{16,208},{24,216},{32,224},{40,232},{48,240},{56,2... | collective-permute-start | bytes 983048 | tf_op jit(solution)/shard_map/ppermute | solution.py:54
  59.4 1.1 collective-permute-start.10
  60.5 2.4 %shard_map.124 = (f32[256,640]{1,0:T(8,128)S(1)}, bf16[256,640]{1,0:T(8,128)(2,1)S(1)}, bf16[256,640]{1,0:T(8,128)(2,1)S(1)}, bf16[256,640]{1,0:T(8,128)(2,1)S(1)}) custom-call(s32[5]{0:T(128)S(1)} %stack.27.pos, bf16[5,512,256]{2,1,0:T(8,128)(2,1)S(1)} %get-tuple-element.56.ds_ref, bf16[512,640]{1,0:T(8,128)(2,1)S(1)} %get-tuple-element.53.k_ref, ...), custom_call_target="tpu_custom_call" | custom-call | flops 1 | bytes 1 | tf_op jit(solution)/shard_map/pallas_call | solution.py:119
  62.9 2.5 %collective-permute-start.6 = (bf16[256,640]{1,0:T(8,128)(2,1)S(1)}, bf16[256,640]{1,0:T(8,128)(2,1)S(1)}, u32[]{:S(2)}, u32[]{:S(2)}) collective-permute-start(bf16[256,640]{1,0:T(8,128)(2,1)S(1)} %get-tuple-element.64), channel_id=1, source_target_pairs={{0,4},{2,6},{4,0},{6,2},{1,5},{3,7},{5,1},{7,3},{8,12},{10,14},{12... | collective-permute-start | bytes 983048 | tf_op jit(solution)/shard_map/ppermute | solution.py:47
  65.4 1.1 collective-permute-start.7
  66.5 0.8 collective-permute-done.9.b_ref
  67.3 11.2 %collective-permute-start.8 = (bf16[256,640]{1,0:T(8,128)(2,1)S(1)}, bf16[256,640]{1,0:T(8,128)(2,1)S(1)}, u32[]{:S(2)}, u32[]{:S(2)}) collective-permute-start(bf16[256,640]{1,0:T(8,128)(2,1)S(1)} %get-tuple-element.66), channel_id=1, source_target_pairs={{0,6},{2,4},{4,2},{6,0},{1,7},{3,5},{5,3},{7,1},{8,14},{10,12},{12... | collective-permute-start | bytes 983048 | tf_op jit(solution)/shard_map/ppermute | solution.py:47
  78.5 0.0 collective-permute-done.11.d_ref
  78.5 0.0 collective-permute-done.10.c_ref
  78.5 0.9 shard_map.126
  79.4 3.8 %collective-permute-start.12 = (bf16[64,640]{1,0:T(8,128)(2,1)S(1)}, bf16[64,640]{1,0:T(8,128)(2,1)S(1)}, u32[]{:S(2)}, u32[]{:S(2)}) collective-permute-start(bf16[64,640]{1,0:T(8,128)(2,1)S(1)} %get-tuple-element.69), channel_id=1, source_target_pairs={{0,0},{2,34},{4,4},{6,38},{8,8},{10,42},{12,12},{14,46},{16,16},{1... | collective-permute-start | bytes 245768 | tf_op jit(solution)/shard_map/ppermute | solution.py:64
  83.2 3.4 %collective-permute-start.13 = (bf16[64,640]{1,0:T(8,128)(2,1)S(1)}, bf16[64,640]{1,0:T(8,128)(2,1)S(1)}, u32[]{:S(2)}, u32[]{:S(2)}) collective-permute-start(bf16[64,640]{1,0:T(8,128)(2,1)S(1)} %get-tuple-element.70), channel_id=1, source_target_pairs={{0,8},{2,42},{4,12},{6,46},{8,16},{10,50},{12,20},{14,54},{16,24},... | collective-permute-start | bytes 245768 | tf_op jit(solution)/shard_map/ppermute | solution.py:64
  86.6 0.0 collective-permute-done.6.b_ref
  86.6 2.4 %collective-permute-start.14 = (bf16[64,640]{1,0:T(8,128)(2,1)S(1)}, bf16[64,640]{1,0:T(8,128)(2,1)S(1)}, u32[]{:S(2)}, u32[]{:S(2)}) collective-permute-start(bf16[64,640]{1,0:T(8,128)(2,1)S(1)} %get-tuple-element.71), channel_id=1, source_target_pairs={{0,16},{2,50},{4,20},{6,54},{8,24},{10,58},{12,28},{14,62},{16,32}... | collective-permute-start | bytes 245768 | tf_op jit(solution)/shard_map/ppermute | solution.py:64
  89.0 0.0 collective-permute-done.7.c_ref
  89.0 0.0 collective-permute-start.15
  89.0 1.5 %collective-permute-start.20 = (bf16[2,80,640]{2,1,0:T(8,128)(2,1)S(1)}, bf16[2,80,640]{2,1,0:T(8,128)(2,1)S(1)}, u32[]{:S(2)}, u32[]{:S(2)}) collective-permute-start(bf16[2,80,640]{2,1,0:T(8,128)(2,1)S(1)} %get-tuple-element.77.own), channel_id=1, source_target_pairs={{0,8},{8,16},{16,24},{24,32},{32,40},{40,48},{48,56},{56,0},{64,72... | collective-permute-start | bytes 614408 | tf_op jit(solution)/shard_map/ppermute | solution.py:84
  90.4 0.0 collective-permute-done.12.a_ref
  90.5 1.3 %collective-permute-start.19 = (bf16[2,80,640]{2,1,0:T(8,128)(2,1)S(1)}, bf16[2,80,640]{2,1,0:T(8,128)(2,1)S(1)}, u32[]{:S(2)}, u32[]{:S(2)}) collective-permute-start(bf16[2,80,640]{2,1,0:T(8,128)(2,1)S(1)} %get-tuple-element.77.own), channel_id=1, source_target_pairs={{0,56},{8,0},{16,8},{24,16},{32,24},{40,32},{48,40},{56,48},{64,12... | collective-permute-start | bytes 614408 | tf_op jit(solution)/shard_map/ppermute | solution.py:84
  91.7 1.0 collective-permute-start.18
  92.7 1.6 %shard_map.125.after = bf16[2,256,640]{2,1,0:T(8,128)(2,1)} custom-call(s32[5]{0:T(128)S(1)} %stack.27.pos, bf16[256,640]{1,0:T(8,128)(2,1)S(1)} %get-tuple-element.48.after.first_ref, f32[256,640]{1,0:T(8,128)S(1)} %get-tuple-element.63.a_ref, bf16[256,640]{1,0:T(8,128)(2,1)S(1)} %collective-permute-done.6.b_ref, ...), custom_call_target="tpu_custom_call" | custom-call | flops 1 | bytes 1 | tf_op jit(solution)/shard_map/pallas_call | solution.py:119
  94.3 0.0 copy-start
  94.3 1.2 %collective-permute-done.14.c_ref = bf16[64,640]{1,0:T(8,128)(2,1)S(1)} collective-permute-done((bf16[64,640]{1,0:T(8,128)(2,1)S(1)}, bf16[64,640]{1,0:T(8,128)(2,1)S(1)}, u32[]{:S(2)}, u32[]{:S(2)}) %collective-permute-start.14) | collective-permute-done | bytes 81952 | tf_op jit(solution)/shard_map/ppermute | solution.py:64
  95.5 0.1 collective-permute-done.15.d_ref
  95.6 0.6 shard_map.127
  96.1 0.1 collective-permute-start.16
  96.2 1.3 %collective-permute-done.16.came_ref = bf16[64,640]{1,0:T(8,128)(2,1)S(1)} collective-permute-done((bf16[64,640]{1,0:T(8,128)(2,1)S(1)}, bf16[64,640]{1,0:T(8,128)(2,1)S(1)}, u32[]{:S(2)}, u32[]{:S(2)}) %collective-permute-start.16) | collective-permute-done | bytes 81952 | tf_op jit(solution)/shard_map/ppermute | solution.py:47
  97.5 0.6 shard_map.128
  98.1 0.1 collective-permute-start.17
  98.2 0.9 collective-permute-done.19.up
  99.0 8.7 %collective-permute-done.18.two = bf16[2,80,640]{2,1,0:T(8,128)(2,1)S(1)} collective-permute-done((bf16[2,80,640]{2,1,0:T(8,128)(2,1)S(1)}, bf16[2,80,640]{2,1,0:T(8,128)(2,1)S(1)}, u32[]{:S(2)}, u32[]{:S(2)}) %collective-permute-start.18) | collective-permute-done | bytes 204832 | tf_op jit(solution)/shard_map/ppermute | solution.py:79
  107.7 1.6 %shard_map.129 = (f32[16,640]{1,0:T(8,128)S(1)}, bf16[16,640]{1,0:T(8,128)(2,1)S(1)}, bf16[16,640]{1,0:T(8,128)(2,1)S(1)}, bf16[16,640]{1,0:T(8,128)(2,1)S(1)}) custom-call(s32[5]{0:T(128)S(1)} %stack.27.pos, f32[64,640]{1,0:T(8,128)S(1)} %get-tuple-element.75.keep_ref, bf16[64,640]{1,0:T(8,128)(2,1)S(1)} %collective-permute-done.17.far_ref, ...), custom_call_target="tpu_custom_call" | custom-call | flops 1 | bytes 1 | tf_op jit(solution)/shard_map/pallas_call | solution.py:119
  109.3 0.5 collective-permute-start.22
  109.8 2.2 %collective-permute-start.23 = (bf16[16,640]{1,0:T(8,128)(2,1)S(1)}, bf16[16,640]{1,0:T(8,128)(2,1)S(1)}, u32[]{:S(2)}, u32[]{:S(2)}) collective-permute-start(bf16[16,640]{1,0:T(8,128)(2,1)S(1)} %get-tuple-element.81), channel_id=1, source_target_pairs={{0,192},{8,200},{16,208},{24,216},{32,224},{40,232},{48,240},{56,2... | collective-permute-start | bytes 61448 | tf_op jit(solution)/shard_map/ppermute | solution.py:54
  112.0 1.2 %collective-permute-done.21 = bf16[16,640]{1,0:T(8,128)(2,1)S(1)} collective-permute-done((bf16[16,640]{1,0:T(8,128)(2,1)S(1)}, bf16[16,640]{1,0:T(8,128)(2,1)S(1)}, u32[]{:S(2)}, u32[]{:S(2)}) %collective-permute-start.21) | collective-permute-done | bytes 20512 | tf_op jit(solution)/shard_map/ppermute | solution.py:54
  113.2 0.4 collective-permute-done.22
  113.6 0.4 collective-permute-done.23
  114.0 0.7 fusion.3
  (7 shorter events, 0.0 us)
Async XLA Ops:
  7.9 5.1 %collective-permute-start = (bf16[2,256,640]{2,1,0:T(8,128)(2,1)S(1)}, bf16[2,256,640]{2,1,0:T(8,128)(2,1)S(1)}, u32[]{:S(2)}, u32[]{:S(2)}) collective-permute-start(bf16[2,256,640]{2,1,0:T(8,128)(2,1)S(1)} %shard_map.114.rest_0_), channel_id=1, source_target_pairs={{0,2},{2,0},{4,6},{6,4},{1,3},{3,1},{5,7},{7,5},{8,10},{10,8},{12,... | collective-permute-start | bytes 1966088 | tf_op jit(solution)/shard_map/ppermute | solution.py:47
  12.6 2.4 %copy-start.1 = (bf16[80,640]{1,0:T(8,128)(2,1)S(1)}, bf16[80,640]{1,0:T(8,128)(2,1)}, u32[]{:S(2)}) copy-start(bf16[80,640]{1,0:T(8,128)(2,1)} %param.18) | copy-start | bytes 307204
  13.7 17.4 %collective-permute-start.1 = (bf16[256,640]{1,0:T(8,128)(2,1)S(1)}, bf16[256,640]{1,0:T(8,128)(2,1)S(1)}, u32[]{:S(2)}, u32[]{:S(2)}) collective-permute-start(bf16[256,640]{1,0:T(8,128)(2,1)S(1)} %get-tuple-element.46.after), channel_id=1, source_target_pairs={{0,4},{2,6},{4,0},{6,2},{1,5},{3,7},{5,1},{7,3},{8,12},{10,14},{12... | collective-permute-start | bytes 983048 | tf_op jit(solution)/shard_map/ppermute | solution.py:47
  15.0 16.1 %collective-permute-start.3 = (bf16[80,640]{1,0:T(8,128)(2,1)S(1)}, bf16[80,640]{1,0:T(8,128)(2,1)S(1)}, u32[]{:S(2)}, u32[]{:S(2)}) collective-permute-start(bf16[80,640]{1,0:T(8,128)(2,1)S(1)} %copy-done.1), channel_id=1, source_target_pairs={{0,32},{2,96},{4,160},{6,224},{8,40},{10,104},{12,168},{14,232},{1... | collective-permute-start | bytes 307208 | tf_op jit(solution)/shard_map/ppermute | solution.py:74
  23.3 7.7 %collective-permute-start.2 = (bf16[80,640]{1,0:T(8,128)(2,1)S(1)}, bf16[80,640]{1,0:T(8,128)(2,1)S(1)}, u32[]{:S(2)}, u32[]{:S(2)}) collective-permute-start(bf16[80,640]{1,0:T(8,128)(2,1)S(1)} %copy-done.1), channel_id=1, source_target_pairs={{0,0},{2,64},{4,128},{6,192},{8,8},{10,72},{12,136},{14,200},{16,1... | collective-permute-start | bytes 307208 | tf_op jit(solution)/shard_map/ppermute | solution.py:74
  31.7 10.0 %collective-permute-start.4 = (bf16[256,640]{1,0:T(8,128)(2,1)S(1)}, bf16[256,640]{1,0:T(8,128)(2,1)S(1)}, u32[]{:S(2)}, u32[]{:S(2)}) collective-permute-start(bf16[256,640]{1,0:T(8,128)(2,1)S(1)} %get-tuple-element.48.after.first_ref), channel_id=1, source_target_pairs={{8,0},{16,8},{24,16},{32,24},{40,32},{48,40},{56,48},{64,56},{72,6... | collective-permute-start | bytes 983048 | tf_op jit(solution)/shard_map/ppermute | solution.py:88
  47.5 3.1 %collective-permute-start.5 = (bf16[4,640,256]{2,1,0:T(8,128)(2,1)S(1)}, bf16[4,640,256]{2,1,0:T(8,128)(2,1)S(1)}, u32[]{:S(2)}, u32[]{:S(2)}) collective-permute-start(bf16[4,640,256]{2,1,0:T(8,128)(2,1)S(1)} %shard_map.121.rest_0_), channel_id=1, source_target_pairs={{0,2},{2,0},{4,6},{6,4},{1,3},{3,1},{5,7},{7,5},{8,10},{10,8},{12,... | collective-permute-start | bytes 3932168 | tf_op jit(solution)/shard_map/ppermute | solution.py:47
  51.4 15.8 %collective-permute-start.9 = (bf16[640,256]{1,0:T(8,128)(2,1)S(1)}, bf16[640,256]{1,0:T(8,128)(2,1)S(1)}, u32[]{:S(2)}, u32[]{:S(2)}) collective-permute-start(bf16[640,256]{1,0:T(8,128)(2,1)S(1)} %get-tuple-element.67), channel_id=1, source_target_pairs={{0,64},{8,72},{16,80},{24,88},{32,96},{40,104},{48,112},{56,120},{... | collective-permute-start | bytes 983048 | tf_op jit(solution)/shard_map/ppermute | solution.py:54
  52.2 26.3 %collective-permute-start.11 = (bf16[640,256]{1,0:T(8,128)(2,1)S(1)}, bf16[640,256]{1,0:T(8,128)(2,1)S(1)}, u32[]{:S(2)}, u32[]{:S(2)}) collective-permute-start(bf16[640,256]{1,0:T(8,128)(2,1)S(1)} %get-tuple-element.68), channel_id=1, source_target_pairs={{0,192},{8,200},{16,208},{24,216},{32,224},{40,232},{48,240},{56,2... | collective-permute-start | bytes 983048 | tf_op jit(solution)/shard_map/ppermute | solution.py:54
  59.4 19.1 %collective-permute-start.10 = (bf16[640,256]{1,0:T(8,128)(2,1)S(1)}, bf16[640,256]{1,0:T(8,128)(2,1)S(1)}, u32[]{:S(2)}, u32[]{:S(2)}) collective-permute-start(bf16[640,256]{1,0:T(8,128)(2,1)S(1)} %get-tuple-element.62.after), channel_id=1, source_target_pairs={{0,128},{8,136},{16,144},{24,152},{32,160},{40,168},{48,176},{56,1... | collective-permute-start | bytes 983048 | tf_op jit(solution)/shard_map/ppermute | solution.py:54
  62.9 23.7 %collective-permute-start.6 = (bf16[256,640]{1,0:T(8,128)(2,1)S(1)}, bf16[256,640]{1,0:T(8,128)(2,1)S(1)}, u32[]{:S(2)}, u32[]{:S(2)}) collective-permute-start(bf16[256,640]{1,0:T(8,128)(2,1)S(1)} %get-tuple-element.64), channel_id=1, source_target_pairs={{0,4},{2,6},{4,0},{6,2},{1,5},{3,7},{5,1},{7,3},{8,12},{10,14},{12... | collective-permute-start | bytes 983048 | tf_op jit(solution)/shard_map/ppermute | solution.py:47
  65.4 23.6 %collective-permute-start.7 = (bf16[256,640]{1,0:T(8,128)(2,1)S(1)}, bf16[256,640]{1,0:T(8,128)(2,1)S(1)}, u32[]{:S(2)}, u32[]{:S(2)}) collective-permute-start(bf16[256,640]{1,0:T(8,128)(2,1)S(1)} %get-tuple-element.65), channel_id=1, source_target_pairs={{0,2},{2,0},{4,6},{6,4},{1,3},{3,1},{5,7},{7,5},{8,10},{10,8},{12,... | collective-permute-start | bytes 983048 | tf_op jit(solution)/shard_map/ppermute | solution.py:47
  67.3 21.7 %collective-permute-start.8 = (bf16[256,640]{1,0:T(8,128)(2,1)S(1)}, bf16[256,640]{1,0:T(8,128)(2,1)S(1)}, u32[]{:S(2)}, u32[]{:S(2)}) collective-permute-start(bf16[256,640]{1,0:T(8,128)(2,1)S(1)} %get-tuple-element.66), channel_id=1, source_target_pairs={{0,6},{2,4},{4,2},{6,0},{1,7},{3,5},{5,3},{7,1},{8,14},{10,12},{12... | collective-permute-start | bytes 983048 | tf_op jit(solution)/shard_map/ppermute | solution.py:47
  79.4 11.0 %collective-permute-start.12 = (bf16[64,640]{1,0:T(8,128)(2,1)S(1)}, bf16[64,640]{1,0:T(8,128)(2,1)S(1)}, u32[]{:S(2)}, u32[]{:S(2)}) collective-permute-start(bf16[64,640]{1,0:T(8,128)(2,1)S(1)} %get-tuple-element.69), channel_id=1, source_target_pairs={{0,0},{2,34},{4,4},{6,38},{8,8},{10,42},{12,12},{14,46},{16,16},{1... | collective-permute-start | bytes 245768 | tf_op jit(solution)/shard_map/ppermute | solution.py:64
  83.2 8.5 %collective-permute-start.13 = (bf16[64,640]{1,0:T(8,128)(2,1)S(1)}, bf16[64,640]{1,0:T(8,128)(2,1)S(1)}, u32[]{:S(2)}, u32[]{:S(2)}) collective-permute-start(bf16[64,640]{1,0:T(8,128)(2,1)S(1)} %get-tuple-element.70), channel_id=1, source_target_pairs={{0,8},{2,42},{4,12},{6,46},{8,16},{10,50},{12,20},{14,54},{16,24},... | collective-permute-start | bytes 245768 | tf_op jit(solution)/shard_map/ppermute | solution.py:64
  86.6 8.9 %collective-permute-start.14 = (bf16[64,640]{1,0:T(8,128)(2,1)S(1)}, bf16[64,640]{1,0:T(8,128)(2,1)S(1)}, u32[]{:S(2)}, u32[]{:S(2)}) collective-permute-start(bf16[64,640]{1,0:T(8,128)(2,1)S(1)} %get-tuple-element.71), channel_id=1, source_target_pairs={{0,16},{2,50},{4,20},{6,54},{8,24},{10,58},{12,28},{14,62},{16,32}... | collective-permute-start | bytes 245768 | tf_op jit(solution)/shard_map/ppermute | solution.py:64
  89.0 6.6 %collective-permute-start.15 = (bf16[64,640]{1,0:T(8,128)(2,1)S(1)}, bf16[64,640]{1,0:T(8,128)(2,1)S(1)}, u32[]{:S(2)}, u32[]{:S(2)}) collective-permute-start(bf16[64,640]{1,0:T(8,128)(2,1)S(1)} %get-tuple-element.72), channel_id=1, source_target_pairs={{0,24},{2,58},{4,28},{6,62},{8,32},{10,2},{12,36},{14,6},{16,40},{... | collective-permute-start | bytes 245768 | tf_op jit(solution)/shard_map/ppermute | solution.py:64
  89.0 9.2 %collective-permute-start.20 = (bf16[2,80,640]{2,1,0:T(8,128)(2,1)S(1)}, bf16[2,80,640]{2,1,0:T(8,128)(2,1)S(1)}, u32[]{:S(2)}, u32[]{:S(2)}) collective-permute-start(bf16[2,80,640]{2,1,0:T(8,128)(2,1)S(1)} %get-tuple-element.77.own), channel_id=1, source_target_pairs={{0,8},{8,16},{16,24},{24,32},{32,40},{40,48},{48,56},{56,0},{64,72... | collective-permute-start | bytes 614408 | tf_op jit(solution)/shard_map/ppermute | solution.py:84
  90.5 8.6 %collective-permute-start.19 = (bf16[2,80,640]{2,1,0:T(8,128)(2,1)S(1)}, bf16[2,80,640]{2,1,0:T(8,128)(2,1)S(1)}, u32[]{:S(2)}, u32[]{:S(2)}) collective-permute-start(bf16[2,80,640]{2,1,0:T(8,128)(2,1)S(1)} %get-tuple-element.77.own), channel_id=1, source_target_pairs={{0,56},{8,0},{16,8},{24,16},{32,24},{40,32},{48,40},{56,48},{64,12... | collective-permute-start | bytes 614408 | tf_op jit(solution)/shard_map/ppermute | solution.py:84
  91.7 16.0 %collective-permute-start.18 = (bf16[2,80,640]{2,1,0:T(8,128)(2,1)S(1)}, bf16[2,80,640]{2,1,0:T(8,128)(2,1)S(1)}, u32[]{:S(2)}, u32[]{:S(2)}) collective-permute-start(bf16[2,80,640]{2,1,0:T(8,128)(2,1)S(1)} %get-tuple-element.77.own), channel_id=1, source_target_pairs={{0,16},{8,24},{16,0},{24,8},{32,48},{40,56},{48,32},{56,40},{64,80... | collective-permute-start | bytes 614408 | tf_op jit(solution)/shard_map/ppermute | solution.py:79
  94.3 19.7 %copy-start = (bf16[640,16]{0,1:T(8,128)(2,1)S(1)}, bf16[640,16]{0,1:T(8,128)(2,1)}, u32[]{:S(2)}) copy-start(bf16[640,16]{0,1:T(8,128)(2,1)} %param.19) | copy-start | bytes 61444
  96.1 1.4 %collective-permute-start.16 = (bf16[64,640]{1,0:T(8,128)(2,1)S(1)}, bf16[64,640]{1,0:T(8,128)(2,1)S(1)}, u32[]{:S(2)}, u32[]{:S(2)}) collective-permute-start(bf16[64,640]{1,0:T(8,128)(2,1)S(1)} %get-tuple-element.74), channel_id=1, source_target_pairs={{0,2},{2,0},{4,6},{6,4},{1,3},{3,1},{5,7},{7,5},{8,10},{10,8},{12,... | collective-permute-start | bytes 245768 | tf_op jit(solution)/shard_map/ppermute | solution.py:47
  98.1 9.7 %collective-permute-start.17 = (bf16[64,640]{1,0:T(8,128)(2,1)S(1)}, bf16[64,640]{1,0:T(8,128)(2,1)S(1)}, u32[]{:S(2)}, u32[]{:S(2)}) collective-permute-start(bf16[64,640]{1,0:T(8,128)(2,1)S(1)} %get-tuple-element.76), channel_id=1, source_target_pairs={{0,4},{2,6},{4,0},{6,2},{1,5},{3,7},{5,1},{7,3},{8,12},{10,14},{12... | collective-permute-start | bytes 245768 | tf_op jit(solution)/shard_map/ppermute | solution.py:47
  109.3 3.9 %collective-permute-start.21 = (bf16[16,640]{1,0:T(8,128)(2,1)S(1)}, bf16[16,640]{1,0:T(8,128)(2,1)S(1)}, u32[]{:S(2)}, u32[]{:S(2)}) collective-permute-start(bf16[16,640]{1,0:T(8,128)(2,1)S(1)} %get-tuple-element.79), channel_id=1, source_target_pairs={{0,64},{8,72},{16,80},{24,88},{32,96},{40,104},{48,112},{56,120},{... | collective-permute-start | bytes 61448 | tf_op jit(solution)/shard_map/ppermute | solution.py:54
  109.3 4.2 %collective-permute-start.22 = (bf16[16,640]{1,0:T(8,128)(2,1)S(1)}, bf16[16,640]{1,0:T(8,128)(2,1)S(1)}, u32[]{:S(2)}, u32[]{:S(2)}) collective-permute-start(bf16[16,640]{1,0:T(8,128)(2,1)S(1)} %get-tuple-element.80), channel_id=1, source_target_pairs={{0,128},{8,136},{16,144},{24,152},{32,160},{40,168},{48,176},{56,1... | collective-permute-start | bytes 61448 | tf_op jit(solution)/shard_map/ppermute | solution.py:54
  109.8 4.2 %collective-permute-start.23 = (bf16[16,640]{1,0:T(8,128)(2,1)S(1)}, bf16[16,640]{1,0:T(8,128)(2,1)S(1)}, u32[]{:S(2)}, u32[]{:S(2)}) collective-permute-start(bf16[16,640]{1,0:T(8,128)(2,1)S(1)} %get-tuple-element.81), channel_id=1, source_target_pairs={{0,192},{8,200},{16,208},{24,216},{32,224},{40,232},{48,240},{56,2... | collective-permute-start | bytes 61448 | tf_op jit(solution)/shard_map/ppermute | solution.py:54

commit v3 on v2

--- a/solution.py
+++ b/solution.py
@@ -12,6 +12,7 @@
 NX, NZ = 4, 8
 SECTIONS = NX * NZ
 TENSOR = 4
+LONG = 40_000_000_000
 VMEM_LIMIT = 20 * 1024 * 1024
 F32 = jnp.float32
 BF16 = jnp.bfloat16
@@ -64,9 +65,9 @@
     return lax.ppermute(value, ("section", "tensor"), pairs)
 
 
-def turn(value, bits):
+def turn(value):
     pairs = [
-        ((x * NZ + z) * TENSOR + t, (t * NZ + (z ^ bits)) * TENSOR + x)
+        ((x * NZ + z) * TENSOR + t, (t * NZ + z) * TENSOR + x)
         for x in range(NX)
         for z in range(NZ)
         for t in range(TENSOR)
@@ -110,7 +111,7 @@
 ANY = pl.BlockSpec(memory_space=pl.ANY)
 
 
-def call(body, ins, outs, scratch=(), place=VMEM):
+def call(body, ins, outs, scratch=(), place=VMEM, flops=1):
     arrays = [
         pltpu.with_memory_space_constraint(array, pltpu.HBM) if spec is HBM else array
         for array, spec in ins
@@ -123,7 +124,7 @@
         out_shape=shapes,
         scratch_shapes=list(scratch),
         compiler_params=pltpu.CompilerParams(vmem_limit_bytes=VMEM_LIMIT),
-        cost_estimate=pl.CostEstimate(flops=1, bytes_accessed=1, transcendentals=0),
+        cost_estimate=pl.CostEstimate(flops=flops, bytes_accessed=1, transcendentals=0),
     )(*arrays)
 
 
@@ -144,21 +145,18 @@
 ):
     width = k_ref.shape[-1]
     heads = heads_of(width)
-    pairs = []
-    for h in heads:
-        pairs.append((k_hbm.at[0, :, h], k_ref.at[:, h]))
-        pairs.append((q_hbm.at[0, 0, :, h], q_ref.at[:, h]))
-        pairs.append((v_hbm.at[0, :, h], v_ref.at[:, h]))
-        pairs.append((g_hbm.at[0, :, h], g_ref.at[:, h]))
+    refs = ((k_hbm.at[0], k_ref), (q_hbm.at[0, 0], q_ref), (v_hbm.at[0], v_ref), (g_hbm.at[0], g_ref))
+    parts = (slice(0, HEAD), slice(HEAD, width))
+    pairs = [(source.at[:, part], target.at[:, part]) for part in parts for source, target in refs]
     pairs.append((w_hbm.at[0], w_ref))
     started = copies(pairs, sems)
     for i, h in enumerate(heads):
-        for copy in started[4 * i : 4 * i + 4]:
+        for copy in started[4 * i : 4 * i + 4] if i < 2 else ():
             copy.wait()
         k = k_ref[:, h]
         shifted, factor = weights_of(q_ref[:, h], k)
         score_grad = score_gradient(shifted, factor, v_ref[:, h], g_ref[:, h])
-        dq_ref[:, h] = (dot(score_grad, k, TN) * HEAD ** (-0.5)).astype(BF16)
+        dq_ref[h, :] = (dot(k, score_grad, TN) * HEAD ** (-0.5)).astype(BF16)
     started[-1].wait()
 
 
@@ -167,19 +165,18 @@
     width = w_ref.shape[-1]
     for j in range(2):
         weight = rows_of(w_ref, block_for(pos, j, other), width)
-        out_ref[j] = dot(dq_ref[...], weight, NT).astype(BF16)
-
-
-def meet_core_kernel(pos, g_ref, keep_ref, came_ref, near_ref, far_ref):
-    near = keep_ref[0].astype(F32) + came_ref[0].astype(F32)
-    near_ref[...] = near + g_ref[...].astype(F32)
+        out_ref[j] = dot(weight, dq_ref[...], NN).astype(BF16)
+
+
+def meet_core_kernel(pos, keep_ref, came_ref, near_ref, far_ref):
+    near_ref[...] = keep_ref[0].astype(F32) + came_ref[0].astype(F32)
     far_ref[...] = (keep_ref[1].astype(F32) + came_ref[1].astype(F32)).astype(BF16)
 
 
-def meet_far_kernel(pos, near_ref, far_ref, text_a, text_b, after, out_ref, text_ref):
-    out_ref[...] = (near_ref[...] + far_ref[...].astype(F32)).astype(BF16)
-    text_ref[0] = text_a[...]
-    text_ref[1] = text_b[...]
+def meet_far_kernel(pos, g_ref, near_ref, far_ref, text, after, out_ref, text_ref):
+    text_ref[...] = text[...]
+    total = (near_ref[...] + far_ref[...].astype(F32)).T
+    out_ref[...] = (total + g_ref[...].astype(F32)).astype(BF16)
 
 
 def between_kernel(
@@ -198,8 +195,7 @@
     k_ref,
     v_ref,
     top_ref,
-    wk_ref,
-    wv_ref,
+    wkv_ref,
     q0_ref,
     g_ref,
     sems,
@@ -218,8 +214,9 @@
     first = len(pairs)
     pairs.append((q_hbm.at[0, 1], q_ref))
     pairs.append((top_hbm.at[0], top_ref))
-    pairs.append((wk_hbm.at[0], wk_ref))
-    pairs.append((wv_hbm.at[0], wv_ref))
+    width = k_ref.shape[-1]
+    pairs.append((wk_hbm.at[0], wkv_ref.at[:, :width]))
+    pairs.append((wv_hbm.at[0], wkv_ref.at[:, width:]))
     started = copies(pairs, sems)
     for copy in started[:first]:
         copy.wait()
@@ -243,8 +240,9 @@
 
 
 def second_kernel(
-    pos, q_ref, v_ref, came_ref, top_ref, dk_ref, dv_ref, p_ref, p_low_ref, g_ref, ds_ref, low_ref
+    pos, q_ref, v_ref, came_ref, top_ref, dk_ref, dv_ref, p_ref, p_low_ref, *rest
 ):
+    *waited, g_ref, ds_ref, low_ref = rest
     width = q_ref.shape[-1]
     g_ref[...] = jnp.where(pos[4] == 1, top_ref[...].astype(F32), came_ref[...].astype(F32)).astype(
         BF16
@@ -261,65 +259,59 @@
         low_ref[:, slice(width + h.start, width + h.stop)] = dv.astype(BF16)
 
 
-def context_block(pos, step, half, low_ref, kw_ref, vw_ref):
-    width = kw_ref.shape[-1]
+def context_block(pos, step, half, low_ref, w_ref):
+    width = w_ref.shape[-1] // 2
     count = low_ref.shape[0] // 2
     rows = slice(half * count, (half + 1) * count)
-    block = (pos[0] + step) % NX
-    total = dot(rows_of(kw_ref, block, width), low_ref[rows, :width], NT)
-    return total + dot(rows_of(vw_ref, block, width), low_ref[rows, width:], NT)
-
-
-def context_kernel(half, pos, low_ref, kw_ref, vw_ref, *rest):
+    return dot(rows_of(w_ref, (pos[0] + step) % NX, width), low_ref[rows, :], NT)
+
+
+def context_kernel(half, steps, pos, low_ref, w_ref, *rest):
     out_ref = rest[-1]
-    for step in range(NX):
-        total = context_block(pos, step, half, low_ref, kw_ref, vw_ref)
-        out_ref[step] = total.astype(BF16)
-
-
-def x_add_kernel(pos, keep_ref, came_ref, two_ref, late_two, *outs):
-    late_two[...] = two_ref[...]
-    for i, out in enumerate(outs):
-        out[...] = (keep_ref[i + 1].astype(F32) + came_ref[i + 1].astype(F32)).astype(BF16)
-
-
-def z_add_kernel(pos, keep_ref, came_ref, b_ref, c_ref, d_ref, *outs):
+    for i, step in enumerate(steps):
+        out_ref[i] = context_block(pos, step, half, low_ref, w_ref).astype(BF16)
+
+
+def across_kernel(pos, low_ref, w_ref, came_ref, after, top_ref, bottom_ref):
+    total = context_block(pos, 2, 1, low_ref, w_ref) + came_ref[0].astype(F32)
+    half = top_ref.shape[0]
+    top_ref[...] = total[:half].astype(BF16)
+    bottom_ref[...] = total[half:].astype(BF16)
+
+
+def x_add_kernel(
+    pos, keep_ref, came_ref, top_ref, bottom_ref, one_ref, after, late_one, next_ref, previous_ref
+):
+    late_one[...] = one_ref[...]
+    half = top_ref.shape[0]
+    next_ref[...] = (keep_ref[1].astype(F32) + came_ref[1].astype(F32)).astype(BF16)
+    total = keep_ref[1, :half].astype(F32) + came_ref[1, :half].astype(F32)
+    next_ref[:half] = (total + top_ref[...].astype(F32)).astype(BF16)
+    previous_ref[...] = (keep_ref[2].astype(F32) + came_ref[2].astype(F32)).astype(BF16)
+    total = keep_ref[2, half:].astype(F32) + came_ref[2, half:].astype(F32)
+    previous_ref[half:] = (total + bottom_ref[...].astype(F32)).astype(BF16)
+
+
+def z_add_kernel(pos, keep_ref, came_ref, b_ref, c_ref, text_a, text_b, two_ref, *outs):
+    two_ref[0] = text_a[...]
+    two_ref[1] = text_b[...]
     rows = outs[0].shape[0]
     width = outs[0].shape[1]
     for place in (slice(0, width // 2), slice(width // 2, width)):
         total = keep_ref[0, place, :].astype(F32) + came_ref[0, place, :].astype(F32)
-        total = total + b_ref[place, :].astype(F32)
-        total = total + c_ref[place, :].astype(F32) + d_ref[place, :].astype(F32)
+        total = total + b_ref[place, :].astype(F32) + c_ref[place, :].astype(F32)
         total = total.T.astype(BF16)
         for j, out in enumerate(outs):
             out[:, place] = total[j * rows : (j + 1) * rows]
 
 
-def third_kernel(
-    pos,
-    ds_ref,
-    k_ref,
-    w_ref,
-    g_ref,
-    after,
-    near_ref,
-    far_out,
-    core_out,
-    both_out,
-    dq_ref,
-):
-    width = w_ref.shape[-1]
-    for i, h in enumerate(heads_of(width)):
-        dq_ref[:, h] = (dot(ds_ref[i], k_ref[:, h], TN) * HEAD ** (-0.5)).astype(BF16)
-    for j, out in enumerate((near_ref, far_out, core_out, both_out)):
-        weight = rows_of(w_ref, block_for(pos, j, 0), width)
-        total = dot(dq_ref[...], weight, NT)
-        if j == 0:
-            total = total + g_ref[...].astype(F32)
-        out[...] = total.astype(out.dtype)
-
-
-def z_sum_kernel(pos, a_ref, b_ref, c_ref, d_ref, after, keep_ref, send_ref):
+def third_kernel(pos, ds_ref, k_ref, w_ref, after, dq_ref, out_ref):
+    for i, h in enumerate(heads_of(k_ref.shape[-1])):
+        dq_ref[h, :] = (dot(k_ref[:, h], ds_ref[i], TN) * HEAD ** (-0.5)).astype(BF16)
+    project_kernel(1, pos, dq_ref, w_ref, out_ref)
+
+
+def z_sum_kernel(pos, a_ref, b_ref, c_ref, d_ref, keep_ref, send_ref):
     total = a_ref[...].astype(F32) + b_ref[...].astype(F32)
     total = total + c_ref[...].astype(F32) + d_ref[...].astype(F32)
     keep_ref[...] = total
@@ -332,14 +324,17 @@
     send_ref[...] = total.astype(BF16)
 
 
-def text_kernel(pos, keep_ref, far_ref, own, two, up, down, *rest):
-    *outs, context_ref, w_ref = rest
+def gather_kernel(pos, own, up, down, two, w_ref):
     rows = own.shape[1]
     places = (pos[1], pos[1] ^ 2, (pos[1] + 1) % NZ, (pos[1] + NZ - 1) % NZ)
     for ref, z in zip((own, two, up, down), places):
         for r in range(2):
             row = pl.multiple_of((z ^ (4 * r)) * rows, rows)
             w_ref[pl.ds(row, rows), :] = ref[r]
+
+
+def text_kernel(pos, keep_ref, far_ref, w_ref, after, *rest):
+    *outs, context_ref = rest
     context_ref[...] = (keep_ref[...] + far_ref[...].astype(F32)).astype(BF16)
     tokens = outs[0].shape[0]
     for i, out in enumerate(outs):
@@ -348,11 +343,10 @@
         out[...] = total.astype(out.dtype)
 
 
-def sent_kernel(pos, first_ref, a_ref, b_ref, c_ref, d_ref, out_hbm, out_ref, sems):
+def sent_kernel(pos, first_ref, g_ref, near_ref, far_ref, out_hbm, out_ref, sems):
     out_ref[0] = first_ref[...]
-    total = a_ref[...] + b_ref[...].astype(F32)
-    total = total + c_ref[...].astype(F32) + d_ref[...].astype(F32)
-    out_ref[1] = total.astype(BF16)
+    total = (near_ref[...] + far_ref[...].astype(F32)).T
+    out_ref[1] = (total + g_ref[...].astype(F32)).astype(BF16)
     copies([(out_ref, out_hbm)], sems)[0].wait()
 
 
@@ -385,7 +379,8 @@
     where = (pos, pl.BlockSpec(memory_space=pltpu.SMEM))
 
     act = ((rows, width), BF16)
-    pair = ((2, rows, width), BF16)
+    turned = ((width, rows), BF16)
+    pair = ((2, width, rows), BF16)
     square = ((text, width), F32)
     narrow = ((text, width), BF16)
     matrix = ((model, width), BF16)
@@ -397,32 +392,31 @@
         return pltpu.SemaphoreType.DMA((count,))
 
     block = text_weight.shape
-    text_a, text_b = turn(text_weight, 0), turn(text_weight, 4)
 
     dq0, wq, g_first = call(
         first_kernel,
         [where, (queries, HBM), (keys, HBM), (values, HBM), (grad_in, HBM), (query_weight, HBM)],
-        [act, matrix, act],
-        [vm(*act), vm(*narrow), vm(*narrow), dma(4 * heads + 1)],
-    )
-    def project(other, *after):
+        [turned, matrix, act],
+        [vm(*act), vm(*narrow), vm(*narrow), dma(9)],
+    )
+    def project(other, dq, *after):
         return call(
             functools.partial(project_kernel, other),
-            [where, (dq0, VMEM), (wq, VMEM)] + [(a, ANY) for a in after],
+            [where, (dq, VMEM), (wq, VMEM)] + [(a, ANY) for a in after],
             [pair],
         )[0]
 
-    send0 = project(1)
+    send0 = project(1, dq0)
     came0 = swap_tensor(send0, 1)
-    keep0 = project(0, send0)
+    keep0 = project(0, dq0, send0)
     near0, far0 = call(
         meet_core_kernel,
-        [where] + [(a, VMEM) for a in (g_first, keep0, came0)],
-        [((rows, width), F32), act],
+        [where] + [(a, VMEM) for a in (keep0, came0)],
+        [((width, rows), F32), turned],
     )
     far0_back = swap_tensor(far0, 2)
 
-    dk0, dv0, q1, k, v, top, wk, wv = call(
+    dk0, dv0, q1, k, v, top, wkv = call(
         between_kernel,
         [
             where,
@@ -435,15 +429,16 @@
             (value_weight, HBM),
             (far0, ANY),
         ],
-        [square, square, act, narrow, narrow, act, matrix, matrix],
+        [square, square, act, narrow, narrow, act, ((model, 2 * width), BF16)],
         [vm(*act), vm(*act), dma(2 * SECTIONS + 6)],
     )
 
-    sent0, text_two = call(
+    sent0, text_one = call(
         meet_far_kernel,
-        [where] + [(a, VMEM) for a in (near0, far0_back, text_a, text_b)]
+        [where]
+        + [(a, VMEM) for a in (g_first, near0, far0_back, turn(text_weight))]
         + [(dk0, ANY)],
-        [act, ((2,) + block, BF16)],
+        [act, (block, BF16)],
     )
     came_back = pass_back(sent0)
     p1, p1_low = call(
@@ -458,54 +453,70 @@
         [act, ((heads, text, rows), BF16), ((text, 2 * width), BF16)],
     )
 
-    terms = ((NX, width, text // 2), BF16)
-    (send,) = call(
-        functools.partial(context_kernel, 0), [where, (low, VMEM), (wk, VMEM), (wv, VMEM)], [terms]
-    )
+    def context_terms(half, steps, *after, flops=1):
+        return call(
+            functools.partial(context_kernel, half, steps),
+            [where, (low, VMEM), (wkv, VMEM)] + [(a, ANY) for a in after],
+            [((len(steps), width, text // 2), BF16)],
+            flops=flops,
+        )[0]
+
+    near_steps = (0, 1, 3)
+    send_across = context_terms(0, (2,))
+    came_across = swap_tensor(send_across, 1)
+    send = context_terms(0, near_steps, send_across)
     came = swap_tensor(send, 1)
-    (keep,) = call(
-        functools.partial(context_kernel, 1),
-        [where, (low, VMEM), (wk, VMEM), (wv, VMEM), (send, ANY)],
-        [terms],
-    )
-    text_two, *by_x = call(
+    top, bottom = call(
+        across_kernel,
+        [where]
+        + [(a, VMEM) for a in (low, wkv, came_across)]
+        + [(send, ANY)],
+        [((width // 2, text // 2), BF16)] * 2,
+    )
+    across = [send_x(top, 1), send_x(bottom, -1)]
+    keep = context_terms(1, near_steps, top, flops=LONG)
+    dq1, send1 = call(
+        third_kernel,
+        [where, (ds1, VMEM), (k, VMEM), (wq, VMEM), (keep, ANY)],
+        [turned, pair],
+    )
+    came1 = swap_tensor(send1, 1)
+    text_one, to_next, to_previous = call(
         x_add_kernel,
-        [where, (keep, VMEM), (came, VMEM), (text_two, VMEM)],
-        [((2,) + block, BF16)] + [((width, text // 2), BF16)] * (NX - 1),
-    )
-    came_x = [send_x(piece, i + 1) for i, piece in enumerate(by_x)]
-    text_more = [swap_z(text_two, 2), from_z(text_two, 1), from_z(text_two, -1)]
-
-    near1, far1, core1, both1 = call(
-        third_kernel,
-        [where, (ds1, VMEM), (k, VMEM), (wq, VMEM), (g1, VMEM), (by_x[1], ANY)],
-        [((rows, width), F32)] + [act] * 3,
-        [vm(*act)],
-    )
-    others = (
-        near1,
-        swap_tensor(far1, 2),
-        swap_tensor(core1, 1),
-        swap_tensor(both1, 3),
-    )
+        [where] + [(a, VMEM) for a in (keep, came, *across, text_one)]
+        + [(send1, ANY)],
+        [(block, BF16)] + [((width, text // 2), BF16)] * 2,
+        flops=LONG,
+    )
+    came_x = [send_x(to_next, 1), send_x(to_previous, -1)]
+    text_across = swap_z(text_one, 4)
+
+    keep1 = project(0, dq1, to_next)
+    near1, far1 = call(
+        meet_core_kernel,
+        [where, (keep1, VMEM), (came1, VMEM)],
+        [((width, rows), F32), turned],
+    )
+    others = (near1, swap_tensor(far1, 2))
     (sent,) = call(
         sent_kernel,
-        [where, (sent0, VMEM)] + [(a, VMEM) for a in others],
-        [pair],
-        [vm(*pair), dma(1)],
+        [where, (sent0, VMEM), (g1, VMEM)] + [(a, VMEM) for a in others],
+        [((2, rows, width), BF16)],
+        [vm((2, rows, width), BF16), dma(1)],
         ANY,
     )
 
     few = text // NZ
-    by_z = call(
+    text_two, *by_z = call(
         z_add_kernel,
-        [where] + [(a, VMEM) for a in (keep, came, *came_x)],
-        [((few, width), BF16)] * (NZ // 2),
-    )
+        [where] + [(a, VMEM) for a in (keep, came, *came_x, text_one, text_across)],
+        [((2,) + block, BF16)] + [((few, width), BF16)] * (NZ // 2),
+    )
+    text_more = [from_z(text_two, 1), from_z(text_two, -1), swap_z(text_two, 2)]
     came_z = [send_z(by_z[i], i) for i in range(NZ // 2)]
     context, context_low = call(
         z_sum_kernel,
-        [where] + [(a, VMEM) for a in came_z] + [(sent, HBM)],
+        [where] + [(a, VMEM) for a in came_z],
         [((few, width), F32), ((few, width), BF16)],
     )
     context, context_low = call(
@@ -515,11 +526,16 @@
     )
     far_context = swap_tensor(context_low, 2)
     tokens = few // NX
+    (gathered,) = call(
+        gather_kernel,
+        [where] + [(a, VMEM) for a in (text_two, *text_more)],
+        [((width, width), BF16)],
+    )
     hidden, *to_send = call(
         text_kernel,
-        [where] + [(a, VMEM) for a in (context, far_context, text_two, *text_more)],
+        [where] + [(a, VMEM) for a in (context, far_context, gathered)] + [(sent, HBM)],
         [((tokens, width), F32)] + [((tokens, width), BF16)] * (NX - 1),
-        [vm((few, width), BF16), vm((width, width), BF16)],
+        [vm((few, width), BF16)],
     )
     for i, piece in enumerate(to_send):
         hidden = hidden + send_x(piece, i + 1).astype(F32)

time: 115 us -> 105 us (0.913)
  starting transfers between devices: 56.5 us -> 42.8 us
  waiting for transfers between devices: 22.2 us -> 24.1 us
    ppermute x8, starting transfers between devices: 19.7 us -> 9.72 us  [swap_tensor(): return lax.ppermute(value, 'tensor', [(i, i ^ bit) for i in range(TENSOR)])]
    ppermute x1 -> x2, waiting for transfers between devices: 8.7 us -> 1.33 us  [swap_z(): return lax.ppermute(value, 'section', pairs)]
    ppermute x2 -> x1, starting transfers between devices: 10.3 us -> 3.64 us  [turn(): return lax.ppermute(value, ('section', 'tensor'), pairs)]
    ppermute x4, waiting for transfers between devices: 1.26 us -> 6.42 us  [send_z(): return lax.ppermute(value, ('section', 'tensor'), pairs)]
    ppermute x1 -> x2, starting transfers between devices: 0.98 us -> 4.19 us  [swap_z(): return lax.ppermute(value, 'section', pairs)]
    ppermute x6 -> x7, waiting for transfers between devices: 2.73 us -> 5.31 us  [send_x(): return lax.ppermute(value, 'section', pairs)]
    ppermute x6 -> x7, starting transfers between devices: 11.8 us -> 9.27 us  [send_x(): return lax.ppermute(value, 'section', pairs)]
    ppermute x4, starting transfers between devices: 9.52 us -> 10.9 us  [send_z(): return lax.ppermute(value, ('section', 'tensor'), pairs)]
  transfers between devices with their start and end apart: 24 -> 25, of which waited for: 12 -> 13; matrix products, arithmetic and copies ran while one was open for 0% -> 0% of each run, Pallas kernels for 15% -> 22%
where the time goes in v3:
time: 105 us; the launch traced here: 104 us
  starting transfers between devices  42.8 us (41%)
  Pallas kernels  35 us (33%)
  waiting for transfers between devices  24.1 us (23%)
    pallas_call x22, Pallas kernels, call(): pl.pallas_call(body, in_specs=[spec for array, spec in ins], out_specs=[p...  35 us
    ppermute x4, starting transfers between devices, send_z(): return lax.ppermute(value, ('section', 'tensor'), pairs)  10.9 us
    ppermute x8, starting transfers between devices, swap_tensor(): return lax.ppermute(value, 'tensor', [(i, i ^ bit) for i in range(TENSOR)])  9.72 us
    ppermute x7, starting transfers between devices, send_x(): return lax.ppermute(value, 'section', pairs)  9.27 us
    ppermute x1, waiting for transfers between devices, pass_back(): lax.ppermute(value, 'section', [(s + 1, s) for s in range(SECTIONS - 1)])  7.47 us
    ppermute x4, waiting for transfers between devices, send_z(): return lax.ppermute(value, ('section', 'tensor'), pairs)  6.42 us
    ppermute x7, waiting for transfers between devices, send_x(): return lax.ppermute(value, 'section', pairs)  5.31 us
    ppermute x2, starting transfers between devices, swap_z(): return lax.ppermute(value, 'section', pairs)  4.19 us
  transfers between devices with their start and end apart: 25, of which 13 were waited for; matrix products, arithmetic and copies ran while one was open for 0% of the time, Pallas kernels for 22%

profile of v3, /device:TPU:1, one launch (start us, length us, event | category | flops | bytes accessed | tf_op | source)
XLA Modules:
  0.0 103.6 jit_solution(6266619950743796180)
XLA Ops:
  0.7 0.1 stack.27.pos
  0.8 4.3 %shard_map.113 = (bf16[640,256]{1,0:T(8,128)(2,1)S(1)}, bf16[2560,640]{1,0:T(8,128)(2,1)S(1)}, bf16[256,640]{1,0:T(8,128)(2,1)S(1)}) custom-call(s32[5]{0:T(128)S(1)} %stack.27.pos, bf16[1,2,256,640]{3,2,1,0:T(8,128)(2,1)} %q_hbm.3, bf16[1,512,640]{2,1,0:T(8,128)(2,1)} %k_hbm.3, bf16[1,512,640]{2,1,0:T(8,128)(2,1)} %v_hbm.3, bf16[1,256,640]{2,1,0:T(8,128)(2,1)} %g_hbm.3, ...), custom_call_target="tpu_custom_call" | custom-call | flops 1 | bytes 1 | tf_op jit(solution)/shard_map/pallas_call | solution.py:120
  5.1 1.2 %shard_map.114.rest_0_ = bf16[2,640,256]{2,1,0:T(8,128)(2,1)S(1)} custom-call(s32[5]{0:T(128)S(1)} %stack.27.pos, bf16[640,256]{1,0:T(8,128)(2,1)S(1)} %get-tuple-element.44.dq_ref, bf16[2560,640]{1,0:T(8,128)(2,1)S(1)} %get-tuple-element.45.w_ref), custom_call_target="tpu_custom_call" | custom-call | flops 1 | bytes 1 | tf_op jit(solution)/shard_map/pallas_call | solution.py:120
  6.3 0.0 copy-start.1
  6.3 3.3 %collective-permute-start = (bf16[2,640,256]{2,1,0:T(8,128)(2,1)S(1)}, bf16[2,640,256]{2,1,0:T(8,128)(2,1)S(1)}, u32[]{:S(2)}, u32[]{:S(2)}) collective-permute-start(bf16[2,640,256]{2,1,0:T(8,128)(2,1)S(1)} %shard_map.114.rest_0_), channel_id=1, source_target_pairs={{0,2},{2,0},{4,6},{6,4},{1,3},{3,1},{5,7},{7,5},{8,10},{10,8},{12,... | collective-permute-start | bytes 1966088 | tf_op jit(solution)/shard_map/ppermute | solution.py:48
  9.6 1.2 %shard_map.115.keep_ref = bf16[2,640,256]{2,1,0:T(8,128)(2,1)S(1)} custom-call(s32[5]{0:T(128)S(1)} %stack.27.pos, bf16[640,256]{1,0:T(8,128)(2,1)S(1)} %get-tuple-element.44.dq_ref, bf16[2560,640]{1,0:T(8,128)(2,1)S(1)} %get-tuple-element.45.w_ref, bf16[2,640,256]{2,1,0:T(8,128)(2,1)S(1)} %shard_map.114.rest_0_), custom_call_target="tpu_custom_call" | custom-call | flops 1 | bytes 1 | tf_op jit(solution)/shard_map/pallas_call | solution.py:120
  10.8 0.5 collective-permute-done.came_ref
  11.4 0.7 shard_map.116
  12.0 1.3 %collective-permute-start.1 = (bf16[640,256]{1,0:T(8,128)(2,1)S(1)}, bf16[640,256]{1,0:T(8,128)(2,1)S(1)}, u32[]{:S(2)}, u32[]{:S(2)}) collective-permute-start(bf16[640,256]{1,0:T(8,128)(2,1)S(1)} %get-tuple-element.47.after), channel_id=1, source_target_pairs={{0,4},{2,6},{4,0},{6,2},{1,5},{3,7},{5,1},{7,3},{8,12},{10,14},{12... | collective-permute-start | bytes 983048 | tf_op jit(solution)/shard_map/ppermute | solution.py:48
  13.3 3.6 %collective-permute-start.2 = (bf16[80,640]{1,0:T(8,128)(2,1)S(1)}, bf16[80,640]{1,0:T(8,128)(2,1)S(1)}, u32[]{:S(2)}, u32[]{:S(2)}) collective-permute-start(bf16[80,640]{1,0:T(8,128)(2,1)S(1)} %copy-done.1), channel_id=1, source_target_pairs={{0,0},{2,64},{4,128},{6,192},{8,8},{10,72},{12,136},{14,200},{16,1... | collective-permute-start | bytes 307208 | tf_op jit(solution)/shard_map/ppermute | solution.py:75
  17.0 5.8 %shard_map.117 = (f32[512,640]{1,0:T(8,128)S(1)}, f32[512,640]{1,0:T(8,128)S(1)}, bf16[256,640]{1,0:T(8,128)(2,1)S(1)}, bf16[512,640]{1,0:T(8,128)(2,1)S(1)}, bf...) custom-call(s32[5]{0:T(128)S(1)} %stack.27.pos, ...), custom_call_target="tpu_custom_call" | custom-call | flops 1 | bytes 1 | tf_op jit(solution)/shard_map/pallas_call | solution.py:120
  22.8 0.0 collective-permute-done.2.text
  22.8 0.8 shard_map.118
  23.6 1.3 %collective-permute-start.3 = (bf16[256,640]{1,0:T(8,128)(2,1)S(1)}, bf16[256,640]{1,0:T(8,128)(2,1)S(1)}, u32[]{:S(2)}, u32[]{:S(2)}) collective-permute-start(bf16[256,640]{1,0:T(8,128)(2,1)S(1)} %get-tuple-element.49.after.first_ref), channel_id=1, source_target_pairs={{8,0},{16,8},{24,16},{32,24},{40,32},{48,40},{56,48},{64,56},{72,6... | collective-permute-start | bytes 983048 | tf_op jit(solution)/shard_map/ppermute | solution.py:89
  24.9 1.7 %shard_map.119 = (f32[5,512,256]{2,1,0:T(8,128)S(1)}, bf16[5,512,256]{2,1,0:T(8,128)(2,1)S(1)}) custom-call(s32[5]{0:T(128)S(1)} %stack.27.pos, bf16[256,640]{1,0:T(8,128)(2,1)S(1)} %get-tuple-element.50.q_ref, bf16[512,640]{1,0:T(8,128)(2,1)S(1)} %get-tuple-element.54.k_ref, bf16[256,640]{1,0:T(8,128)(2,1)S(1)} %get-tuple-element.49.after.first_ref), custom_call_target="tpu_custom_call" | custom-call | flops 1 | bytes 1 | tf_op jit(solution)/shard_map/pallas_call | solution.py:120
  26.6 7.5 %collective-permute-done.3.came_ref = bf16[256,640]{1,0:T(8,128)(2,1)S(1)} collective-permute-done((bf16[256,640]{1,0:T(8,128)(2,1)S(1)}, bf16[256,640]{1,0:T(8,128)(2,1)S(1)}, u32[]{:S(2)}, u32[]{:S(2)}) %collective-permute-start.3) | collective-permute-done | bytes 327712 | tf_op jit(solution)/shard_map/ppermute | solution.py:89
  34.1 3.1 %shard_map.120 = (bf16[256,640]{1,0:T(8,128)(2,1)S(1)}, bf16[5,512,256]{2,1,0:T(8,128)(2,1)S(1)}, bf16[512,1280]{1,0:T(8,128)(2,1)S(1)}) custom-call(s32[5]{0:T(128)S(1)} %stack.27.pos, bf16[256,640]{1,0:T(8,128)(2,1)S(1)} %get-tuple-element.50.q_ref, bf16[512,640]{1,0:T(8,128)(2,1)S(1)} %get-tuple-element.51.v_ref, ...), custom_call_target="tpu_custom_call" | custom-call | flops 1 | bytes 1 | tf_op jit(solution)/shard_map/pallas_call | solution.py:120
  37.1 1.2 %shard_map.121.rest_0_ = bf16[1,640,256]{2,1,0:T(8,128)(2,1)S(1)} custom-call(s32[5]{0:T(128)S(1)} %stack.27.pos, bf16[512,1280]{1,0:T(8,128)(2,1)S(1)} %get-tuple-element.59.low_ref, bf16[2560,1280]{1,0:T(8,128)(2,1)S(1)} %get-tuple-element.60.w_ref), custom_call_target="tpu_custom_call" | custom-call | flops 1 | bytes 1 | tf_op jit(solution)/shard_map/pallas_call | solution.py:120
  38.3 2.0 %collective-permute-start.4 = (bf16[1,640,256]{2,1,0:T(8,128)(2,1)S(1)}, bf16[1,640,256]{2,1,0:T(8,128)(2,1)S(1)}, u32[]{:S(2)}, u32[]{:S(2)}) collective-permute-start(bf16[1,640,256]{2,1,0:T(8,128)(2,1)S(1)} %shard_map.121.rest_0_), channel_id=1, source_target_pairs={{0,2},{2,0},{4,6},{6,4},{1,3},{3,1},{5,7},{7,5},{8,10},{10,8},{12,... | collective-permute-start | bytes 983048 | tf_op jit(solution)/shard_map/ppermute | solution.py:48
  40.3 2.0 %shard_map.122.after = bf16[3,640,256]{2,1,0:T(8,128)(2,1)S(1)} custom-call(s32[5]{0:T(128)S(1)} %stack.27.pos, bf16[512,1280]{1,0:T(8,128)(2,1)S(1)} %get-tuple-element.59.low_ref, bf16[2560,1280]{1,0:T(8,128)(2,1)S(1)} %get-tuple-element.60.w_ref, bf16[1,640,256]{2,1,0:T(8,128)(2,1)S(1)} %shard_map.121.rest_0_), custom_call_target="tpu_custom_call" | custom-call | flops 1 | bytes 1 | tf_op jit(solution)/shard_map/pallas_call | solution.py:120
  42.3 0.1 collective-permute-start.5
  42.4 1.2 %shard_map.123 = (bf16[320,256]{1,0:T(8,128)(2,1)S(1)}, bf16[320,256]{1,0:T(8,128)(2,1)S(1)}) custom-call(s32[5]{0:T(128)S(1)} %stack.27.pos, bf16[512,1280]{1,0:T(8,128)(2,1)S(1)} %get-tuple-element.59.low_ref, bf16[2560,1280]{1,0:T(8,128)(2,1)S(1)} %get-tuple-element.60.w_ref, bf16[1,640,256]{2,1,0:T(8,128)(2,1)S(1)} %collective-permute-done.4.came_ref, ...), custom_call_target="tpu_custom_call" | custom-call | flops 1 | bytes 1 | tf_op jit(solution)/shard_map/pallas_call | solution.py:120
  43.6 5.0 %collective-permute-start.7 = (bf16[320,256]{1,0:T(8,128)(2,1)S(1)}, bf16[320,256]{1,0:T(8,128)(2,1)S(1)}, u32[]{:S(2)}, u32[]{:S(2)}) collective-permute-start(bf16[320,256]{1,0:T(8,128)(2,1)S(1)} %get-tuple-element.63), channel_id=1, source_target_pairs={{0,192},{8,200},{16,208},{24,216},{32,224},{40,232},{48,240},{56,2... | collective-permute-start | bytes 491528 | tf_op jit(solution)/shard_map/ppermute | solution.py:55
  48.6 2.0 %shard_map.124.after.keep_ref = bf16[3,640,256]{2,1,0:T(8,128)(2,1)S(1)} custom-call(s32[5]{0:T(128)S(1)} %stack.27.pos, bf16[512,1280]{1,0:T(8,128)(2,1)S(1)} %get-tuple-element.59.low_ref, bf16[2560,1280]{1,0:T(8,128)(2,1)S(1)} %get-tuple-element.60.w_ref, bf16[320,256]{1,0:T(8,128)(2,1)S(1)} %get-tuple-element.61.rest_0_), custom_call_target="tpu_custom_call" | custom-call | flops 40000000000 | bytes 1 | tf_op jit(solution)/shard_map/pallas_call | solution.py:120
  50.6 1.5 %shard_map.125 = (bf16[640,256]{1,0:T(8,128)(2,1)S(1)}, bf16[2,640,256]{2,1,0:T(8,128)(2,1)S(1)}) custom-call(s32[5]{0:T(128)S(1)} %stack.27.pos, bf16[5,512,256]{2,1,0:T(8,128)(2,1)S(1)} %get-tuple-element.58.ds_ref, bf16[512,640]{1,0:T(8,128)(2,1)S(1)} %get-tuple-element.54.k_ref, bf16[2560,640]{1,0:T(8,128)(2,1)S(1)} %get-tuple-element.45.w_ref, ...), custom_call_target="tpu_custom_call" | custom-call | flops 1 | bytes 1 | tf_op jit(solution)/shard_map/pallas_call | solution.py:120
  52.1 0.8 collective-permute-start.8
  52.9 1.8 %collective-permute-done.6.top_ref = bf16[320,256]{1,0:T(8,128)(2,1)S(1)} collective-permute-done((bf16[320,256]{1,0:T(8,128)(2,1)S(1)}, bf16[320,256]{1,0:T(8,128)(2,1)S(1)}, u32[]{:S(2)}, u32[]{:S(2)}) %collective-permute-start.6) | collective-permute-done | bytes 163872 | tf_op jit(solution)/shard_map/ppermute | solution.py:55
  54.8 0.0 collective-permute-done.5.came_ref
  54.8 0.8 shard_map.126
  55.5 1.2 %collective-permute-start.11 = (bf16[640,256]{1,0:T(8,128)(2,1)S(1)}, bf16[640,256]{1,0:T(8,128)(2,1)S(1)}, u32[]{:S(2)}, u32[]{:S(2)}) collective-permute-start(bf16[640,256]{1,0:T(8,128)(2,1)S(1)} %get-tuple-element.69), channel_id=1, source_target_pairs={{0,192},{8,200},{16,208},{24,216},{32,224},{40,232},{48,240},{56,2... | collective-permute-start | bytes 983048 | tf_op jit(solution)/shard_map/ppermute | solution.py:55
  56.8 0.3 collective-permute-start.10
  57.1 4.2 %collective-permute-start.12 = (bf16[80,640]{1,0:T(8,128)(2,1)S(1)}, bf16[80,640]{1,0:T(8,128)(2,1)S(1)}, u32[]{:S(2)}, u32[]{:S(2)}) collective-permute-start(bf16[80,640]{1,0:T(8,128)(2,1)S(1)} %get-tuple-element.70.text_a), channel_id=1, source_target_pairs={{0,32},{8,40},{16,48},{24,56},{32,0},{40,8},{48,16},{56,24},{64,96... | collective-permute-start | bytes 307208 | tf_op jit(solution)/shard_map/ppermute | solution.py:80
  61.3 1.2 %shard_map.127.keep_ref = bf16[2,640,256]{2,1,0:T(8,128)(2,1)S(1)} custom-call(s32[5]{0:T(128)S(1)} %stack.27.pos, bf16[640,256]{1,0:T(8,128)(2,1)S(1)} %get-tuple-element.62.dq_ref, bf16[2560,640]{1,0:T(8,128)(2,1)S(1)} %get-tuple-element.45.w_ref, bf16[640,256]{1,0:T(8,128)(2,1)S(1)} %get-tuple-element.66.rest_0_), custom_call_target="tpu_custom_call" | custom-call | flops 1 | bytes 1 | tf_op jit(solution)/shard_map/pallas_call | solution.py:120
  62.5 0.7 shard_map.128
  63.2 2.0 %collective-permute-start.9 = (bf16[640,256]{1,0:T(8,128)(2,1)S(1)}, bf16[640,256]{1,0:T(8,128)(2,1)S(1)}, u32[]{:S(2)}, u32[]{:S(2)}) collective-permute-start(bf16[640,256]{1,0:T(8,128)(2,1)S(1)} %get-tuple-element.68), channel_id=1, source_target_pairs={{0,4},{2,6},{4,0},{6,2},{1,5},{3,7},{5,1},{7,3},{8,12},{10,14},{12... | collective-permute-start | bytes 983048 | tf_op jit(solution)/shard_map/ppermute | solution.py:48
  65.2 1.2 %collective-permute-done.10.b_ref = bf16[640,256]{1,0:T(8,128)(2,1)S(1)} collective-permute-done((bf16[640,256]{1,0:T(8,128)(2,1)S(1)}, bf16[640,256]{1,0:T(8,128)(2,1)S(1)}, u32[]{:S(2)}, u32[]{:S(2)}) %collective-permute-start.10) | collective-permute-done | bytes 327712 | tf_op jit(solution)/shard_map/ppermute | solution.py:55
  66.4 0.9 shard_map.130
  67.3 6.1 %collective-permute-start.13 = (bf16[64,640]{1,0:T(8,128)(2,1)S(1)}, bf16[64,640]{1,0:T(8,128)(2,1)S(1)}, u32[]{:S(2)}, u32[]{:S(2)}) collective-permute-start(bf16[64,640]{1,0:T(8,128)(2,1)S(1)} %get-tuple-element.71), channel_id=1, source_target_pairs={{0,0},{2,34},{4,4},{6,38},{8,8},{10,42},{12,12},{14,46},{16,16},{1... | collective-permute-start | bytes 245768 | tf_op jit(solution)/shard_map/ppermute | solution.py:65
  73.4 0.1 collective-permute-start.14
  73.5 2.4 %collective-permute-start.15 = (bf16[64,640]{1,0:T(8,128)(2,1)S(1)}, bf16[64,640]{1,0:T(8,128)(2,1)S(1)}, u32[]{:S(2)}, u32[]{:S(2)}) collective-permute-start(bf16[64,640]{1,0:T(8,128)(2,1)S(1)} %get-tuple-element.73), channel_id=1, source_target_pairs={{0,16},{2,50},{4,20},{6,54},{8,24},{10,58},{12,28},{14,62},{16,32}... | collective-permute-start | bytes 245768 | tf_op jit(solution)/shard_map/ppermute | solution.py:65
  75.9 2.3 %collective-permute-start.16 = (bf16[64,640]{1,0:T(8,128)(2,1)S(1)}, bf16[64,640]{1,0:T(8,128)(2,1)S(1)}, u32[]{:S(2)}, u32[]{:S(2)}) collective-permute-start(bf16[64,640]{1,0:T(8,128)(2,1)S(1)} %get-tuple-element.74), channel_id=1, source_target_pairs={{0,24},{2,58},{4,28},{6,62},{8,32},{10,2},{12,36},{14,6},{16,40},{... | collective-permute-start | bytes 245768 | tf_op jit(solution)/shard_map/ppermute | solution.py:65
  78.2 0.0 collective-permute-done.13.a_ref
  78.2 0.0 collective-permute-start.21
  78.2 0.5 collective-permute-done.14.b_ref
  78.8 3.8 %collective-permute-start.20 = (bf16[2,80,640]{2,1,0:T(8,128)(2,1)S(1)}, bf16[2,80,640]{2,1,0:T(8,128)(2,1)S(1)}, u32[]{:S(2)}, u32[]{:S(2)}) collective-permute-start(bf16[2,80,640]{2,1,0:T(8,128)(2,1)S(1)} %get-tuple-element.79.own), channel_id=1, source_target_pairs={{0,8},{8,16},{16,24},{24,32},{32,40},{40,48},{48,56},{56,0},{64,72... | collective-permute-start | bytes 614408 | tf_op jit(solution)/shard_map/ppermute | solution.py:85
  82.6 5.9 %collective-permute-done.15.c_ref = bf16[64,640]{1,0:T(8,128)(2,1)S(1)} collective-permute-done((bf16[64,640]{1,0:T(8,128)(2,1)S(1)}, bf16[64,640]{1,0:T(8,128)(2,1)S(1)}, u32[]{:S(2)}, u32[]{:S(2)}) %collective-permute-start.15) | collective-permute-done | bytes 81952 | tf_op jit(solution)/shard_map/ppermute | solution.py:65
  88.5 0.6 shard_map.131
  89.1 0.1 collective-permute-start.17
  89.2 1.3 %collective-permute-done.17.came_ref = bf16[64,640]{1,0:T(8,128)(2,1)S(1)} collective-permute-done((bf16[64,640]{1,0:T(8,128)(2,1)S(1)}, bf16[64,640]{1,0:T(8,128)(2,1)S(1)}, u32[]{:S(2)}, u32[]{:S(2)}) %collective-permute-start.17) | collective-permute-done | bytes 81952 | tf_op jit(solution)/shard_map/ppermute | solution.py:48
  90.4 0.6 shard_map.132
  91.0 0.1 collective-permute-start.18
  91.1 0.0 copy-start
  91.1 1.6 %shard_map.129.after = bf16[2,256,640]{2,1,0:T(8,128)(2,1)} custom-call(s32[5]{0:T(128)S(1)} %stack.27.pos, bf16[256,640]{1,0:T(8,128)(2,1)S(1)} %get-tuple-element.49.after.first_ref, bf16[256,640]{1,0:T(8,128)(2,1)S(1)} %get-tuple-element.57.g_ref, f32[640,256]{1,0:T(8,128)S(1)} %get-tuple-element.67.near_ref, ...), custom_call_target="tpu_custom_call" | custom-call | flops 1 | bytes 1 | tf_op jit(solution)/shard_map/pallas_call | solution.py:120
  92.8 1.3 %collective-permute-done.21.two = bf16[2,80,640]{2,1,0:T(8,128)(2,1)S(1)} collective-permute-done((bf16[2,80,640]{2,1,0:T(8,128)(2,1)S(1)}, bf16[2,80,640]{2,1,0:T(8,128)(2,1)S(1)}, u32[]{:S(2)}, u32[]{:S(2)}) %collective-permute-start.21) | collective-permute-done | bytes 204832 | tf_op jit(solution)/shard_map/ppermute | solution.py:80
  94.1 0.7 collective-permute-done.19.up
  94.8 0.6 shard_map.133.w_ref
  95.4 1.1 %collective-permute-done.18.far_ref = bf16[64,640]{1,0:T(8,128)(2,1)S(1)} collective-permute-done((bf16[64,640]{1,0:T(8,128)(2,1)S(1)}, bf16[64,640]{1,0:T(8,128)(2,1)S(1)}, u32[]{:S(2)}, u32[]{:S(2)}) %collective-permute-start.18) | collective-permute-done | bytes 81952 | tf_op jit(solution)/shard_map/ppermute | solution.py:48
  96.5 1.5 %shard_map.134 = (f32[16,640]{1,0:T(8,128)S(1)}, bf16[16,640]{1,0:T(8,128)(2,1)S(1)}, bf16[16,640]{1,0:T(8,128)(2,1)S(1)}, bf16[16,640]{1,0:T(8,128)(2,1)S(1)}) custom-call(s32[5]{0:T(128)S(1)} %stack.27.pos, f32[64,640]{1,0:T(8,128)S(1)} %get-tuple-element.77.keep_ref, bf16[64,640]{1,0:T(8,128)(2,1)S(1)} %collective-permute-done.18.far_ref, ...), custom_call_target="tpu_custom_call" | custom-call | flops 1 | bytes 1 | tf_op jit(solution)/shard_map/pallas_call | solution.py:120
  98.0 0.1 collective-permute-start.23
  98.1 2.6 %collective-permute-start.24 = (bf16[16,640]{1,0:T(8,128)(2,1)S(1)}, bf16[16,640]{1,0:T(8,128)(2,1)S(1)}, u32[]{:S(2)}, u32[]{:S(2)}) collective-permute-start(bf16[16,640]{1,0:T(8,128)(2,1)S(1)} %get-tuple-element.83), channel_id=1, source_target_pairs={{0,192},{8,200},{16,208},{24,216},{32,224},{40,232},{48,240},{56,2... | collective-permute-start | bytes 61448 | tf_op jit(solution)/shard_map/ppermute | solution.py:55
  100.7 1.2 %collective-permute-done.22 = bf16[16,640]{1,0:T(8,128)(2,1)S(1)} collective-permute-done((bf16[16,640]{1,0:T(8,128)(2,1)S(1)}, bf16[16,640]{1,0:T(8,128)(2,1)S(1)}, u32[]{:S(2)}, u32[]{:S(2)}) %collective-permute-start.22) | collective-permute-done | bytes 20512 | tf_op jit(solution)/shard_map/ppermute | solution.py:55
  101.9 0.4 collective-permute-done.23
  102.2 0.7 collective-permute-done.24
  103.0 0.7 fusion.3
  (14 shorter events, 0.0 us)
Async XLA Ops:
  6.3 7.0 %copy-start.1 = (bf16[80,640]{1,0:T(8,128)(2,1)S(1)}, bf16[80,640]{1,0:T(8,128)(2,1)}, u32[]{:S(2)}) copy-start(bf16[80,640]{1,0:T(8,128)(2,1)} %param.18) | copy-start | bytes 307204
  6.3 5.1 %collective-permute-start = (bf16[2,640,256]{2,1,0:T(8,128)(2,1)S(1)}, bf16[2,640,256]{2,1,0:T(8,128)(2,1)S(1)}, u32[]{:S(2)}, u32[]{:S(2)}) collective-permute-start(bf16[2,640,256]{2,1,0:T(8,128)(2,1)S(1)} %shard_map.114.rest_0_), channel_id=1, source_target_pairs={{0,2},{2,0},{4,6},{6,4},{1,3},{3,1},{5,7},{7,5},{8,10},{10,8},{12,... | collective-permute-start | bytes 1966088 | tf_op jit(solution)/shard_map/ppermute | solution.py:48
  12.0 10.7 %collective-permute-start.1 = (bf16[640,256]{1,0:T(8,128)(2,1)S(1)}, bf16[640,256]{1,0:T(8,128)(2,1)S(1)}, u32[]{:S(2)}, u32[]{:S(2)}) collective-permute-start(bf16[640,256]{1,0:T(8,128)(2,1)S(1)} %get-tuple-element.47.after), channel_id=1, source_target_pairs={{0,4},{2,6},{4,0},{6,2},{1,5},{3,7},{5,1},{7,3},{8,12},{10,14},{12... | collective-permute-start | bytes 983048 | tf_op jit(solution)/shard_map/ppermute | solution.py:48
  13.3 9.4 %collective-permute-start.2 = (bf16[80,640]{1,0:T(8,128)(2,1)S(1)}, bf16[80,640]{1,0:T(8,128)(2,1)S(1)}, u32[]{:S(2)}, u32[]{:S(2)}) collective-permute-start(bf16[80,640]{1,0:T(8,128)(2,1)S(1)} %copy-done.1), channel_id=1, source_target_pairs={{0,0},{2,64},{4,128},{6,192},{8,8},{10,72},{12,136},{14,200},{16,1... | collective-permute-start | bytes 307208 | tf_op jit(solution)/shard_map/ppermute | solution.py:75
  23.6 10.5 %collective-permute-start.3 = (bf16[256,640]{1,0:T(8,128)(2,1)S(1)}, bf16[256,640]{1,0:T(8,128)(2,1)S(1)}, u32[]{:S(2)}, u32[]{:S(2)}) collective-permute-start(bf16[256,640]{1,0:T(8,128)(2,1)S(1)} %get-tuple-element.49.after.first_ref), channel_id=1, source_target_pairs={{8,0},{16,8},{24,16},{32,24},{40,32},{48,40},{56,48},{64,56},{72,6... | collective-permute-start | bytes 983048 | tf_op jit(solution)/shard_map/ppermute | solution.py:89
  38.3 4.1 %collective-permute-start.4 = (bf16[1,640,256]{2,1,0:T(8,128)(2,1)S(1)}, bf16[1,640,256]{2,1,0:T(8,128)(2,1)S(1)}, u32[]{:S(2)}, u32[]{:S(2)}) collective-permute-start(bf16[1,640,256]{2,1,0:T(8,128)(2,1)S(1)} %shard_map.121.rest_0_), channel_id=1, source_target_pairs={{0,2},{2,0},{4,6},{6,4},{1,3},{3,1},{5,7},{7,5},{8,10},{10,8},{12,... | collective-permute-start | bytes 983048 | tf_op jit(solution)/shard_map/ppermute | solution.py:48
  42.3 12.5 %collective-permute-start.5 = (bf16[3,640,256]{2,1,0:T(8,128)(2,1)S(1)}, bf16[3,640,256]{2,1,0:T(8,128)(2,1)S(1)}, u32[]{:S(2)}, u32[]{:S(2)}) collective-permute-start(bf16[3,640,256]{2,1,0:T(8,128)(2,1)S(1)} %shard_map.122.after), channel_id=1, source_target_pairs={{0,2},{2,0},{4,6},{6,4},{1,3},{3,1},{5,7},{7,5},{8,10},{10,8},{12,... | collective-permute-start | bytes 2949128 | tf_op jit(solution)/shard_map/ppermute | solution.py:48
  43.6 9.4 %collective-permute-start.7 = (bf16[320,256]{1,0:T(8,128)(2,1)S(1)}, bf16[320,256]{1,0:T(8,128)(2,1)S(1)}, u32[]{:S(2)}, u32[]{:S(2)}) collective-permute-start(bf16[320,256]{1,0:T(8,128)(2,1)S(1)} %get-tuple-element.63), channel_id=1, source_target_pairs={{0,192},{8,200},{16,208},{24,216},{32,224},{40,232},{48,240},{56,2... | collective-permute-start | bytes 491528 | tf_op jit(solution)/shard_map/ppermute | solution.py:55
  48.6 6.2 %collective-permute-start.6 = (bf16[320,256]{1,0:T(8,128)(2,1)S(1)}, bf16[320,256]{1,0:T(8,128)(2,1)S(1)}, u32[]{:S(2)}, u32[]{:S(2)}) collective-permute-start(bf16[320,256]{1,0:T(8,128)(2,1)S(1)} %get-tuple-element.61.rest_0_), channel_id=1, source_target_pairs={{0,64},{8,72},{16,80},{24,88},{32,96},{40,104},{48,112},{56,120},{... | collective-permute-start | bytes 491528 | tf_op jit(solution)/shard_map/ppermute | solution.py:55
  52.1 10.4 %collective-permute-start.8 = (bf16[2,640,256]{2,1,0:T(8,128)(2,1)S(1)}, bf16[2,640,256]{2,1,0:T(8,128)(2,1)S(1)}, u32[]{:S(2)}, u32[]{:S(2)}) collective-permute-start(bf16[2,640,256]{2,1,0:T(8,128)(2,1)S(1)} %get-tuple-element.65.after), channel_id=1, source_target_pairs={{0,2},{2,0},{4,6},{6,4},{1,3},{3,1},{5,7},{7,5},{8,10},{10,8},{12,... | collective-permute-start | bytes 1966088 | tf_op jit(solution)/shard_map/ppermute | solution.py:48
  55.5 9.7 %collective-permute-start.11 = (bf16[640,256]{1,0:T(8,128)(2,1)S(1)}, bf16[640,256]{1,0:T(8,128)(2,1)S(1)}, u32[]{:S(2)}, u32[]{:S(2)}) collective-permute-start(bf16[640,256]{1,0:T(8,128)(2,1)S(1)} %get-tuple-element.69), channel_id=1, source_target_pairs={{0,192},{8,200},{16,208},{24,216},{32,224},{40,232},{48,240},{56,2... | collective-permute-start | bytes 983048 | tf_op jit(solution)/shard_map/ppermute | solution.py:55
  56.8 9.7 %collective-permute-start.10 = (bf16[640,256]{1,0:T(8,128)(2,1)S(1)}, bf16[640,256]{1,0:T(8,128)(2,1)S(1)}, u32[]{:S(2)}, u32[]{:S(2)}) collective-permute-start(bf16[640,256]{1,0:T(8,128)(2,1)S(1)} %get-tuple-element.66.rest_0_), channel_id=1, source_target_pairs={{0,64},{8,72},{16,80},{24,88},{32,96},{40,104},{48,112},{56,120},{... | collective-permute-start | bytes 983048 | tf_op jit(solution)/shard_map/ppermute | solution.py:55
  57.1 8.1 %collective-permute-start.12 = (bf16[80,640]{1,0:T(8,128)(2,1)S(1)}, bf16[80,640]{1,0:T(8,128)(2,1)S(1)}, u32[]{:S(2)}, u32[]{:S(2)}) collective-permute-start(bf16[80,640]{1,0:T(8,128)(2,1)S(1)} %get-tuple-element.70.text_a), channel_id=1, source_target_pairs={{0,32},{8,40},{16,48},{24,56},{32,0},{40,8},{48,16},{56,24},{64,96... | collective-permute-start | bytes 307208 | tf_op jit(solution)/shard_map/ppermute | solution.py:80
  63.2 27.9 %collective-permute-start.9 = (bf16[640,256]{1,0:T(8,128)(2,1)S(1)}, bf16[640,256]{1,0:T(8,128)(2,1)S(1)}, u32[]{:S(2)}, u32[]{:S(2)}) collective-permute-start(bf16[640,256]{1,0:T(8,128)(2,1)S(1)} %get-tuple-element.68), channel_id=1, source_target_pairs={{0,4},{2,6},{4,0},{6,2},{1,5},{3,7},{5,1},{7,3},{8,12},{10,14},{12... | collective-permute-start | bytes 983048 | tf_op jit(solution)/shard_map/ppermute | solution.py:48
  67.3 10.9 %collective-permute-start.13 = (bf16[64,640]{1,0:T(8,128)(2,1)S(1)}, bf16[64,640]{1,0:T(8,128)(2,1)S(1)}, u32[]{:S(2)}, u32[]{:S(2)}) collective-permute-start(bf16[64,640]{1,0:T(8,128)(2,1)S(1)} %get-tuple-element.71), channel_id=1, source_target_pairs={{0,0},{2,34},{4,4},{6,38},{8,8},{10,42},{12,12},{14,46},{16,16},{1... | collective-permute-start | bytes 245768 | tf_op jit(solution)/shard_map/ppermute | solution.py:65
  73.4 5.4 %collective-permute-start.14 = (bf16[64,640]{1,0:T(8,128)(2,1)S(1)}, bf16[64,640]{1,0:T(8,128)(2,1)S(1)}, u32[]{:S(2)}, u32[]{:S(2)}) collective-permute-start(bf16[64,640]{1,0:T(8,128)(2,1)S(1)} %get-tuple-element.72), channel_id=1, source_target_pairs={{0,8},{2,42},{4,12},{6,46},{8,16},{10,50},{12,20},{14,54},{16,24},... | collective-permute-start | bytes 245768 | tf_op jit(solution)/shard_map/ppermute | solution.py:65
  73.5 15.0 %collective-permute-start.15 = (bf16[64,640]{1,0:T(8,128)(2,1)S(1)}, bf16[64,640]{1,0:T(8,128)(2,1)S(1)}, u32[]{:S(2)}, u32[]{:S(2)}) collective-permute-start(bf16[64,640]{1,0:T(8,128)(2,1)S(1)} %get-tuple-element.73), channel_id=1, source_target_pairs={{0,16},{2,50},{4,20},{6,54},{8,24},{10,58},{12,28},{14,62},{16,32}... | collective-permute-start | bytes 245768 | tf_op jit(solution)/shard_map/ppermute | solution.py:65
  75.9 12.5 %collective-permute-start.16 = (bf16[64,640]{1,0:T(8,128)(2,1)S(1)}, bf16[64,640]{1,0:T(8,128)(2,1)S(1)}, u32[]{:S(2)}, u32[]{:S(2)}) collective-permute-start(bf16[64,640]{1,0:T(8,128)(2,1)S(1)} %get-tuple-element.74), channel_id=1, source_target_pairs={{0,24},{2,58},{4,28},{6,62},{8,32},{10,2},{12,36},{14,6},{16,40},{... | collective-permute-start | bytes 245768 | tf_op jit(solution)/shard_map/ppermute | solution.py:65
  78.2 15.9 %collective-permute-start.21 = (bf16[2,80,640]{2,1,0:T(8,128)(2,1)S(1)}, bf16[2,80,640]{2,1,0:T(8,128)(2,1)S(1)}, u32[]{:S(2)}, u32[]{:S(2)}) collective-permute-start(bf16[2,80,640]{2,1,0:T(8,128)(2,1)S(1)} %get-tuple-element.79.own), channel_id=1, source_target_pairs={{0,16},{8,24},{16,0},{24,8},{32,48},{40,56},{48,32},{56,40},{64,80... | collective-permute-start | bytes 614408 | tf_op jit(solution)/shard_map/ppermute | solution.py:80
  78.8 15.3 %collective-permute-start.20 = (bf16[2,80,640]{2,1,0:T(8,128)(2,1)S(1)}, bf16[2,80,640]{2,1,0:T(8,128)(2,1)S(1)}, u32[]{:S(2)}, u32[]{:S(2)}) collective-permute-start(bf16[2,80,640]{2,1,0:T(8,128)(2,1)S(1)} %get-tuple-element.79.own), channel_id=1, source_target_pairs={{0,8},{8,16},{16,24},{24,32},{32,40},{40,48},{48,56},{56,0},{64,72... | collective-permute-start | bytes 614408 | tf_op jit(solution)/shard_map/ppermute | solution.py:85
  88.5 6.3 %collective-permute-start.19 = (bf16[2,80,640]{2,1,0:T(8,128)(2,1)S(1)}, bf16[2,80,640]{2,1,0:T(8,128)(2,1)S(1)}, u32[]{:S(2)}, u32[]{:S(2)}) collective-permute-start(bf16[2,80,640]{2,1,0:T(8,128)(2,1)S(1)} %get-tuple-element.79.own), channel_id=1, source_target_pairs={{0,56},{8,0},{16,8},{24,16},{32,24},{40,32},{48,40},{56,48},{64,12... | collective-permute-start | bytes 614408 | tf_op jit(solution)/shard_map/ppermute | solution.py:85
  89.1 1.4 %collective-permute-start.17 = (bf16[64,640]{1,0:T(8,128)(2,1)S(1)}, bf16[64,640]{1,0:T(8,128)(2,1)S(1)}, u32[]{:S(2)}, u32[]{:S(2)}) collective-permute-start(bf16[64,640]{1,0:T(8,128)(2,1)S(1)} %get-tuple-element.76), channel_id=1, source_target_pairs={{0,2},{2,0},{4,6},{6,4},{1,3},{3,1},{5,7},{7,5},{8,10},{10,8},{12,... | collective-permute-start | bytes 245768 | tf_op jit(solution)/shard_map/ppermute | solution.py:48
  91.0 5.5 %collective-permute-start.18 = (bf16[64,640]{1,0:T(8,128)(2,1)S(1)}, bf16[64,640]{1,0:T(8,128)(2,1)S(1)}, u32[]{:S(2)}, u32[]{:S(2)}) collective-permute-start(bf16[64,640]{1,0:T(8,128)(2,1)S(1)} %get-tuple-element.78), channel_id=1, source_target_pairs={{0,4},{2,6},{4,0},{6,2},{1,5},{3,7},{5,1},{7,3},{8,12},{10,14},{12... | collective-permute-start | bytes 245768 | tf_op jit(solution)/shard_map/ppermute | solution.py:48
  91.1 11.9 %copy-start = (bf16[640,16]{0,1:T(8,128)(2,1)S(1)}, bf16[640,16]{0,1:T(8,128)(2,1)}, u32[]{:S(2)}) copy-start(bf16[640,16]{0,1:T(8,128)(2,1)} %param.19) | copy-start | bytes 61444
  98.0 3.9 %collective-permute-start.22 = (bf16[16,640]{1,0:T(8,128)(2,1)S(1)}, bf16[16,640]{1,0:T(8,128)(2,1)S(1)}, u32[]{:S(2)}, u32[]{:S(2)}) collective-permute-start(bf16[16,640]{1,0:T(8,128)(2,1)S(1)} %get-tuple-element.81), channel_id=1, source_target_pairs={{0,64},{8,72},{16,80},{24,88},{32,96},{40,104},{48,112},{56,120},{... | collective-permute-start | bytes 61448 | tf_op jit(solution)/shard_map/ppermute | solution.py:55
  98.0 4.2 %collective-permute-start.23 = (bf16[16,640]{1,0:T(8,128)(2,1)S(1)}, bf16[16,640]{1,0:T(8,128)(2,1)S(1)}, u32[]{:S(2)}, u32[]{:S(2)}) collective-permute-start(bf16[16,640]{1,0:T(8,128)(2,1)S(1)} %get-tuple-element.82), channel_id=1, source_target_pairs={{0,128},{8,136},{16,144},{24,152},{32,160},{40,168},{48,176},{56,1... | collective-permute-start | bytes 61448 | tf_op jit(solution)/shard_map/ppermute | solution.py:55
  98.1 4.9 %collective-permute-start.24 = (bf16[16,640]{1,0:T(8,128)(2,1)S(1)}, bf16[16,640]{1,0:T(8,128)(2,1)S(1)}, u32[]{:S(2)}, u32[]{:S(2)}) collective-permute-start(bf16[16,640]{1,0:T(8,128)(2,1)S(1)} %get-tuple-element.83), channel_id=1, source_target_pairs={{0,192},{8,200},{16,208},{24,216},{32,224},{40,232},{48,240},{56,2... | collective-permute-start | bytes 61448 | tf_op jit(solution)/shard_map/ppermute | solution.py:55

commit v4 on v3

--- a/solution.py
+++ b/solution.py
@@ -231,7 +231,8 @@
         copy.wait()
 
 
-def ahead_kernel(pos, q_ref, k_ref, after, p_ref, low_ref):
+def ahead_kernel(pos, q_ref, k_ref, one_ref, after, p_ref, low_ref, late_one):
+    late_one[...] = one_ref[...]
     for i, h in enumerate(heads_of(k_ref.shape[-1])):
         shifted, factor = weights_of(q_ref[:, h], k_ref[:, h])
         attention = shifted * factor
@@ -280,9 +281,10 @@
 
 
 def x_add_kernel(
-    pos, keep_ref, came_ref, top_ref, bottom_ref, one_ref, after, late_one, next_ref, previous_ref
+    pos, keep_ref, came_ref, top_ref, bottom_ref, text_a, text_b, after, two_ref, next_ref, previous_ref
 ):
-    late_one[...] = one_ref[...]
+    two_ref[0] = text_a[...]
+    two_ref[1] = text_b[...]
     half = top_ref.shape[0]
     next_ref[...] = (keep_ref[1].astype(F32) + came_ref[1].astype(F32)).astype(BF16)
     total = keep_ref[1, :half].astype(F32) + came_ref[1, :half].astype(F32)
@@ -292,9 +294,8 @@
     previous_ref[half:] = (total + bottom_ref[...].astype(F32)).astype(BF16)
 
 
-def z_add_kernel(pos, keep_ref, came_ref, b_ref, c_ref, text_a, text_b, two_ref, *outs):
-    two_ref[0] = text_a[...]
-    two_ref[1] = text_b[...]
+def z_add_kernel(pos, keep_ref, came_ref, b_ref, c_ref, text, two_ref, *outs):
+    two_ref[...] = text[...]
     rows = outs[0].shape[0]
     width = outs[0].shape[1]
     for place in (slice(0, width // 2), slice(width // 2, width)):
@@ -311,7 +312,7 @@
     project_kernel(1, pos, dq_ref, w_ref, out_ref)
 
 
-def z_sum_kernel(pos, a_ref, b_ref, c_ref, d_ref, keep_ref, send_ref):
+def z_sum_kernel(pos, a_ref, b_ref, c_ref, d_ref, after, keep_ref, send_ref):
     total = a_ref[...].astype(F32) + b_ref[...].astype(F32)
     total = total + c_ref[...].astype(F32) + d_ref[...].astype(F32)
     keep_ref[...] = total
@@ -334,13 +335,13 @@
 
 
 def text_kernel(pos, keep_ref, far_ref, w_ref, after, *rest):
-    *outs, context_ref = rest
-    context_ref[...] = (keep_ref[...] + far_ref[...].astype(F32)).astype(BF16)
+    *outs, total_ref = rest
+    context = (keep_ref[...] + far_ref[...].astype(F32)).astype(BF16)
+    total_ref[...] = dot(context, w_ref[...], NT)
     tokens = outs[0].shape[0]
     for i, out in enumerate(outs):
         row = pl.multiple_of((pos[0] + i) % NX * tokens, tokens)
-        total = dot(context_ref[pl.ds(row, tokens), :], w_ref[...], NT)
-        out[...] = total.astype(out.dtype)
+        out[...] = total_ref[pl.ds(row, tokens), :].astype(out.dtype)
 
 
 def sent_kernel(pos, first_ref, g_ref, near_ref, far_ref, out_hbm, out_ref, sems):
@@ -441,11 +442,12 @@
         [act, (block, BF16)],
     )
     came_back = pass_back(sent0)
-    p1, p1_low = call(
+    p1, p1_low, text_one = call(
         ahead_kernel,
-        [where, (q1, VMEM), (k, VMEM), (sent0, ANY)],
-        [((heads, text, rows), F32), ((heads, text, rows), BF16)],
-    )
+        [where, (q1, VMEM), (k, VMEM), (text_one, VMEM), (sent0, ANY)],
+        [((heads, text, rows), F32), ((heads, text, rows), BF16), (block, BF16)],
+    )
+    text_across = swap_z(text_one, 4)
 
     g1, ds1, low = call(
         second_kernel,
@@ -462,7 +464,7 @@
         )[0]
 
     near_steps = (0, 1, 3)
-    send_across = context_terms(0, (2,))
+    send_across = context_terms(0, (2,), text_across)
     came_across = swap_tensor(send_across, 1)
     send = context_terms(0, near_steps, send_across)
     came = swap_tensor(send, 1)
@@ -481,15 +483,15 @@
         [turned, pair],
     )
     came1 = swap_tensor(send1, 1)
-    text_one, to_next, to_previous = call(
+    text_two, to_next, to_previous = call(
         x_add_kernel,
-        [where] + [(a, VMEM) for a in (keep, came, *across, text_one)]
+        [where] + [(a, VMEM) for a in (keep, came, *across, text_one, text_across)]
         + [(send1, ANY)],
-        [(block, BF16)] + [((width, text // 2), BF16)] * 2,
+        [((2,) + block, BF16)] + [((width, text // 2), BF16)] * 2,
         flops=LONG,
     )
+    text_second = swap_z(text_two, 2)
     came_x = [send_x(to_next, 1), send_x(to_previous, -1)]
-    text_across = swap_z(text_one, 4)
 
     keep1 = project(0, dq1, to_next)
     near1, far1 = call(
@@ -509,14 +511,14 @@
     few = text // NZ
     text_two, *by_z = call(
         z_add_kernel,
-        [where] + [(a, VMEM) for a in (keep, came, *came_x, text_one, text_across)],
+        [where] + [(a, VMEM) for a in (keep, came, *came_x, text_two)],
         [((2,) + block, BF16)] + [((few, width), BF16)] * (NZ // 2),
     )
-    text_more = [from_z(text_two, 1), from_z(text_two, -1), swap_z(text_two, 2)]
+    text_more = [from_z(text_two, 1), from_z(text_two, -1), text_second]
     came_z = [send_z(by_z[i], i) for i in range(NZ // 2)]
     context, context_low = call(
         z_sum_kernel,
-        [where] + [(a, VMEM) for a in came_z],
+        [where] + [(a, VMEM) for a in came_z] + [(text_second, ANY)],
         [((few, width), F32), ((few, width), BF16)],
     )
     context, context_low = call(
@@ -535,7 +537,7 @@
         text_kernel,
         [where] + [(a, VMEM) for a in (context, far_context, gathered)] + [(sent, HBM)],
         [((tokens, width), F32)] + [((tokens, width), BF16)] * (NX - 1),
-        [vm((few, width), BF16)],
+        [vm((few, width), F32)],
     )
     for i, piece in enumerate(to_send):
         hidden = hidden + send_x(piece, i + 1).astype(F32)

time: 105 us -> 103 us (0.981)
  waiting for transfers between devices: 24.1 us -> 11.6 us
  starting transfers between devices: 42.8 us -> 53.8 us
    ppermute x1, waiting for transfers between devices: 7.47 us -> 0.01 us  [pass_back(): lax.ppermute(value, 'section', [(s + 1, s) for s in range(SECTIONS - 1)])]
    ppermute x4, waiting for transfers between devices: 6.42 us -> 0.01 us  [send_z(): return lax.ppermute(value, ('section', 'tensor'), pairs)]
    ppermute x7, waiting for transfers between devices: 5.31 us -> 9.53 us  [send_x(): return lax.ppermute(value, 'section', pairs)]
    ppermute x7, starting transfers between devices: 9.27 us -> 13.1 us  [send_x(): return lax.ppermute(value, 'section', pairs)]
    ppermute x8, starting transfers between devices: 9.72 us -> 13.5 us  [swap_tensor(): return lax.ppermute(value, 'tensor', [(i, i ^ bit) for i in range(TENSOR)])]
    ppermute x2, starting transfers between devices: 4.19 us -> 7.62 us  [swap_z(): return lax.ppermute(value, 'section', pairs)]
    ppermute x2, waiting for transfers between devices: 1.33 us -> 0.01 us  [swap_z(): return lax.ppermute(value, 'section', pairs)]
    ppermute x4, starting transfers between devices: 10.9 us -> 9.84 us  [send_z(): return lax.ppermute(value, ('section', 'tensor'), pairs)]
  transfers between devices with their start and end apart: 25 -> 25, of which waited for: 13 -> 9; matrix products, arithmetic and copies ran while one was open for 0% -> 0% of each run, Pallas kernels for 22% -> 25%
where the time goes in v4:
time: 103 us; the launch traced here: 101 us
  starting transfers between devices  53.8 us (52%)
  Pallas kernels  34.4 us (33%)
  waiting for transfers between devices  11.6 us (11%)
    pallas_call x22, Pallas kernels, call(): pl.pallas_call(body, in_specs=[spec for array, spec in ins], out_specs=[p...  34.4 us
    ppermute x8, starting transfers between devices, swap_tensor(): return lax.ppermute(value, 'tensor', [(i, i ^ bit) for i in range(TENSOR)])  13.5 us
    ppermute x7, starting transfers between devices, send_x(): return lax.ppermute(value, 'section', pairs)  13.1 us
    ppermute x4, starting transfers between devices, send_z(): return lax.ppermute(value, ('section', 'tensor'), pairs)  9.84 us
    ppermute x7, waiting for transfers between devices, send_x(): return lax.ppermute(value, 'section', pairs)  9.53 us
    ppermute x2, starting transfers between devices, swap_z(): return lax.ppermute(value, 'section', pairs)  7.62 us
    ppermute x2, starting transfers between devices, from_z(): return lax.ppermute(value, 'section', pairs)  4.73 us
    ppermute x1, starting transfers between devices, turn(): return lax.ppermute(value, ('section', 'tensor'), pairs)  3.64 us
  transfers between devices with their start and end apart: 25, of which 9 were waited for; matrix products, arithmetic and copies ran while one was open for 0% of the time, Pallas kernels for 25%

profile of v4, /device:TPU:1, one launch (start us, length us, event | category | flops | bytes accessed | tf_op | source)
XLA Modules:
  0.0 101.4 jit_solution(17468696235641831608)
XLA Ops:
  0.7 0.1 stack.27.pos
  0.8 4.3 %shard_map.113 = (bf16[640,256]{1,0:T(8,128)(2,1)S(1)}, bf16[2560,640]{1,0:T(8,128)(2,1)S(1)}, bf16[256,640]{1,0:T(8,128)(2,1)S(1)}) custom-call(s32[5]{0:T(128)S(1)} %stack.27.pos, bf16[1,2,256,640]{3,2,1,0:T(8,128)(2,1)} %q_hbm.3, bf16[1,512,640]{2,1,0:T(8,128)(2,1)} %k_hbm.3, bf16[1,512,640]{2,1,0:T(8,128)(2,1)} %v_hbm.3, bf16[1,256,640]{2,1,0:T(8,128)(2,1)} %g_hbm.3, ...), custom_call_target="tpu_custom_call" | custom-call | flops 1 | bytes 1 | tf_op jit(solution)/shard_map/pallas_call | solution.py:120
  5.1 1.2 %shard_map.114.rest_0_ = bf16[2,640,256]{2,1,0:T(8,128)(2,1)S(1)} custom-call(s32[5]{0:T(128)S(1)} %stack.27.pos, bf16[640,256]{1,0:T(8,128)(2,1)S(1)} %get-tuple-element.45.dq_ref, bf16[2560,640]{1,0:T(8,128)(2,1)S(1)} %get-tuple-element.46.w_ref), custom_call_target="tpu_custom_call" | custom-call | flops 1 | bytes 1 | tf_op jit(solution)/shard_map/pallas_call | solution.py:120
  6.3 0.0 copy-start.1
  6.3 3.3 %collective-permute-start = (bf16[2,640,256]{2,1,0:T(8,128)(2,1)S(1)}, bf16[2,640,256]{2,1,0:T(8,128)(2,1)S(1)}, u32[]{:S(2)}, u32[]{:S(2)}) collective-permute-start(bf16[2,640,256]{2,1,0:T(8,128)(2,1)S(1)} %shard_map.114.rest_0_), channel_id=1, source_target_pairs={{0,2},{2,0},{4,6},{6,4},{1,3},{3,1},{5,7},{7,5},{8,10},{10,8},{12,... | collective-permute-start | bytes 1966088 | tf_op jit(solution)/shard_map/ppermute | solution.py:48
  9.6 1.2 %shard_map.115.keep_ref = bf16[2,640,256]{2,1,0:T(8,128)(2,1)S(1)} custom-call(s32[5]{0:T(128)S(1)} %stack.27.pos, bf16[640,256]{1,0:T(8,128)(2,1)S(1)} %get-tuple-element.45.dq_ref, bf16[2560,640]{1,0:T(8,128)(2,1)S(1)} %get-tuple-element.46.w_ref, bf16[2,640,256]{2,1,0:T(8,128)(2,1)S(1)} %shard_map.114.rest_0_), custom_call_target="tpu_custom_call" | custom-call | flops 1 | bytes 1 | tf_op jit(solution)/shard_map/pallas_call | solution.py:120
  10.8 0.5 collective-permute-done.came_ref
  11.4 0.7 shard_map.116
  12.0 1.3 %collective-permute-start.1 = (bf16[640,256]{1,0:T(8,128)(2,1)S(1)}, bf16[640,256]{1,0:T(8,128)(2,1)S(1)}, u32[]{:S(2)}, u32[]{:S(2)}) collective-permute-start(bf16[640,256]{1,0:T(8,128)(2,1)S(1)} %get-tuple-element.48.after), channel_id=1, source_target_pairs={{0,4},{2,6},{4,0},{6,2},{1,5},{3,7},{5,1},{7,3},{8,12},{10,14},{12... | collective-permute-start | bytes 983048 | tf_op jit(solution)/shard_map/ppermute | solution.py:48
  13.3 3.6 %collective-permute-start.2 = (bf16[80,640]{1,0:T(8,128)(2,1)S(1)}, bf16[80,640]{1,0:T(8,128)(2,1)S(1)}, u32[]{:S(2)}, u32[]{:S(2)}) collective-permute-start(bf16[80,640]{1,0:T(8,128)(2,1)S(1)} %copy-done.1), channel_id=1, source_target_pairs={{0,0},{2,64},{4,128},{6,192},{8,8},{10,72},{12,136},{14,200},{16,1... | collective-permute-start | bytes 307208 | tf_op jit(solution)/shard_map/ppermute | solution.py:75
  17.0 5.8 %shard_map.117 = (f32[512,640]{1,0:T(8,128)S(1)}, f32[512,640]{1,0:T(8,128)S(1)}, bf16[256,640]{1,0:T(8,128)(2,1)S(1)}, bf16[512,640]{1,0:T(8,128)(2,1)S(1)}, bf...) custom-call(s32[5]{0:T(128)S(1)} %stack.27.pos, ...), custom_call_target="tpu_custom_call" | custom-call | flops 1 | bytes 1 | tf_op jit(solution)/shard_map/pallas_call | solution.py:120
  22.8 0.0 collective-permute-done.1.far_ref
  22.8 0.8 shard_map.118
  23.6 1.3 %collective-permute-start.3 = (bf16[256,640]{1,0:T(8,128)(2,1)S(1)}, bf16[256,640]{1,0:T(8,128)(2,1)S(1)}, u32[]{:S(2)}, u32[]{:S(2)}) collective-permute-start(bf16[256,640]{1,0:T(8,128)(2,1)S(1)} %get-tuple-element.50.after.first_ref), channel_id=1, source_target_pairs={{8,0},{16,8},{24,16},{32,24},{40,32},{48,40},{56,48},{64,56},{72,6... | collective-permute-start | bytes 983048 | tf_op jit(solution)/shard_map/ppermute | solution.py:89
  24.9 1.7 %shard_map.119 = (f32[5,512,256]{2,1,0:T(8,128)S(1)}, bf16[5,512,256]{2,1,0:T(8,128)(2,1)S(1)}, bf16[80,640]{1,0:T(8,128)(2,1)S(1)}) custom-call(s32[5]{0:T(128)S(1)} %stack.27.pos, bf16[256,640]{1,0:T(8,128)(2,1)S(1)} %get-tuple-element.51.q_ref, bf16[512,640]{1,0:T(8,128)(2,1)S(1)} %get-tuple-element.55.k_ref, ...), custom_call_target="tpu_custom_call" | custom-call | flops 1 | bytes 1 | tf_op jit(solution)/shard_map/pallas_call | solution.py:120
  26.6 7.6 %collective-permute-start.4 = (bf16[80,640]{1,0:T(8,128)(2,1)S(1)}, bf16[80,640]{1,0:T(8,128)(2,1)S(1)}, u32[]{:S(2)}, u32[]{:S(2)}) collective-permute-start(bf16[80,640]{1,0:T(8,128)(2,1)S(1)} %get-tuple-element.63.text_a), channel_id=1, source_target_pairs={{0,32},{8,40},{16,48},{24,56},{32,0},{40,8},{48,16},{56,24},{64,96... | collective-permute-start | bytes 307208 | tf_op jit(solution)/shard_map/ppermute | solution.py:80
  34.2 3.0 %shard_map.120 = (bf16[256,640]{1,0:T(8,128)(2,1)S(1)}, bf16[5,512,256]{2,1,0:T(8,128)(2,1)S(1)}, bf16[512,1280]{1,0:T(8,128)(2,1)S(1)}) custom-call(s32[5]{0:T(128)S(1)} %stack.27.pos, bf16[256,640]{1,0:T(8,128)(2,1)S(1)} %get-tuple-element.51.q_ref, bf16[512,640]{1,0:T(8,128)(2,1)S(1)} %get-tuple-element.52.v_ref, ...), custom_call_target="tpu_custom_call" | custom-call | flops 1 | bytes 1 | tf_op jit(solution)/shard_map/pallas_call | solution.py:120
  37.3 1.2 %shard_map.121.rest_0_ = bf16[1,640,256]{2,1,0:T(8,128)(2,1)S(1)} custom-call(s32[5]{0:T(128)S(1)} %stack.27.pos, bf16[512,1280]{1,0:T(8,128)(2,1)S(1)} %get-tuple-element.61.low_ref, bf16[2560,1280]{1,0:T(8,128)(2,1)S(1)} %get-tuple-element.62.w_ref, bf16[80,640]{1,0:T(8,128)(2,1)S(1)} %collective-permute-done.4.rest_0_.text_b), custom_call_target="tpu_custom_call" | custom-call | flops 1 | bytes 1 | tf_op jit(solution)/shard_map/pallas_call | solution.py:120
  38.4 2.4 %collective-permute-start.5 = (bf16[1,640,256]{2,1,0:T(8,128)(2,1)S(1)}, bf16[1,640,256]{2,1,0:T(8,128)(2,1)S(1)}, u32[]{:S(2)}, u32[]{:S(2)}) collective-permute-start(bf16[1,640,256]{2,1,0:T(8,128)(2,1)S(1)} %shard_map.121.rest_0_), channel_id=1, source_target_pairs={{0,2},{2,0},{4,6},{6,4},{1,3},{3,1},{5,7},{7,5},{8,10},{10,8},{12,... | collective-permute-start | bytes 983048 | tf_op jit(solution)/shard_map/ppermute | solution.py:48
  40.8 2.0 %shard_map.122.after = bf16[3,640,256]{2,1,0:T(8,128)(2,1)S(1)} custom-call(s32[5]{0:T(128)S(1)} %stack.27.pos, bf16[512,1280]{1,0:T(8,128)(2,1)S(1)} %get-tuple-element.61.low_ref, bf16[2560,1280]{1,0:T(8,128)(2,1)S(1)} %get-tuple-element.62.w_ref, bf16[1,640,256]{2,1,0:T(8,128)(2,1)S(1)} %shard_map.121.rest_0_), custom_call_target="tpu_custom_call" | custom-call | flops 1 | bytes 1 | tf_op jit(solution)/shard_map/pallas_call | solution.py:120
  42.9 0.1 collective-permute-start.6
  43.0 0.0 collective-permute-done.5.came_ref
  43.0 1.2 %shard_map.123 = (bf16[320,256]{1,0:T(8,128)(2,1)S(1)}, bf16[320,256]{1,0:T(8,128)(2,1)S(1)}) custom-call(s32[5]{0:T(128)S(1)} %stack.27.pos, bf16[512,1280]{1,0:T(8,128)(2,1)S(1)} %get-tuple-element.61.low_ref, bf16[2560,1280]{1,0:T(8,128)(2,1)S(1)} %get-tuple-element.62.w_ref, bf16[1,640,256]{2,1,0:T(8,128)(2,1)S(1)} %collective-permute-done.5.came_ref, ...), custom_call_target="tpu_custom_call" | custom-call | flops 1 | bytes 1 | tf_op jit(solution)/shard_map/pallas_call | solution.py:120
  44.1 8.8 %collective-permute-start.8 = (bf16[320,256]{1,0:T(8,128)(2,1)S(1)}, bf16[320,256]{1,0:T(8,128)(2,1)S(1)}, u32[]{:S(2)}, u32[]{:S(2)}) collective-permute-start(bf16[320,256]{1,0:T(8,128)(2,1)S(1)} %get-tuple-element.66), channel_id=1, source_target_pairs={{0,192},{8,200},{16,208},{24,216},{32,224},{40,232},{48,240},{56,2... | collective-permute-start | bytes 491528 | tf_op jit(solution)/shard_map/ppermute | solution.py:55
  53.0 0.0 collective-permute-start.7
  53.0 2.0 %shard_map.124.after.keep_ref = bf16[3,640,256]{2,1,0:T(8,128)(2,1)S(1)} custom-call(s32[5]{0:T(128)S(1)} %stack.27.pos, bf16[512,1280]{1,0:T(8,128)(2,1)S(1)} %get-tuple-element.61.low_ref, bf16[2560,1280]{1,0:T(8,128)(2,1)S(1)} %get-tuple-element.62.w_ref, bf16[320,256]{1,0:T(8,128)(2,1)S(1)} %get-tuple-element.64.rest_0_), custom_call_target="tpu_custom_call" | custom-call | flops 40000000000 | bytes 1 | tf_op jit(solution)/shard_map/pallas_call | solution.py:120
  55.0 1.5 %shard_map.125 = (bf16[640,256]{1,0:T(8,128)(2,1)S(1)}, bf16[2,640,256]{2,1,0:T(8,128)(2,1)S(1)}) custom-call(s32[5]{0:T(128)S(1)} %stack.27.pos, bf16[5,512,256]{2,1,0:T(8,128)(2,1)S(1)} %get-tuple-element.60.ds_ref, bf16[512,640]{1,0:T(8,128)(2,1)S(1)} %get-tuple-element.55.k_ref, bf16[2560,640]{1,0:T(8,128)(2,1)S(1)} %get-tuple-element.46.w_ref, ...), custom_call_target="tpu_custom_call" | custom-call | flops 1 | bytes 1 | tf_op jit(solution)/shard_map/pallas_call | solution.py:120
  56.5 0.9 collective-permute-start.9
  57.3 1.8 %collective-permute-done.7.top_ref = bf16[320,256]{1,0:T(8,128)(2,1)S(1)} collective-permute-done((bf16[320,256]{1,0:T(8,128)(2,1)S(1)}, bf16[320,256]{1,0:T(8,128)(2,1)S(1)}, u32[]{:S(2)}, u32[]{:S(2)}) %collective-permute-start.7) | collective-permute-done | bytes 163872 | tf_op jit(solution)/shard_map/ppermute | solution.py:55
  59.1 0.0 collective-permute-done.6.came_ref
  59.1 0.7 shard_map.126
  59.9 1.2 %collective-permute-start.12 = (bf16[640,256]{1,0:T(8,128)(2,1)S(1)}, bf16[640,256]{1,0:T(8,128)(2,1)S(1)}, u32[]{:S(2)}, u32[]{:S(2)}) collective-permute-start(bf16[640,256]{1,0:T(8,128)(2,1)S(1)} %get-tuple-element.71), channel_id=1, source_target_pairs={{0,192},{8,200},{16,208},{24,216},{32,224},{40,232},{48,240},{56,2... | collective-permute-start | bytes 983048 | tf_op jit(solution)/shard_map/ppermute | solution.py:55
  61.1 0.3 collective-permute-start.11
  61.5 1.2 %shard_map.127.keep_ref = bf16[2,640,256]{2,1,0:T(8,128)(2,1)S(1)} custom-call(s32[5]{0:T(128)S(1)} %stack.27.pos, bf16[640,256]{1,0:T(8,128)(2,1)S(1)} %get-tuple-element.65.dq_ref, bf16[2560,640]{1,0:T(8,128)(2,1)S(1)} %get-tuple-element.46.w_ref, bf16[640,256]{1,0:T(8,128)(2,1)S(1)} %get-tuple-element.68.rest_0_), custom_call_target="tpu_custom_call" | custom-call | flops 1 | bytes 1 | tf_op jit(solution)/shard_map/pallas_call | solution.py:120
  62.7 0.7 shard_map.128
  63.4 2.0 %collective-permute-start.10 = (bf16[640,256]{1,0:T(8,128)(2,1)S(1)}, bf16[640,256]{1,0:T(8,128)(2,1)S(1)}, u32[]{:S(2)}, u32[]{:S(2)}) collective-permute-start(bf16[640,256]{1,0:T(8,128)(2,1)S(1)} %get-tuple-element.70), channel_id=1, source_target_pairs={{0,4},{2,6},{4,0},{6,2},{1,5},{3,7},{5,1},{7,3},{8,12},{10,14},{12... | collective-permute-start | bytes 983048 | tf_op jit(solution)/shard_map/ppermute | solution.py:48
  65.4 2.3 %collective-permute-done.12.c_ref = bf16[640,256]{1,0:T(8,128)(2,1)S(1)} collective-permute-done((bf16[640,256]{1,0:T(8,128)(2,1)S(1)}, bf16[640,256]{1,0:T(8,128)(2,1)S(1)}, u32[]{:S(2)}, u32[]{:S(2)}) %collective-permute-start.12) | collective-permute-done | bytes 327712 | tf_op jit(solution)/shard_map/ppermute | solution.py:55
  67.7 3.1 %collective-permute-done.11.b_ref = bf16[640,256]{1,0:T(8,128)(2,1)S(1)} collective-permute-done((bf16[640,256]{1,0:T(8,128)(2,1)S(1)}, bf16[640,256]{1,0:T(8,128)(2,1)S(1)}, u32[]{:S(2)}, u32[]{:S(2)}) %collective-permute-start.11) | collective-permute-done | bytes 327712 | tf_op jit(solution)/shard_map/ppermute | solution.py:55
  70.8 0.9 shard_map.130
  71.7 3.9 %collective-permute-start.13 = (bf16[64,640]{1,0:T(8,128)(2,1)S(1)}, bf16[64,640]{1,0:T(8,128)(2,1)S(1)}, u32[]{:S(2)}, u32[]{:S(2)}) collective-permute-start(bf16[64,640]{1,0:T(8,128)(2,1)S(1)} %get-tuple-element.73), channel_id=1, source_target_pairs={{0,0},{2,34},{4,4},{6,38},{8,8},{10,42},{12,12},{14,46},{16,16},{1... | collective-permute-start | bytes 245768 | tf_op jit(solution)/shard_map/ppermute | solution.py:65
  75.6 2.3 %collective-permute-start.14 = (bf16[64,640]{1,0:T(8,128)(2,1)S(1)}, bf16[64,640]{1,0:T(8,128)(2,1)S(1)}, u32[]{:S(2)}, u32[]{:S(2)}) collective-permute-start(bf16[64,640]{1,0:T(8,128)(2,1)S(1)} %get-tuple-element.74), channel_id=1, source_target_pairs={{0,8},{2,42},{4,12},{6,46},{8,16},{10,50},{12,20},{14,54},{16,24},... | collective-permute-start | bytes 245768 | tf_op jit(solution)/shard_map/ppermute | solution.py:65
  77.9 2.4 %collective-permute-start.15 = (bf16[64,640]{1,0:T(8,128)(2,1)S(1)}, bf16[64,640]{1,0:T(8,128)(2,1)S(1)}, u32[]{:S(2)}, u32[]{:S(2)}) collective-permute-start(bf16[64,640]{1,0:T(8,128)(2,1)S(1)} %get-tuple-element.75), channel_id=1, source_target_pairs={{0,16},{2,50},{4,20},{6,54},{8,24},{10,58},{12,28},{14,62},{16,32}... | collective-permute-start | bytes 245768 | tf_op jit(solution)/shard_map/ppermute | solution.py:65
  80.3 0.0 collective-permute-done.17.after.two
  80.3 1.2 %collective-permute-start.16 = (bf16[64,640]{1,0:T(8,128)(2,1)S(1)}, bf16[64,640]{1,0:T(8,128)(2,1)S(1)}, u32[]{:S(2)}, u32[]{:S(2)}) collective-permute-start(bf16[64,640]{1,0:T(8,128)(2,1)S(1)} %get-tuple-element.76), channel_id=1, source_target_pairs={{0,24},{2,58},{4,28},{6,62},{8,32},{10,2},{12,36},{14,6},{16,40},{... | collective-permute-start | bytes 245768 | tf_op jit(solution)/shard_map/ppermute | solution.py:65
  81.5 0.3 collective-permute-start.21
  81.8 0.0 collective-permute-done.14.b_ref
  81.8 4.5 %collective-permute-start.20 = (bf16[2,80,640]{2,1,0:T(8,128)(2,1)S(1)}, bf16[2,80,640]{2,1,0:T(8,128)(2,1)S(1)}, u32[]{:S(2)}, u32[]{:S(2)}) collective-permute-start(bf16[2,80,640]{2,1,0:T(8,128)(2,1)S(1)} %get-tuple-element.81.own), channel_id=1, source_target_pairs={{0,56},{8,0},{16,8},{24,16},{32,24},{40,32},{48,40},{56,48},{64,12... | collective-permute-start | bytes 614408 | tf_op jit(solution)/shard_map/ppermute | solution.py:85
  86.3 0.6 shard_map.131
  86.9 0.1 collective-permute-start.18
  87.0 1.3 %collective-permute-done.18.came_ref = bf16[64,640]{1,0:T(8,128)(2,1)S(1)} collective-permute-done((bf16[64,640]{1,0:T(8,128)(2,1)S(1)}, bf16[64,640]{1,0:T(8,128)(2,1)S(1)}, u32[]{:S(2)}, u32[]{:S(2)}) %collective-permute-start.18) | collective-permute-done | bytes 81952 | tf_op jit(solution)/shard_map/ppermute | solution.py:48
  88.3 0.6 shard_map.132
  88.8 3.4 %collective-permute-start.19 = (bf16[64,640]{1,0:T(8,128)(2,1)S(1)}, bf16[64,640]{1,0:T(8,128)(2,1)S(1)}, u32[]{:S(2)}, u32[]{:S(2)}) collective-permute-start(bf16[64,640]{1,0:T(8,128)(2,1)S(1)} %get-tuple-element.80), channel_id=1, source_target_pairs={{0,4},{2,6},{4,0},{6,2},{1,5},{3,7},{5,1},{7,3},{8,12},{10,14},{12... | collective-permute-start | bytes 245768 | tf_op jit(solution)/shard_map/ppermute | solution.py:48
  92.2 0.0 collective-permute-done.10.far_ref
  92.2 1.6 %shard_map.129.after = bf16[2,256,640]{2,1,0:T(8,128)(2,1)} custom-call(s32[5]{0:T(128)S(1)} %stack.27.pos, bf16[256,640]{1,0:T(8,128)(2,1)S(1)} %get-tuple-element.50.after.first_ref, bf16[256,640]{1,0:T(8,128)(2,1)S(1)} %get-tuple-element.59.g_ref, f32[640,256]{1,0:T(8,128)S(1)} %get-tuple-element.69.near_ref, ...), custom_call_target="tpu_custom_call" | custom-call | flops 1 | bytes 1 | tf_op jit(solution)/shard_map/pallas_call | solution.py:120
  93.9 0.6 shard_map.133.w_ref
  94.5 0.2 collective-permute-done.19.far_ref
  94.7 0.9 shard_map.134
  95.7 0.1 collective-permute-start.22
  95.8 2.0 %collective-permute-start.23 = (bf16[16,640]{1,0:T(8,128)(2,1)S(1)}, bf16[16,640]{1,0:T(8,128)(2,1)S(1)}, u32[]{:S(2)}, u32[]{:S(2)}) collective-permute-start(bf16[16,640]{1,0:T(8,128)(2,1)S(1)} %get-tuple-element.84), channel_id=1, source_target_pairs={{0,128},{8,136},{16,144},{24,152},{32,160},{40,168},{48,176},{56,1... | collective-permute-start | bytes 61448 | tf_op jit(solution)/shard_map/ppermute | solution.py:55
  97.8 0.6 collective-permute-start.24
  98.4 1.2 %collective-permute-done.22 = bf16[16,640]{1,0:T(8,128)(2,1)S(1)} collective-permute-done((bf16[16,640]{1,0:T(8,128)(2,1)S(1)}, bf16[16,640]{1,0:T(8,128)(2,1)S(1)}, u32[]{:S(2)}, u32[]{:S(2)}) %collective-permute-start.22) | collective-permute-done | bytes 20512 | tf_op jit(solution)/shard_map/ppermute | solution.py:55
  99.6 0.4 collective-permute-done.23
  100.0 0.8 collective-permute-done.24
  100.8 0.7 fusion.3
  (14 shorter events, 0.0 us)
Async XLA Ops:
  6.3 7.0 %copy-start.1 = (bf16[80,640]{1,0:T(8,128)(2,1)S(1)}, bf16[80,640]{1,0:T(8,128)(2,1)}, u32[]{:S(2)}) copy-start(bf16[80,640]{1,0:T(8,128)(2,1)} %param.18) | copy-start | bytes 307204
  6.3 5.1 %collective-permute-start = (bf16[2,640,256]{2,1,0:T(8,128)(2,1)S(1)}, bf16[2,640,256]{2,1,0:T(8,128)(2,1)S(1)}, u32[]{:S(2)}, u32[]{:S(2)}) collective-permute-start(bf16[2,640,256]{2,1,0:T(8,128)(2,1)S(1)} %shard_map.114.rest_0_), channel_id=1, source_target_pairs={{0,2},{2,0},{4,6},{6,4},{1,3},{3,1},{5,7},{7,5},{8,10},{10,8},{12,... | collective-permute-start | bytes 1966088 | tf_op jit(solution)/shard_map/ppermute | solution.py:48
  12.0 10.7 %collective-permute-start.1 = (bf16[640,256]{1,0:T(8,128)(2,1)S(1)}, bf16[640,256]{1,0:T(8,128)(2,1)S(1)}, u32[]{:S(2)}, u32[]{:S(2)}) collective-permute-start(bf16[640,256]{1,0:T(8,128)(2,1)S(1)} %get-tuple-element.48.after), channel_id=1, source_target_pairs={{0,4},{2,6},{4,0},{6,2},{1,5},{3,7},{5,1},{7,3},{8,12},{10,14},{12... | collective-permute-start | bytes 983048 | tf_op jit(solution)/shard_map/ppermute | solution.py:48
  13.3 9.4 %collective-permute-start.2 = (bf16[80,640]{1,0:T(8,128)(2,1)S(1)}, bf16[80,640]{1,0:T(8,128)(2,1)S(1)}, u32[]{:S(2)}, u32[]{:S(2)}) collective-permute-start(bf16[80,640]{1,0:T(8,128)(2,1)S(1)} %copy-done.1), channel_id=1, source_target_pairs={{0,0},{2,64},{4,128},{6,192},{8,8},{10,72},{12,136},{14,200},{16,1... | collective-permute-start | bytes 307208 | tf_op jit(solution)/shard_map/ppermute | solution.py:75
  23.6 10.7 %collective-permute-start.3 = (bf16[256,640]{1,0:T(8,128)(2,1)S(1)}, bf16[256,640]{1,0:T(8,128)(2,1)S(1)}, u32[]{:S(2)}, u32[]{:S(2)}) collective-permute-start(bf16[256,640]{1,0:T(8,128)(2,1)S(1)} %get-tuple-element.50.after.first_ref), channel_id=1, source_target_pairs={{8,0},{16,8},{24,16},{32,24},{40,32},{48,40},{56,48},{64,56},{72,6... | collective-permute-start | bytes 983048 | tf_op jit(solution)/shard_map/ppermute | solution.py:89
  26.6 10.7 %collective-permute-start.4 = (bf16[80,640]{1,0:T(8,128)(2,1)S(1)}, bf16[80,640]{1,0:T(8,128)(2,1)S(1)}, u32[]{:S(2)}, u32[]{:S(2)}) collective-permute-start(bf16[80,640]{1,0:T(8,128)(2,1)S(1)} %get-tuple-element.63.text_a), channel_id=1, source_target_pairs={{0,32},{8,40},{16,48},{24,56},{32,0},{40,8},{48,16},{56,24},{64,96... | collective-permute-start | bytes 307208 | tf_op jit(solution)/shard_map/ppermute | solution.py:80
  38.4 4.5 %collective-permute-start.5 = (bf16[1,640,256]{2,1,0:T(8,128)(2,1)S(1)}, bf16[1,640,256]{2,1,0:T(8,128)(2,1)S(1)}, u32[]{:S(2)}, u32[]{:S(2)}) collective-permute-start(bf16[1,640,256]{2,1,0:T(8,128)(2,1)S(1)} %shard_map.121.rest_0_), channel_id=1, source_target_pairs={{0,2},{2,0},{4,6},{6,4},{1,3},{3,1},{5,7},{7,5},{8,10},{10,8},{12,... | collective-permute-start | bytes 983048 | tf_op jit(solution)/shard_map/ppermute | solution.py:48
  42.9 16.3 %collective-permute-start.6 = (bf16[3,640,256]{2,1,0:T(8,128)(2,1)S(1)}, bf16[3,640,256]{2,1,0:T(8,128)(2,1)S(1)}, u32[]{:S(2)}, u32[]{:S(2)}) collective-permute-start(bf16[3,640,256]{2,1,0:T(8,128)(2,1)S(1)} %shard_map.122.after), channel_id=1, source_target_pairs={{0,2},{2,0},{4,6},{6,4},{1,3},{3,1},{5,7},{7,5},{8,10},{10,8},{12,... | collective-permute-start | bytes 2949128 | tf_op jit(solution)/shard_map/ppermute | solution.py:48
  44.1 13.2 %collective-permute-start.8 = (bf16[320,256]{1,0:T(8,128)(2,1)S(1)}, bf16[320,256]{1,0:T(8,128)(2,1)S(1)}, u32[]{:S(2)}, u32[]{:S(2)}) collective-permute-start(bf16[320,256]{1,0:T(8,128)(2,1)S(1)} %get-tuple-element.66), channel_id=1, source_target_pairs={{0,192},{8,200},{16,208},{24,216},{32,224},{40,232},{48,240},{56,2... | collective-permute-start | bytes 491528 | tf_op jit(solution)/shard_map/ppermute | solution.py:55
  53.0 6.2 %collective-permute-start.7 = (bf16[320,256]{1,0:T(8,128)(2,1)S(1)}, bf16[320,256]{1,0:T(8,128)(2,1)S(1)}, u32[]{:S(2)}, u32[]{:S(2)}) collective-permute-start(bf16[320,256]{1,0:T(8,128)(2,1)S(1)} %get-tuple-element.64.rest_0_), channel_id=1, source_target_pairs={{0,64},{8,72},{16,80},{24,88},{32,96},{40,104},{48,112},{56,120},{... | collective-permute-start | bytes 491528 | tf_op jit(solution)/shard_map/ppermute | solution.py:55
  56.5 6.2 %collective-permute-start.9 = (bf16[2,640,256]{2,1,0:T(8,128)(2,1)S(1)}, bf16[2,640,256]{2,1,0:T(8,128)(2,1)S(1)}, u32[]{:S(2)}, u32[]{:S(2)}) collective-permute-start(bf16[2,640,256]{2,1,0:T(8,128)(2,1)S(1)} %get-tuple-element.67.after), channel_id=1, source_target_pairs={{0,2},{2,0},{4,6},{6,4},{1,3},{3,1},{5,7},{7,5},{8,10},{10,8},{12,... | collective-permute-start | bytes 1966088 | tf_op jit(solution)/shard_map/ppermute | solution.py:48
  59.9 7.8 %collective-permute-start.12 = (bf16[640,256]{1,0:T(8,128)(2,1)S(1)}, bf16[640,256]{1,0:T(8,128)(2,1)S(1)}, u32[]{:S(2)}, u32[]{:S(2)}) collective-permute-start(bf16[640,256]{1,0:T(8,128)(2,1)S(1)} %get-tuple-element.71), channel_id=1, source_target_pairs={{0,192},{8,200},{16,208},{24,216},{32,224},{40,232},{48,240},{56,2... | collective-permute-start | bytes 983048 | tf_op jit(solution)/shard_map/ppermute | solution.py:55
  61.1 9.7 %collective-permute-start.11 = (bf16[640,256]{1,0:T(8,128)(2,1)S(1)}, bf16[640,256]{1,0:T(8,128)(2,1)S(1)}, u32[]{:S(2)}, u32[]{:S(2)}) collective-permute-start(bf16[640,256]{1,0:T(8,128)(2,1)S(1)} %get-tuple-element.68.rest_0_), channel_id=1, source_target_pairs={{0,64},{8,72},{16,80},{24,88},{32,96},{40,104},{48,112},{56,120},{... | collective-permute-start | bytes 983048 | tf_op jit(solution)/shard_map/ppermute | solution.py:55
  61.4 18.9 %collective-permute-start.17 = (bf16[2,80,640]{2,1,0:T(8,128)(2,1)S(1)}, bf16[2,80,640]{2,1,0:T(8,128)(2,1)S(1)}, u32[]{:S(2)}, u32[]{:S(2)}) collective-permute-start(bf16[2,80,640]{2,1,0:T(8,128)(2,1)S(1)} %get-tuple-element.72.text), channel_id=1, source_target_pairs={{0,16},{8,24},{16,0},{24,8},{32,48},{40,56},{48,32},{56,40},{64,80... | collective-permute-start | bytes 614408 | tf_op jit(solution)/shard_map/ppermute | solution.py:80
  63.4 28.9 %collective-permute-start.10 = (bf16[640,256]{1,0:T(8,128)(2,1)S(1)}, bf16[640,256]{1,0:T(8,128)(2,1)S(1)}, u32[]{:S(2)}, u32[]{:S(2)}) collective-permute-start(bf16[640,256]{1,0:T(8,128)(2,1)S(1)} %get-tuple-element.70), channel_id=1, source_target_pairs={{0,4},{2,6},{4,0},{6,2},{1,5},{3,7},{5,1},{7,3},{8,12},{10,14},{12... | collective-permute-start | bytes 983048 | tf_op jit(solution)/shard_map/ppermute | solution.py:48
  71.7 9.9 %collective-permute-start.13 = (bf16[64,640]{1,0:T(8,128)(2,1)S(1)}, bf16[64,640]{1,0:T(8,128)(2,1)S(1)}, u32[]{:S(2)}, u32[]{:S(2)}) collective-permute-start(bf16[64,640]{1,0:T(8,128)(2,1)S(1)} %get-tuple-element.73), channel_id=1, source_target_pairs={{0,0},{2,34},{4,4},{6,38},{8,8},{10,42},{12,12},{14,46},{16,16},{1... | collective-permute-start | bytes 245768 | tf_op jit(solution)/shard_map/ppermute | solution.py:65
  75.6 6.2 %collective-permute-start.14 = (bf16[64,640]{1,0:T(8,128)(2,1)S(1)}, bf16[64,640]{1,0:T(8,128)(2,1)S(1)}, u32[]{:S(2)}, u32[]{:S(2)}) collective-permute-start(bf16[64,640]{1,0:T(8,128)(2,1)S(1)} %get-tuple-element.74), channel_id=1, source_target_pairs={{0,8},{2,42},{4,12},{6,46},{8,16},{10,50},{12,20},{14,54},{16,24},... | collective-permute-start | bytes 245768 | tf_op jit(solution)/shard_map/ppermute | solution.py:65
  77.9 8.4 %collective-permute-start.15 = (bf16[64,640]{1,0:T(8,128)(2,1)S(1)}, bf16[64,640]{1,0:T(8,128)(2,1)S(1)}, u32[]{:S(2)}, u32[]{:S(2)}) collective-permute-start(bf16[64,640]{1,0:T(8,128)(2,1)S(1)} %get-tuple-element.75), channel_id=1, source_target_pairs={{0,16},{2,50},{4,20},{6,54},{8,24},{10,58},{12,28},{14,62},{16,32}... | collective-permute-start | bytes 245768 | tf_op jit(solution)/shard_map/ppermute | solution.py:65
  80.3 6.0 %collective-permute-start.16 = (bf16[64,640]{1,0:T(8,128)(2,1)S(1)}, bf16[64,640]{1,0:T(8,128)(2,1)S(1)}, u32[]{:S(2)}, u32[]{:S(2)}) collective-permute-start(bf16[64,640]{1,0:T(8,128)(2,1)S(1)} %get-tuple-element.76), channel_id=1, source_target_pairs={{0,24},{2,58},{4,28},{6,62},{8,32},{10,2},{12,36},{14,6},{16,40},{... | collective-permute-start | bytes 245768 | tf_op jit(solution)/shard_map/ppermute | solution.py:65
  81.5 12.3 %collective-permute-start.21 = (bf16[2,80,640]{2,1,0:T(8,128)(2,1)S(1)}, bf16[2,80,640]{2,1,0:T(8,128)(2,1)S(1)}, u32[]{:S(2)}, u32[]{:S(2)}) collective-permute-start(bf16[2,80,640]{2,1,0:T(8,128)(2,1)S(1)} %get-tuple-element.81.own), channel_id=1, source_target_pairs={{0,8},{8,16},{16,24},{24,32},{32,40},{40,48},{48,56},{56,0},{64,72... | collective-permute-start | bytes 614408 | tf_op jit(solution)/shard_map/ppermute | solution.py:85
  81.8 12.1 %collective-permute-start.20 = (bf16[2,80,640]{2,1,0:T(8,128)(2,1)S(1)}, bf16[2,80,640]{2,1,0:T(8,128)(2,1)S(1)}, u32[]{:S(2)}, u32[]{:S(2)}) collective-permute-start(bf16[2,80,640]{2,1,0:T(8,128)(2,1)S(1)} %get-tuple-element.81.own), channel_id=1, source_target_pairs={{0,56},{8,0},{16,8},{24,16},{32,24},{40,32},{48,40},{56,48},{64,12... | collective-permute-start | bytes 614408 | tf_op jit(solution)/shard_map/ppermute | solution.py:85
  86.9 1.4 %collective-permute-start.18 = (bf16[64,640]{1,0:T(8,128)(2,1)S(1)}, bf16[64,640]{1,0:T(8,128)(2,1)S(1)}, u32[]{:S(2)}, u32[]{:S(2)}) collective-permute-start(bf16[64,640]{1,0:T(8,128)(2,1)S(1)} %get-tuple-element.78), channel_id=1, source_target_pairs={{0,2},{2,0},{4,6},{6,4},{1,3},{3,1},{5,7},{7,5},{8,10},{10,8},{12,... | collective-permute-start | bytes 245768 | tf_op jit(solution)/shard_map/ppermute | solution.py:48
  88.8 5.9 %collective-permute-start.19 = (bf16[64,640]{1,0:T(8,128)(2,1)S(1)}, bf16[64,640]{1,0:T(8,128)(2,1)S(1)}, u32[]{:S(2)}, u32[]{:S(2)}) collective-permute-start(bf16[64,640]{1,0:T(8,128)(2,1)S(1)} %get-tuple-element.80), channel_id=1, source_target_pairs={{0,4},{2,6},{4,0},{6,2},{1,5},{3,7},{5,1},{7,3},{8,12},{10,14},{12... | collective-permute-start | bytes 245768 | tf_op jit(solution)/shard_map/ppermute | solution.py:48
  92.2 8.5 %copy-start = (bf16[640,16]{0,1:T(8,128)(2,1)S(1)}, bf16[640,16]{0,1:T(8,128)(2,1)}, u32[]{:S(2)}) copy-start(bf16[640,16]{0,1:T(8,128)(2,1)} %param.19) | copy-start | bytes 61444
  95.7 3.9 %collective-permute-start.22 = (bf16[16,640]{1,0:T(8,128)(2,1)S(1)}, bf16[16,640]{1,0:T(8,128)(2,1)S(1)}, u32[]{:S(2)}, u32[]{:S(2)}) collective-permute-start(bf16[16,640]{1,0:T(8,128)(2,1)S(1)} %get-tuple-element.83), channel_id=1, source_target_pairs={{0,64},{8,72},{16,80},{24,88},{32,96},{40,104},{48,112},{56,120},{... | collective-permute-start | bytes 61448 | tf_op jit(solution)/shard_map/ppermute | solution.py:55
  95.8 4.2 %collective-permute-start.23 = (bf16[16,640]{1,0:T(8,128)(2,1)S(1)}, bf16[16,640]{1,0:T(8,128)(2,1)S(1)}, u32[]{:S(2)}, u32[]{:S(2)}) collective-permute-start(bf16[16,640]{1,0:T(8,128)(2,1)S(1)} %get-tuple-element.84), channel_id=1, source_target_pairs={{0,128},{8,136},{16,144},{24,152},{32,160},{40,168},{48,176},{56,1... | collective-permute-start | bytes 61448 | tf_op jit(solution)/shard_map/ppermute | solution.py:55
  97.8 2.9 %collective-permute-start.24 = (bf16[16,640]{1,0:T(8,128)(2,1)S(1)}, bf16[16,640]{1,0:T(8,128)(2,1)S(1)}, u32[]{:S(2)}, u32[]{:S(2)}) collective-permute-start(bf16[16,640]{1,0:T(8,128)(2,1)S(1)} %get-tuple-element.85), channel_id=1, source_target_pairs={{0,192},{8,200},{16,208},{24,216},{32,224},{40,232},{48,240},{56,2... | collective-permute-start | bytes 61448 | tf_op jit(solution)/shard_map/ppermute | solution.py:55

commit v5 on v4

--- a/solution.py
+++ b/solution.py
@@ -240,8 +240,13 @@
         low_ref[i] = attention.astype(BF16)
 
 
+def mix_kernel(pos, p_low_ref, v_ref, mixed_ref):
+    for i, h in enumerate(heads_of(v_ref.shape[-1])):
+        mixed_ref[h, :] = dot(v_ref[:, h], p_low_ref[i], TN)
+
+
 def second_kernel(
-    pos, q_ref, v_ref, came_ref, top_ref, dk_ref, dv_ref, p_ref, p_low_ref, *rest
+    pos, q_ref, v_ref, came_ref, top_ref, dk_ref, dv_ref, p_ref, p_low_ref, mixed_ref, *rest
 ):
     *waited, g_ref, ds_ref, low_ref = rest
     width = q_ref.shape[-1]
@@ -251,7 +256,7 @@
     for i, h in enumerate(heads_of(width)):
         g = g_ref[:, h]
         attention_grad = dot(v_ref[:, h], g, NT)
-        row_dot = jnp.sum(p_ref[i] * attention_grad, axis=0, keepdims=True)
+        row_dot = jnp.sum(mixed_ref[h, :] * g.astype(F32).T, axis=0, keepdims=True)
         score_grad = (p_ref[i] * (attention_grad - row_dot)).astype(BF16)
         ds_ref[i] = score_grad
         dk = dk_ref[:, h] + dot(score_grad, q_ref[:, h], NN) * HEAD ** (-0.5)
@@ -444,14 +449,15 @@
     came_back = pass_back(sent0)
     p1, p1_low, text_one = call(
         ahead_kernel,
-        [where, (q1, VMEM), (k, VMEM), (text_one, VMEM), (sent0, ANY)],
+        [where] + [(a, VMEM) for a in (q1, k, text_one)] + [(sent0, ANY)],
         [((heads, text, rows), F32), ((heads, text, rows), BF16), (block, BF16)],
     )
     text_across = swap_z(text_one, 4)
+    (mixed,) = call(mix_kernel, [where, (p1_low, VMEM), (v, VMEM)], [((width, rows), F32)])
 
     g1, ds1, low = call(
         second_kernel,
-        [where] + [(a, VMEM) for a in (q1, v, came_back, top, dk0, dv0, p1, p1_low)],
+        [where] + [(a, VMEM) for a in (q1, v, came_back, top, dk0, dv0, p1, p1_low, mixed)],
         [act, ((heads, text, rows), BF16), ((text, 2 * width), BF16)],
     )
 

time: 103 us -> 104 us (level)
  starting transfers between devices: 53.8 us -> 58.7 us
  waiting for transfers between devices: 11.6 us -> 8.35 us
    ppermute x7, waiting for transfers between devices: 9.53 us -> 3.24 us  [send_x(): return lax.ppermute(value, 'section', pairs)]
    ppermute x4, starting transfers between devices: 9.84 us -> 13.8 us  [send_z(): return lax.ppermute(value, ('section', 'tensor'), pairs)]
    ppermute x4, waiting for transfers between devices: 0.01 us -> 2.02 us  [send_z(): return lax.ppermute(value, ('section', 'tensor'), pairs)]
    ppermute x8, waiting for transfers between devices: 2.02 us -> 3.08 us  [swap_tensor(): return lax.ppermute(value, 'tensor', [(i, i ^ bit) for i in range(TENSOR)])]
    pallas_call x22 -> x23, Pallas kernels: 34.4 us -> 34.4 us  [call(): pl.pallas_call(body, in_specs=[spec for array, spec in ins], out_specs=[p...]
  transfers between devices with their start and end apart: 25 -> 25, of which waited for: 9 -> 8; matrix products, arithmetic and copies ran while one was open for 0% -> 0% of each run, Pallas kernels for 25% -> 24%
where the time goes in v5:
time: 104 us; the launch traced here: 103 us
  starting transfers between devices  58.7 us (56%)
  Pallas kernels  34.4 us (33%)
  waiting for transfers between devices  8.35 us (8%)
    pallas_call x23, Pallas kernels, call(): pl.pallas_call(body, in_specs=[spec for array, spec in ins], out_specs=[p...  34.4 us
    ppermute x8, starting transfers between devices, swap_tensor(): return lax.ppermute(value, 'tensor', [(i, i ^ bit) for i in range(TENSOR)])  13.9 us
    ppermute x4, starting transfers between devices, send_z(): return lax.ppermute(value, ('section', 'tensor'), pairs)  13.8 us
    ppermute x7, starting transfers between devices, send_x(): return lax.ppermute(value, 'section', pairs)  13.5 us
    ppermute x2, starting transfers between devices, swap_z(): return lax.ppermute(value, 'section', pairs)  7.62 us
    ppermute x2, starting transfers between devices, from_z(): return lax.ppermute(value, 'section', pairs)  4.98 us
    ppermute x1, starting transfers between devices, turn(): return lax.ppermute(value, ('section', 'tensor'), pairs)  3.65 us
    ppermute x7, waiting for transfers between devices, send_x(): return lax.ppermute(value, 'section', pairs)  3.24 us
  transfers between devices with their start and end apart: 25, of which 8 were waited for; matrix products, arithmetic and copies ran while one was open for 0% of the time, Pallas kernels for 24%

profile of v5, /device:TPU:1, one launch (start us, length us, event | category | flops | bytes accessed | tf_op | source)
XLA Modules:
  0.0 103.2 jit_solution(17737559411043712862)
XLA Ops:
  0.7 0.1 stack.27.pos
  0.8 4.3 %shard_map.113 = (bf16[640,256]{1,0:T(8,128)(2,1)S(1)}, bf16[2560,640]{1,0:T(8,128)(2,1)S(1)}, bf16[256,640]{1,0:T(8,128)(2,1)S(1)}) custom-call(s32[5]{0:T(128)S(1)} %stack.27.pos, bf16[1,2,256,640]{3,2,1,0:T(8,128)(2,1)} %q_hbm.3, bf16[1,512,640]{2,1,0:T(8,128)(2,1)} %k_hbm.3, bf16[1,512,640]{2,1,0:T(8,128)(2,1)} %v_hbm.3, bf16[1,256,640]{2,1,0:T(8,128)(2,1)} %g_hbm.3, ...), custom_call_target="tpu_custom_call" | custom-call | flops 1 | bytes 1 | tf_op jit(solution)/shard_map/pallas_call | solution.py:120
  5.1 1.2 %shard_map.114.rest_0_ = bf16[2,640,256]{2,1,0:T(8,128)(2,1)S(1)} custom-call(s32[5]{0:T(128)S(1)} %stack.27.pos, bf16[640,256]{1,0:T(8,128)(2,1)S(1)} %get-tuple-element.45.dq_ref, bf16[2560,640]{1,0:T(8,128)(2,1)S(1)} %get-tuple-element.46.w_ref), custom_call_target="tpu_custom_call" | custom-call | flops 1 | bytes 1 | tf_op jit(solution)/shard_map/pallas_call | solution.py:120
  6.3 0.0 copy-start.1
  6.3 3.3 %collective-permute-start = (bf16[2,640,256]{2,1,0:T(8,128)(2,1)S(1)}, bf16[2,640,256]{2,1,0:T(8,128)(2,1)S(1)}, u32[]{:S(2)}, u32[]{:S(2)}) collective-permute-start(bf16[2,640,256]{2,1,0:T(8,128)(2,1)S(1)} %shard_map.114.rest_0_), channel_id=1, source_target_pairs={{0,2},{2,0},{4,6},{6,4},{1,3},{3,1},{5,7},{7,5},{8,10},{10,8},{12,... | collective-permute-start | bytes 1966088 | tf_op jit(solution)/shard_map/ppermute | solution.py:48
  9.6 1.2 %shard_map.115.keep_ref = bf16[2,640,256]{2,1,0:T(8,128)(2,1)S(1)} custom-call(s32[5]{0:T(128)S(1)} %stack.27.pos, bf16[640,256]{1,0:T(8,128)(2,1)S(1)} %get-tuple-element.45.dq_ref, bf16[2560,640]{1,0:T(8,128)(2,1)S(1)} %get-tuple-element.46.w_ref, bf16[2,640,256]{2,1,0:T(8,128)(2,1)S(1)} %shard_map.114.rest_0_), custom_call_target="tpu_custom_call" | custom-call | flops 1 | bytes 1 | tf_op jit(solution)/shard_map/pallas_call | solution.py:120
  10.8 0.5 collective-permute-done.came_ref
  11.4 0.7 shard_map.116
  12.0 1.3 %collective-permute-start.1 = (bf16[640,256]{1,0:T(8,128)(2,1)S(1)}, bf16[640,256]{1,0:T(8,128)(2,1)S(1)}, u32[]{:S(2)}, u32[]{:S(2)}) collective-permute-start(bf16[640,256]{1,0:T(8,128)(2,1)S(1)} %get-tuple-element.48.after), channel_id=1, source_target_pairs={{0,4},{2,6},{4,0},{6,2},{1,5},{3,7},{5,1},{7,3},{8,12},{10,14},{12... | collective-permute-start | bytes 983048 | tf_op jit(solution)/shard_map/ppermute | solution.py:48
  13.3 3.6 %collective-permute-start.2 = (bf16[80,640]{1,0:T(8,128)(2,1)S(1)}, bf16[80,640]{1,0:T(8,128)(2,1)S(1)}, u32[]{:S(2)}, u32[]{:S(2)}) collective-permute-start(bf16[80,640]{1,0:T(8,128)(2,1)S(1)} %copy-done.1), channel_id=1, source_target_pairs={{0,0},{2,64},{4,128},{6,192},{8,8},{10,72},{12,136},{14,200},{16,1... | collective-permute-start | bytes 307208 | tf_op jit(solution)/shard_map/ppermute | solution.py:75
  17.0 5.8 %shard_map.117 = (f32[512,640]{1,0:T(8,128)S(1)}, f32[512,640]{1,0:T(8,128)S(1)}, bf16[256,640]{1,0:T(8,128)(2,1)S(1)}, bf16[512,640]{1,0:T(8,128)(2,1)S(1)}, bf...) custom-call(s32[5]{0:T(128)S(1)} %stack.27.pos, ...), custom_call_target="tpu_custom_call" | custom-call | flops 1 | bytes 1 | tf_op jit(solution)/shard_map/pallas_call | solution.py:120
  22.7 0.0 collective-permute-done.2.text
  22.8 0.0 collective-permute-done.1.far_ref
  22.8 0.8 shard_map.118
  23.5 1.3 %collective-permute-start.3 = (bf16[256,640]{1,0:T(8,128)(2,1)S(1)}, bf16[256,640]{1,0:T(8,128)(2,1)S(1)}, u32[]{:S(2)}, u32[]{:S(2)}) collective-permute-start(bf16[256,640]{1,0:T(8,128)(2,1)S(1)} %get-tuple-element.50.after.first_ref), channel_id=1, source_target_pairs={{8,0},{16,8},{24,16},{32,24},{40,32},{48,40},{56,48},{64,56},{72,6... | collective-permute-start | bytes 983048 | tf_op jit(solution)/shard_map/ppermute | solution.py:89
  24.8 1.7 %shard_map.119 = (f32[5,512,256]{2,1,0:T(8,128)S(1)}, bf16[5,512,256]{2,1,0:T(8,128)(2,1)S(1)}, bf16[80,640]{1,0:T(8,128)(2,1)S(1)}) custom-call(s32[5]{0:T(128)S(1)} %stack.27.pos, bf16[256,640]{1,0:T(8,128)(2,1)S(1)} %get-tuple-element.51.q_ref, bf16[512,640]{1,0:T(8,128)(2,1)S(1)} %get-tuple-element.55.k_ref, ...), custom_call_target="tpu_custom_call" | custom-call | flops 1 | bytes 1 | tf_op jit(solution)/shard_map/pallas_call | solution.py:120
  26.6 7.6 %collective-permute-start.4 = (bf16[80,640]{1,0:T(8,128)(2,1)S(1)}, bf16[80,640]{1,0:T(8,128)(2,1)S(1)}, u32[]{:S(2)}, u32[]{:S(2)}) collective-permute-start(bf16[80,640]{1,0:T(8,128)(2,1)S(1)} %get-tuple-element.63.text_a), channel_id=1, source_target_pairs={{0,32},{8,40},{16,48},{24,56},{32,0},{40,8},{48,16},{56,24},{64,96... | collective-permute-start | bytes 307208 | tf_op jit(solution)/shard_map/ppermute | solution.py:80
  34.2 0.9 shard_map.120.mixed_ref
  35.1 2.1 %shard_map.121 = (bf16[256,640]{1,0:T(8,128)(2,1)S(1)}, bf16[5,512,256]{2,1,0:T(8,128)(2,1)S(1)}, bf16[512,1280]{1,0:T(8,128)(2,1)S(1)}) custom-call(s32[5]{0:T(128)S(1)} %stack.27.pos, bf16[256,640]{1,0:T(8,128)(2,1)S(1)} %get-tuple-element.51.q_ref, bf16[512,640]{1,0:T(8,128)(2,1)S(1)} %get-tuple-element.52.v_ref, ...), custom_call_target="tpu_custom_call" | custom-call | flops 1 | bytes 1 | tf_op jit(solution)/shard_map/pallas_call | solution.py:120
  37.2 1.2 %shard_map.122.rest_0_ = bf16[1,640,256]{2,1,0:T(8,128)(2,1)S(1)} custom-call(s32[5]{0:T(128)S(1)} %stack.27.pos, bf16[512,1280]{1,0:T(8,128)(2,1)S(1)} %get-tuple-element.61.low_ref, bf16[2560,1280]{1,0:T(8,128)(2,1)S(1)} %get-tuple-element.62.w_ref, bf16[80,640]{1,0:T(8,128)(2,1)S(1)} %collective-permute-done.4.rest_0_.text_b), custom_call_target="tpu_custom_call" | custom-call | flops 1 | bytes 1 | tf_op jit(solution)/shard_map/pallas_call | solution.py:120
  38.4 2.4 %collective-permute-start.5 = (bf16[1,640,256]{2,1,0:T(8,128)(2,1)S(1)}, bf16[1,640,256]{2,1,0:T(8,128)(2,1)S(1)}, u32[]{:S(2)}, u32[]{:S(2)}) collective-permute-start(bf16[1,640,256]{2,1,0:T(8,128)(2,1)S(1)} %shard_map.122.rest_0_), channel_id=1, source_target_pairs={{0,2},{2,0},{4,6},{6,4},{1,3},{3,1},{5,7},{7,5},{8,10},{10,8},{12,... | collective-permute-start | bytes 983048 | tf_op jit(solution)/shard_map/ppermute | solution.py:48
  40.8 2.0 %shard_map.123.after = bf16[3,640,256]{2,1,0:T(8,128)(2,1)S(1)} custom-call(s32[5]{0:T(128)S(1)} %stack.27.pos, bf16[512,1280]{1,0:T(8,128)(2,1)S(1)} %get-tuple-element.61.low_ref, bf16[2560,1280]{1,0:T(8,128)(2,1)S(1)} %get-tuple-element.62.w_ref, bf16[1,640,256]{2,1,0:T(8,128)(2,1)S(1)} %shard_map.122.rest_0_), custom_call_target="tpu_custom_call" | custom-call | flops 1 | bytes 1 | tf_op jit(solution)/shard_map/pallas_call | solution.py:120
  42.8 0.1 collective-permute-start.6
  42.9 0.0 collective-permute-done.5.came_ref
  42.9 1.2 %shard_map.124 = (bf16[320,256]{1,0:T(8,128)(2,1)S(1)}, bf16[320,256]{1,0:T(8,128)(2,1)S(1)}) custom-call(s32[5]{0:T(128)S(1)} %stack.27.pos, bf16[512,1280]{1,0:T(8,128)(2,1)S(1)} %get-tuple-element.61.low_ref, bf16[2560,1280]{1,0:T(8,128)(2,1)S(1)} %get-tuple-element.62.w_ref, bf16[1,640,256]{2,1,0:T(8,128)(2,1)S(1)} %collective-permute-done.5.came_ref, ...), custom_call_target="tpu_custom_call" | custom-call | flops 1 | bytes 1 | tf_op jit(solution)/shard_map/pallas_call | solution.py:120
  44.1 7.3 %collective-permute-start.7 = (bf16[320,256]{1,0:T(8,128)(2,1)S(1)}, bf16[320,256]{1,0:T(8,128)(2,1)S(1)}, u32[]{:S(2)}, u32[]{:S(2)}) collective-permute-start(bf16[320,256]{1,0:T(8,128)(2,1)S(1)} %get-tuple-element.64.rest_0_), channel_id=1, source_target_pairs={{0,64},{8,72},{16,80},{24,88},{32,96},{40,104},{48,112},{56,120},{... | collective-permute-start | bytes 491528 | tf_op jit(solution)/shard_map/ppermute | solution.py:55
  51.4 0.7 collective-permute-start.8
  52.1 2.0 %shard_map.125.after.keep_ref = bf16[3,640,256]{2,1,0:T(8,128)(2,1)S(1)} custom-call(s32[5]{0:T(128)S(1)} %stack.27.pos, bf16[512,1280]{1,0:T(8,128)(2,1)S(1)} %get-tuple-element.61.low_ref, bf16[2560,1280]{1,0:T(8,128)(2,1)S(1)} %get-tuple-element.62.w_ref, bf16[320,256]{1,0:T(8,128)(2,1)S(1)} %get-tuple-element.64.rest_0_), custom_call_target="tpu_custom_call" | custom-call | flops 40000000000 | bytes 1 | tf_op jit(solution)/shard_map/pallas_call | solution.py:120
  54.1 1.5 %shard_map.126 = (bf16[640,256]{1,0:T(8,128)(2,1)S(1)}, bf16[2,640,256]{2,1,0:T(8,128)(2,1)S(1)}) custom-call(s32[5]{0:T(128)S(1)} %stack.27.pos, bf16[5,512,256]{2,1,0:T(8,128)(2,1)S(1)} %get-tuple-element.60.ds_ref, bf16[512,640]{1,0:T(8,128)(2,1)S(1)} %get-tuple-element.55.k_ref, bf16[2560,640]{1,0:T(8,128)(2,1)S(1)} %get-tuple-element.46.w_ref, ...), custom_call_target="tpu_custom_call" | custom-call | flops 1 | bytes 1 | tf_op jit(solution)/shard_map/pallas_call | solution.py:120
  55.6 0.9 collective-permute-start.9
  56.4 0.0 collective-permute-done.8.bottom_ref
  56.4 0.0 collective-permute-done.6.came_ref
  56.5 0.8 shard_map.127
  57.2 1.1 %collective-permute-start.11 = (bf16[640,256]{1,0:T(8,128)(2,1)S(1)}, bf16[640,256]{1,0:T(8,128)(2,1)S(1)}, u32[]{:S(2)}, u32[]{:S(2)}) collective-permute-start(bf16[640,256]{1,0:T(8,128)(2,1)S(1)} %get-tuple-element.68.rest_0_), channel_id=1, source_target_pairs={{0,64},{8,72},{16,80},{24,88},{32,96},{40,104},{48,112},{56,120},{... | collective-permute-start | bytes 983048 | tf_op jit(solution)/shard_map/ppermute | solution.py:55
  58.3 1.6 %collective-permute-start.12 = (bf16[640,256]{1,0:T(8,128)(2,1)S(1)}, bf16[640,256]{1,0:T(8,128)(2,1)S(1)}, u32[]{:S(2)}, u32[]{:S(2)}) collective-permute-start(bf16[640,256]{1,0:T(8,128)(2,1)S(1)} %get-tuple-element.71), channel_id=1, source_target_pairs={{0,192},{8,200},{16,208},{24,216},{32,224},{40,232},{48,240},{56,2... | collective-permute-start | bytes 983048 | tf_op jit(solution)/shard_map/ppermute | solution.py:55
  60.0 0.0 collective-permute-start.17
  60.0 1.2 %shard_map.128.keep_ref = bf16[2,640,256]{2,1,0:T(8,128)(2,1)S(1)} custom-call(s32[5]{0:T(128)S(1)} %stack.27.pos, bf16[640,256]{1,0:T(8,128)(2,1)S(1)} %get-tuple-element.65.dq_ref, bf16[2560,640]{1,0:T(8,128)(2,1)S(1)} %get-tuple-element.46.w_ref, bf16[640,256]{1,0:T(8,128)(2,1)S(1)} %get-tuple-element.68.rest_0_), custom_call_target="tpu_custom_call" | custom-call | flops 1 | bytes 1 | tf_op jit(solution)/shard_map/pallas_call | solution.py:120
  61.2 0.7 shard_map.129
  61.9 3.9 %collective-permute-start.10 = (bf16[640,256]{1,0:T(8,128)(2,1)S(1)}, bf16[640,256]{1,0:T(8,128)(2,1)S(1)}, u32[]{:S(2)}, u32[]{:S(2)}) collective-permute-start(bf16[640,256]{1,0:T(8,128)(2,1)S(1)} %get-tuple-element.70), channel_id=1, source_target_pairs={{0,4},{2,6},{4,0},{6,2},{1,5},{3,7},{5,1},{7,3},{8,12},{10,14},{12... | collective-permute-start | bytes 983048 | tf_op jit(solution)/shard_map/ppermute | solution.py:48
  65.8 0.3 collective-permute-done.11.b_ref
  66.2 0.9 shard_map.131
  67.0 5.4 %collective-permute-start.13 = (bf16[64,640]{1,0:T(8,128)(2,1)S(1)}, bf16[64,640]{1,0:T(8,128)(2,1)S(1)}, u32[]{:S(2)}, u32[]{:S(2)}) collective-permute-start(bf16[64,640]{1,0:T(8,128)(2,1)S(1)} %get-tuple-element.73), channel_id=1, source_target_pairs={{0,0},{2,34},{4,4},{6,38},{8,8},{10,42},{12,12},{14,46},{16,16},{1... | collective-permute-start | bytes 245768 | tf_op jit(solution)/shard_map/ppermute | solution.py:65
  72.4 4.3 %collective-permute-start.14 = (bf16[64,640]{1,0:T(8,128)(2,1)S(1)}, bf16[64,640]{1,0:T(8,128)(2,1)S(1)}, u32[]{:S(2)}, u32[]{:S(2)}) collective-permute-start(bf16[64,640]{1,0:T(8,128)(2,1)S(1)} %get-tuple-element.74), channel_id=1, source_target_pairs={{0,8},{2,42},{4,12},{6,46},{8,16},{10,50},{12,20},{14,54},{16,24},... | collective-permute-start | bytes 245768 | tf_op jit(solution)/shard_map/ppermute | solution.py:65
  76.7 4.1 %collective-permute-start.15 = (bf16[64,640]{1,0:T(8,128)(2,1)S(1)}, bf16[64,640]{1,0:T(8,128)(2,1)S(1)}, u32[]{:S(2)}, u32[]{:S(2)}) collective-permute-start(bf16[64,640]{1,0:T(8,128)(2,1)S(1)} %get-tuple-element.75), channel_id=1, source_target_pairs={{0,16},{2,50},{4,20},{6,54},{8,24},{10,58},{12,28},{14,62},{16,32}... | collective-permute-start | bytes 245768 | tf_op jit(solution)/shard_map/ppermute | solution.py:65
  80.9 0.0 collective-permute-start.16
  80.9 2.1 %collective-permute-start.20 = (bf16[2,80,640]{2,1,0:T(8,128)(2,1)S(1)}, bf16[2,80,640]{2,1,0:T(8,128)(2,1)S(1)}, u32[]{:S(2)}, u32[]{:S(2)}) collective-permute-start(bf16[2,80,640]{2,1,0:T(8,128)(2,1)S(1)} %get-tuple-element.81.own), channel_id=1, source_target_pairs={{0,56},{8,0},{16,8},{24,16},{32,24},{40,32},{48,40},{56,48},{64,12... | collective-permute-start | bytes 614408 | tf_op jit(solution)/shard_map/ppermute | solution.py:85
  83.0 2.9 %collective-permute-start.21 = (bf16[2,80,640]{2,1,0:T(8,128)(2,1)S(1)}, bf16[2,80,640]{2,1,0:T(8,128)(2,1)S(1)}, u32[]{:S(2)}, u32[]{:S(2)}) collective-permute-start(bf16[2,80,640]{2,1,0:T(8,128)(2,1)S(1)} %get-tuple-element.81.own), channel_id=1, source_target_pairs={{0,8},{8,16},{16,24},{24,32},{32,40},{40,48},{48,56},{56,0},{64,72... | collective-permute-start | bytes 614408 | tf_op jit(solution)/shard_map/ppermute | solution.py:85
  85.8 2.0 %collective-permute-done.16.d_ref = bf16[64,640]{1,0:T(8,128)(2,1)S(1)} collective-permute-done((bf16[64,640]{1,0:T(8,128)(2,1)S(1)}, bf16[64,640]{1,0:T(8,128)(2,1)S(1)}, u32[]{:S(2)}, u32[]{:S(2)}) %collective-permute-start.16) | collective-permute-done | bytes 81952 | tf_op jit(solution)/shard_map/ppermute | solution.py:65
  87.9 0.6 shard_map.132
  88.5 0.1 collective-permute-start.18
  88.6 1.3 %collective-permute-done.18.came_ref = bf16[64,640]{1,0:T(8,128)(2,1)S(1)} collective-permute-done((bf16[64,640]{1,0:T(8,128)(2,1)S(1)}, bf16[64,640]{1,0:T(8,128)(2,1)S(1)}, u32[]{:S(2)}, u32[]{:S(2)}) %collective-permute-start.18) | collective-permute-done | bytes 81952 | tf_op jit(solution)/shard_map/ppermute | solution.py:48
  89.8 0.6 shard_map.133
  90.4 1.9 %collective-permute-start.19 = (bf16[64,640]{1,0:T(8,128)(2,1)S(1)}, bf16[64,640]{1,0:T(8,128)(2,1)S(1)}, u32[]{:S(2)}, u32[]{:S(2)}) collective-permute-start(bf16[64,640]{1,0:T(8,128)(2,1)S(1)} %get-tuple-element.80), channel_id=1, source_target_pairs={{0,4},{2,6},{4,0},{6,2},{1,5},{3,7},{5,1},{7,3},{8,12},{10,14},{12... | collective-permute-start | bytes 245768 | tf_op jit(solution)/shard_map/ppermute | solution.py:48
  92.3 1.6 %shard_map.130.after = bf16[2,256,640]{2,1,0:T(8,128)(2,1)} custom-call(s32[5]{0:T(128)S(1)} %stack.27.pos, bf16[256,640]{1,0:T(8,128)(2,1)S(1)} %get-tuple-element.50.after.first_ref, bf16[256,640]{1,0:T(8,128)(2,1)S(1)} %get-tuple-element.59.g_ref, f32[640,256]{1,0:T(8,128)S(1)} %get-tuple-element.69.near_ref, ...), custom_call_target="tpu_custom_call" | custom-call | flops 1 | bytes 1 | tf_op jit(solution)/shard_map/pallas_call | solution.py:120
  94.0 0.6 shard_map.134.w_ref
  94.6 1.3 %collective-permute-done.19.far_ref = bf16[64,640]{1,0:T(8,128)(2,1)S(1)} collective-permute-done((bf16[64,640]{1,0:T(8,128)(2,1)S(1)}, bf16[64,640]{1,0:T(8,128)(2,1)S(1)}, u32[]{:S(2)}, u32[]{:S(2)}) %collective-permute-start.19) | collective-permute-done | bytes 81952 | tf_op jit(solution)/shard_map/ppermute | solution.py:48
  95.9 0.9 shard_map.135
  96.8 0.1 collective-permute-start.22
  96.9 2.6 %collective-permute-start.23 = (bf16[16,640]{1,0:T(8,128)(2,1)S(1)}, bf16[16,640]{1,0:T(8,128)(2,1)S(1)}, u32[]{:S(2)}, u32[]{:S(2)}) collective-permute-start(bf16[16,640]{1,0:T(8,128)(2,1)S(1)} %get-tuple-element.84), channel_id=1, source_target_pairs={{0,128},{8,136},{16,144},{24,152},{32,160},{40,168},{48,176},{56,1... | collective-permute-start | bytes 61448 | tf_op jit(solution)/shard_map/ppermute | solution.py:55
  99.6 0.0 collective-permute-start.24
  99.6 1.2 %collective-permute-done.22 = bf16[16,640]{1,0:T(8,128)(2,1)S(1)} collective-permute-done((bf16[16,640]{1,0:T(8,128)(2,1)S(1)}, bf16[16,640]{1,0:T(8,128)(2,1)S(1)}, u32[]{:S(2)}, u32[]{:S(2)}) %collective-permute-start.22) | collective-permute-done | bytes 20512 | tf_op jit(solution)/shard_map/ppermute | solution.py:55
  100.8 0.4 collective-permute-done.23
  101.1 1.3 %collective-permute-done.24 = bf16[16,640]{1,0:T(8,128)(2,1)S(1)} collective-permute-done((bf16[16,640]{1,0:T(8,128)(2,1)S(1)}, bf16[16,640]{1,0:T(8,128)(2,1)S(1)}, u32[]{:S(2)}, u32[]{:S(2)}) %collective-permute-start.24) | collective-permute-done | bytes 20512 | tf_op jit(solution)/shard_map/ppermute | solution.py:55
  102.5 0.7 fusion.3
  (15 shorter events, 0.0 us)
Async XLA Ops:
  6.3 7.0 %copy-start.1 = (bf16[80,640]{1,0:T(8,128)(2,1)S(1)}, bf16[80,640]{1,0:T(8,128)(2,1)}, u32[]{:S(2)}) copy-start(bf16[80,640]{1,0:T(8,128)(2,1)} %param.18) | copy-start | bytes 307204
  6.3 5.1 %collective-permute-start = (bf16[2,640,256]{2,1,0:T(8,128)(2,1)S(1)}, bf16[2,640,256]{2,1,0:T(8,128)(2,1)S(1)}, u32[]{:S(2)}, u32[]{:S(2)}) collective-permute-start(bf16[2,640,256]{2,1,0:T(8,128)(2,1)S(1)} %shard_map.114.rest_0_), channel_id=1, source_target_pairs={{0,2},{2,0},{4,6},{6,4},{1,3},{3,1},{5,7},{7,5},{8,10},{10,8},{12,... | collective-permute-start | bytes 1966088 | tf_op jit(solution)/shard_map/ppermute | solution.py:48
  12.0 10.7 %collective-permute-start.1 = (bf16[640,256]{1,0:T(8,128)(2,1)S(1)}, bf16[640,256]{1,0:T(8,128)(2,1)S(1)}, u32[]{:S(2)}, u32[]{:S(2)}) collective-permute-start(bf16[640,256]{1,0:T(8,128)(2,1)S(1)} %get-tuple-element.48.after), channel_id=1, source_target_pairs={{0,4},{2,6},{4,0},{6,2},{1,5},{3,7},{5,1},{7,3},{8,12},{10,14},{12... | collective-permute-start | bytes 983048 | tf_op jit(solution)/shard_map/ppermute | solution.py:48
  13.3 9.4 %collective-permute-start.2 = (bf16[80,640]{1,0:T(8,128)(2,1)S(1)}, bf16[80,640]{1,0:T(8,128)(2,1)S(1)}, u32[]{:S(2)}, u32[]{:S(2)}) collective-permute-start(bf16[80,640]{1,0:T(8,128)(2,1)S(1)} %copy-done.1), channel_id=1, source_target_pairs={{0,0},{2,64},{4,128},{6,192},{8,8},{10,72},{12,136},{14,200},{16,1... | collective-permute-start | bytes 307208 | tf_op jit(solution)/shard_map/ppermute | solution.py:75
  23.5 11.6 %collective-permute-start.3 = (bf16[256,640]{1,0:T(8,128)(2,1)S(1)}, bf16[256,640]{1,0:T(8,128)(2,1)S(1)}, u32[]{:S(2)}, u32[]{:S(2)}) collective-permute-start(bf16[256,640]{1,0:T(8,128)(2,1)S(1)} %get-tuple-element.50.after.first_ref), channel_id=1, source_target_pairs={{8,0},{16,8},{24,16},{32,24},{40,32},{48,40},{56,48},{64,56},{72,6... | collective-permute-start | bytes 983048 | tf_op jit(solution)/shard_map/ppermute | solution.py:89
  26.6 10.6 %collective-permute-start.4 = (bf16[80,640]{1,0:T(8,128)(2,1)S(1)}, bf16[80,640]{1,0:T(8,128)(2,1)S(1)}, u32[]{:S(2)}, u32[]{:S(2)}) collective-permute-start(bf16[80,640]{1,0:T(8,128)(2,1)S(1)} %get-tuple-element.63.text_a), channel_id=1, source_target_pairs={{0,32},{8,40},{16,48},{24,56},{32,0},{40,8},{48,16},{56,24},{64,96... | collective-permute-start | bytes 307208 | tf_op jit(solution)/shard_map/ppermute | solution.py:80
  38.4 4.5 %collective-permute-start.5 = (bf16[1,640,256]{2,1,0:T(8,128)(2,1)S(1)}, bf16[1,640,256]{2,1,0:T(8,128)(2,1)S(1)}, u32[]{:S(2)}, u32[]{:S(2)}) collective-permute-start(bf16[1,640,256]{2,1,0:T(8,128)(2,1)S(1)} %shard_map.122.rest_0_), channel_id=1, source_target_pairs={{0,2},{2,0},{4,6},{6,4},{1,3},{3,1},{5,7},{7,5},{8,10},{10,8},{12,... | collective-permute-start | bytes 983048 | tf_op jit(solution)/shard_map/ppermute | solution.py:48
  42.8 13.6 %collective-permute-start.6 = (bf16[3,640,256]{2,1,0:T(8,128)(2,1)S(1)}, bf16[3,640,256]{2,1,0:T(8,128)(2,1)S(1)}, u32[]{:S(2)}, u32[]{:S(2)}) collective-permute-start(bf16[3,640,256]{2,1,0:T(8,128)(2,1)S(1)} %shard_map.123.after), channel_id=1, source_target_pairs={{0,2},{2,0},{4,6},{6,4},{1,3},{3,1},{5,7},{7,5},{8,10},{10,8},{12,... | collective-permute-start | bytes 2949128 | tf_op jit(solution)/shard_map/ppermute | solution.py:48
  44.1 12.3 %collective-permute-start.7 = (bf16[320,256]{1,0:T(8,128)(2,1)S(1)}, bf16[320,256]{1,0:T(8,128)(2,1)S(1)}, u32[]{:S(2)}, u32[]{:S(2)}) collective-permute-start(bf16[320,256]{1,0:T(8,128)(2,1)S(1)} %get-tuple-element.64.rest_0_), channel_id=1, source_target_pairs={{0,64},{8,72},{16,80},{24,88},{32,96},{40,104},{48,112},{56,120},{... | collective-permute-start | bytes 491528 | tf_op jit(solution)/shard_map/ppermute | solution.py:55
  51.4 5.1 %collective-permute-start.8 = (bf16[320,256]{1,0:T(8,128)(2,1)S(1)}, bf16[320,256]{1,0:T(8,128)(2,1)S(1)}, u32[]{:S(2)}, u32[]{:S(2)}) collective-permute-start(bf16[320,256]{1,0:T(8,128)(2,1)S(1)} %get-tuple-element.66), channel_id=1, source_target_pairs={{0,192},{8,200},{16,208},{24,216},{32,224},{40,232},{48,240},{56,2... | collective-permute-start | bytes 491528 | tf_op jit(solution)/shard_map/ppermute | solution.py:55
  55.6 5.6 %collective-permute-start.9 = (bf16[2,640,256]{2,1,0:T(8,128)(2,1)S(1)}, bf16[2,640,256]{2,1,0:T(8,128)(2,1)S(1)}, u32[]{:S(2)}, u32[]{:S(2)}) collective-permute-start(bf16[2,640,256]{2,1,0:T(8,128)(2,1)S(1)} %get-tuple-element.67.after), channel_id=1, source_target_pairs={{0,2},{2,0},{4,6},{6,4},{1,3},{3,1},{5,7},{7,5},{8,10},{10,8},{12,... | collective-permute-start | bytes 1966088 | tf_op jit(solution)/shard_map/ppermute | solution.py:48
  57.2 8.9 %collective-permute-start.11 = (bf16[640,256]{1,0:T(8,128)(2,1)S(1)}, bf16[640,256]{1,0:T(8,128)(2,1)S(1)}, u32[]{:S(2)}, u32[]{:S(2)}) collective-permute-start(bf16[640,256]{1,0:T(8,128)(2,1)S(1)} %get-tuple-element.68.rest_0_), channel_id=1, source_target_pairs={{0,64},{8,72},{16,80},{24,88},{32,96},{40,104},{48,112},{56,120},{... | collective-permute-start | bytes 983048 | tf_op jit(solution)/shard_map/ppermute | solution.py:55
  58.3 7.8 %collective-permute-start.12 = (bf16[640,256]{1,0:T(8,128)(2,1)S(1)}, bf16[640,256]{1,0:T(8,128)(2,1)S(1)}, u32[]{:S(2)}, u32[]{:S(2)}) collective-permute-start(bf16[640,256]{1,0:T(8,128)(2,1)S(1)} %get-tuple-element.71), channel_id=1, source_target_pairs={{0,192},{8,200},{16,208},{24,216},{32,224},{40,232},{48,240},{56,2... | collective-permute-start | bytes 983048 | tf_op jit(solution)/shard_map/ppermute | solution.py:55
  60.0 20.9 %collective-permute-start.17 = (bf16[2,80,640]{2,1,0:T(8,128)(2,1)S(1)}, bf16[2,80,640]{2,1,0:T(8,128)(2,1)S(1)}, u32[]{:S(2)}, u32[]{:S(2)}) collective-permute-start(bf16[2,80,640]{2,1,0:T(8,128)(2,1)S(1)} %get-tuple-element.72.text), channel_id=1, source_target_pairs={{0,16},{8,24},{16,0},{24,8},{32,48},{40,56},{48,32},{56,40},{64,80... | collective-permute-start | bytes 614408 | tf_op jit(solution)/shard_map/ppermute | solution.py:80
  61.9 30.4 %collective-permute-start.10 = (bf16[640,256]{1,0:T(8,128)(2,1)S(1)}, bf16[640,256]{1,0:T(8,128)(2,1)S(1)}, u32[]{:S(2)}, u32[]{:S(2)}) collective-permute-start(bf16[640,256]{1,0:T(8,128)(2,1)S(1)} %get-tuple-element.70), channel_id=1, source_target_pairs={{0,4},{2,6},{4,0},{6,2},{1,5},{3,7},{5,1},{7,3},{8,12},{10,14},{12... | collective-permute-start | bytes 983048 | tf_op jit(solution)/shard_map/ppermute | solution.py:48
  67.0 13.8 %collective-permute-start.13 = (bf16[64,640]{1,0:T(8,128)(2,1)S(1)}, bf16[64,640]{1,0:T(8,128)(2,1)S(1)}, u32[]{:S(2)}, u32[]{:S(2)}) collective-permute-start(bf16[64,640]{1,0:T(8,128)(2,1)S(1)} %get-tuple-element.73), channel_id=1, source_target_pairs={{0,0},{2,34},{4,4},{6,38},{8,8},{10,42},{12,12},{14,46},{16,16},{1... | collective-permute-start | bytes 245768 | tf_op jit(solution)/shard_map/ppermute | solution.py:65
  72.4 10.6 %collective-permute-start.14 = (bf16[64,640]{1,0:T(8,128)(2,1)S(1)}, bf16[64,640]{1,0:T(8,128)(2,1)S(1)}, u32[]{:S(2)}, u32[]{:S(2)}) collective-permute-start(bf16[64,640]{1,0:T(8,128)(2,1)S(1)} %get-tuple-element.74), channel_id=1, source_target_pairs={{0,8},{2,42},{4,12},{6,46},{8,16},{10,50},{12,20},{14,54},{16,24},... | collective-permute-start | bytes 245768 | tf_op jit(solution)/shard_map/ppermute | solution.py:65
  76.7 9.1 %collective-permute-start.15 = (bf16[64,640]{1,0:T(8,128)(2,1)S(1)}, bf16[64,640]{1,0:T(8,128)(2,1)S(1)}, u32[]{:S(2)}, u32[]{:S(2)}) collective-permute-start(bf16[64,640]{1,0:T(8,128)(2,1)S(1)} %get-tuple-element.75), channel_id=1, source_target_pairs={{0,16},{2,50},{4,20},{6,54},{8,24},{10,58},{12,28},{14,62},{16,32}... | collective-permute-start | bytes 245768 | tf_op jit(solution)/shard_map/ppermute | solution.py:65
  80.9 7.0 %collective-permute-start.16 = (bf16[64,640]{1,0:T(8,128)(2,1)S(1)}, bf16[64,640]{1,0:T(8,128)(2,1)S(1)}, u32[]{:S(2)}, u32[]{:S(2)}) collective-permute-start(bf16[64,640]{1,0:T(8,128)(2,1)S(1)} %get-tuple-element.76), channel_id=1, source_target_pairs={{0,24},{2,58},{4,28},{6,62},{8,32},{10,2},{12,36},{14,6},{16,40},{... | collective-permute-start | bytes 245768 | tf_op jit(solution)/shard_map/ppermute | solution.py:65
  80.9 13.1 %collective-permute-start.20 = (bf16[2,80,640]{2,1,0:T(8,128)(2,1)S(1)}, bf16[2,80,640]{2,1,0:T(8,128)(2,1)S(1)}, u32[]{:S(2)}, u32[]{:S(2)}) collective-permute-start(bf16[2,80,640]{2,1,0:T(8,128)(2,1)S(1)} %get-tuple-element.81.own), channel_id=1, source_target_pairs={{0,56},{8,0},{16,8},{24,16},{32,24},{40,32},{48,40},{56,48},{64,12... | collective-permute-start | bytes 614408 | tf_op jit(solution)/shard_map/ppermute | solution.py:85
  83.0 10.9 %collective-permute-start.21 = (bf16[2,80,640]{2,1,0:T(8,128)(2,1)S(1)}, bf16[2,80,640]{2,1,0:T(8,128)(2,1)S(1)}, u32[]{:S(2)}, u32[]{:S(2)}) collective-permute-start(bf16[2,80,640]{2,1,0:T(8,128)(2,1)S(1)} %get-tuple-element.81.own), channel_id=1, source_target_pairs={{0,8},{8,16},{16,24},{24,32},{32,40},{40,48},{48,56},{56,0},{64,72... | collective-permute-start | bytes 614408 | tf_op jit(solution)/shard_map/ppermute | solution.py:85
  88.5 1.4 %collective-permute-start.18 = (bf16[64,640]{1,0:T(8,128)(2,1)S(1)}, bf16[64,640]{1,0:T(8,128)(2,1)S(1)}, u32[]{:S(2)}, u32[]{:S(2)}) collective-permute-start(bf16[64,640]{1,0:T(8,128)(2,1)S(1)} %get-tuple-element.78), channel_id=1, source_target_pairs={{0,2},{2,0},{4,6},{6,4},{1,3},{3,1},{5,7},{7,5},{8,10},{10,8},{12,... | collective-permute-start | bytes 245768 | tf_op jit(solution)/shard_map/ppermute | solution.py:48
  90.4 5.5 %collective-permute-start.19 = (bf16[64,640]{1,0:T(8,128)(2,1)S(1)}, bf16[64,640]{1,0:T(8,128)(2,1)S(1)}, u32[]{:S(2)}, u32[]{:S(2)}) collective-permute-start(bf16[64,640]{1,0:T(8,128)(2,1)S(1)} %get-tuple-element.80), channel_id=1, source_target_pairs={{0,4},{2,6},{4,0},{6,2},{1,5},{3,7},{5,1},{7,3},{8,12},{10,14},{12... | collective-permute-start | bytes 245768 | tf_op jit(solution)/shard_map/ppermute | solution.py:48
  92.3 10.2 %copy-start = (bf16[640,16]{0,1:T(8,128)(2,1)S(1)}, bf16[640,16]{0,1:T(8,128)(2,1)}, u32[]{:S(2)}) copy-start(bf16[640,16]{0,1:T(8,128)(2,1)} %param.19) | copy-start | bytes 61444
  96.8 3.9 %collective-permute-start.22 = (bf16[16,640]{1,0:T(8,128)(2,1)S(1)}, bf16[16,640]{1,0:T(8,128)(2,1)S(1)}, u32[]{:S(2)}, u32[]{:S(2)}) collective-permute-start(bf16[16,640]{1,0:T(8,128)(2,1)S(1)} %get-tuple-element.83), channel_id=1, source_target_pairs={{0,64},{8,72},{16,80},{24,88},{32,96},{40,104},{48,112},{56,120},{... | collective-permute-start | bytes 61448 | tf_op jit(solution)/shard_map/ppermute | solution.py:55
  96.9 4.2 %collective-permute-start.23 = (bf16[16,640]{1,0:T(8,128)(2,1)S(1)}, bf16[16,640]{1,0:T(8,128)(2,1)S(1)}, u32[]{:S(2)}, u32[]{:S(2)}) collective-permute-start(bf16[16,640]{1,0:T(8,128)(2,1)S(1)} %get-tuple-element.84), channel_id=1, source_target_pairs={{0,128},{8,136},{16,144},{24,152},{32,160},{40,168},{48,176},{56,1... | collective-permute-start | bytes 61448 | tf_op jit(solution)/shard_map/ppermute | solution.py:55
  99.6 2.9 %collective-permute-start.24 = (bf16[16,640]{1,0:T(8,128)(2,1)S(1)}, bf16[16,640]{1,0:T(8,128)(2,1)S(1)}, u32[]{:S(2)}, u32[]{:S(2)}) collective-permute-start(bf16[16,640]{1,0:T(8,128)(2,1)S(1)} %get-tuple-element.85), channel_id=1, source_target_pairs={{0,192},{8,200},{16,208},{24,216},{32,224},{40,232},{48,240},{56,2... | collective-permute-start | bytes 61448 | tf_op jit(solution)/shard_map/ppermute | solution.py:55
